TPU v7x, 32 devices: a whole 2x2x4 slice. The times are simulated.
32 devices in a mesh: clip: 4 (over z), frame: 4 (over y, x), seg: 2 (over core).
Axes of the slice: x: 2, y: 2, z: 4, core: 2. Of those that a mesh axis runs over, the one named last changes fastest.
Arguments:
- video: bfloat16 [2, 40, 4, 197, 384], P(None, ('clip', 'seg'), 'frame'), may hold values from -6 to 6
- captions: bfloat16 [2, 8, 128, 384], P(None, ('clip', 'seg'), 'frame'), may hold values from -6 to 6
- caption_lengths: int32 [2, 8, 9], P(None, ('clip', 'seg')), may hold values from 1 to 64, 128 in all within a row
- message_weight: bfloat16 [384, 384], replicated, may hold values from -0.3125 to 0.3125
- message_gain: float32 [384], replicated, may hold values from 0.25 to 1.75
- qkv_weights: bfloat16 [3, 3, 384, 384], replicated, may hold values from -0.3125 to 0.3125
- out_weights: bfloat16 [3, 384, 384], replicated, may hold values from -0.875 to 0.875
- mlp_up: bfloat16 [384, 1536], replicated, may hold values from -0.3125 to 0.3125
- mlp_down: bfloat16 [1536, 384], replicated, may hold values from -0.15625 to 0.15625
- gains: float32 [4, 384], replicated, may hold values from 0.5 to 1.5
- video_cot: bfloat16 [2, 40, 4, 197, 384], P(None, ('clip', 'seg'), 'frame'), may hold values from -6 to 6
- caption_cot: bfloat16 [2, 8, 128, 384], P(None, ('clip', 'seg'), 'frame'), may hold values from -6 to 6
Outputs:
- video_out: bfloat16 [2, 40, 4, 197, 384], P(None, ('clip', 'seg'), 'frame')
- caption_out: bfloat16 [2, 8, 128, 384], P(None, ('clip', 'seg'), 'frame')
- video_grad: bfloat16 [2, 40, 4, 197, 384], P(None, ('clip', 'seg'), 'frame')
- caption_grad: bfloat16 [2, 8, 128, 384], P(None, ('clip', 'seg'), 'frame')
- message_weight_grad: float32 [384, 384], replicated
- message_gain_grad: float32 [384], replicated
- qkv_weights_grad: float32 [3, 3, 384, 384], replicated
- out_weights_grad: float32 [3, 384, 384], replicated
- mlp_up_grad: float32 [384, 1536], replicated
- mlp_down_grad: float32 [1536, 384], replicated
- gains_grad: float32 [4, 384], replicated
Inputs may be any that keep to these rules, and one draw needn't show every extreme that they name: `caption_lengths`: the entries of each row sum to 128; the last entry is the padding at the end of the pack, the others are the lengths of its captions; caption j of a pack describes clip j mod 5 of its group.
All inputs are finite; a program needn't handle non-finite values.
Results may differ from a plain program's by a relative error of at most 0.019.
Values may be sent and summed in bfloat16 or wider, within the bound.
No kernel may reach another device: no remote copies, remote signals or barrier semaphores. Data moves between devices by JAX's collectives and lax.ppermute only.
A program may use at most 192 MiB of HBM per device.

v0:
```python
import jax
import jax.numpy as jnp
from jax import lax
from jax.sharding import PartitionSpec as P

HEADS = 6
HEAD_DIM = 64


epsilon = 1e-05
score_scale = 0.125
masked_score = -1e30
precise = lax.Precision.HIGHEST


def layer_norm(values, gain_row):
    center = values - jnp.mean(values, axis=-1, keepdims=True)
    spread = jnp.mean(center * center, axis=-1, keepdims=True)
    return center * lax.rsqrt(spread + epsilon) * gain_row


def norm_back(values, gain_row, grads):
    _, pull = jax.vjp(layer_norm, values, gain_row)
    return pull(grads)


def quick_gelu(values):
    return values * jax.nn.sigmoid(1.702 * values)


def matmul(left, right):
    return jnp.dot(left, right, preferred_element_type=jnp.float32)


def matmul_back(left, right):
    return lax.dot_general(
        left,
        right,
        (((left.ndim - 1,), (right.ndim - 1,)), ((), ())),
        preferred_element_type=jnp.float32,
    )


def weight_grad(inputs, grads):
    flat_in = inputs.reshape(-1, inputs.shape[-1])
    flat_grad = grads.reshape(-1, grads.shape[-1])
    return lax.dot_general(
        flat_in, flat_grad, (((0,), (0,)), ((), ())), preferred_element_type=jnp.float32
    )


def precise_back(left, right):
    return lax.dot_general(
        left, right, (((left.ndim - 1,), (right.ndim - 1,)), ((), ())), precision=precise
    )


def precise_weight(inputs, grads):
    flat_in = inputs.reshape(-1, inputs.shape[-1])
    flat_grad = grads.reshape(-1, grads.shape[-1])
    return lax.dot_general(flat_in, flat_grad, (((0,), (0,)), ((), ())), precision=precise)


def soft_stats(scores):
    top_score = jnp.max(scores, axis=-1, keepdims=True)
    expo = jnp.exp(scores - top_score)
    total = jnp.sum(expo, axis=-1, keepdims=True)
    return (expo / total, top_score + jnp.log(total))


def soft_back(probs, dprobs):
    return probs * (dprobs - jnp.sum(dprobs * probs, axis=-1, keepdims=True))


def micro_batch(
    video_part,
    caption_part,
    length_part,
    cot_part,
    caption_cot_part,
    params,
    frame_index,
    frame_total,
):
    message_weight, message_gain, qkv_weights, out_weights, mlp_up, mlp_down, gains = params
    clip_count, local_frames, patch_count, width = video_part.shape
    token_count = patch_count + 1
    row_count = clip_count * local_frames
    first_frame = frame_index * local_frames
    bf16 = jnp.bfloat16
    f32 = jnp.float32
    class_rows = video_part[:, :, 0, :]
    start_message = matmul(class_rows, message_weight).astype(bf16)
    gathered = lax.all_gather(start_message, "frame", axis=1, tiled=True)
    normed_all = layer_norm(gathered.astype(f32), message_gain).astype(bf16)
    normed_own = lax.dynamic_slice_in_dim(normed_all, first_frame, local_frames, 1)
    keys_all = matmul(normed_all, qkv_weights[0, 1]).astype(bf16)
    values_all = matmul(normed_all, qkv_weights[0, 2]).astype(bf16)
    msg_queries = matmul(normed_own, qkv_weights[0, 0]).astype(bf16)
    query_heads = msg_queries.reshape(clip_count, local_frames, HEADS, HEAD_DIM)
    key_heads = keys_all.reshape(clip_count, frame_total, HEADS, HEAD_DIM)
    value_heads = values_all.reshape(clip_count, frame_total, HEADS, HEAD_DIM)
    msg_scores = (
        jnp.einsum("cfhd,cghd->chfg", query_heads, key_heads, preferred_element_type=f32)
        * score_scale
    )
    msg_probs, _ = soft_stats(msg_scores)
    msg_probs_low = msg_probs.astype(bf16)
    msg_context = jnp.einsum(
        "chfg,cghd->cfhd", msg_probs_low, value_heads, preferred_element_type=f32
    ).astype(bf16)
    msg_context = msg_context.reshape(clip_count, local_frames, width)
    message = start_message.astype(f32) + matmul(msg_context, out_weights[0])
    tokens = jnp.concatenate([video_part.astype(f32), message[:, :, None, :]], axis=2).reshape(
        row_count, token_count, width
    )
    normed_one = layer_norm(tokens, gains[0]).astype(bf16)
    head_shape = (row_count, token_count, HEADS, HEAD_DIM)
    frame_q = matmul(normed_one, qkv_weights[1, 0]).astype(bf16).reshape(head_shape)
    frame_k = matmul(normed_one, qkv_weights[1, 1]).astype(bf16).reshape(head_shape)
    frame_v = matmul(normed_one, qkv_weights[1, 2]).astype(bf16).reshape(head_shape)
    frame_scores = (
        jnp.einsum("nqhd,nkhd->nhqk", frame_q, frame_k, preferred_element_type=f32) * score_scale
    )
    frame_probs, frame_lse = soft_stats(frame_scores)
    frame_context = jnp.einsum(
        "nhqk,nkhd->nqhd", frame_probs.astype(bf16), frame_v, preferred_element_type=f32
    ).astype(bf16)
    frame_context = frame_context.reshape(row_count, token_count, width)
    mixed = tokens + matmul(frame_context, out_weights[1])
    resid = mixed[:, :patch_count]
    normed_two = layer_norm(resid, gains[1]).astype(bf16)
    hidden = matmul(normed_two, mlp_up)
    active = quick_gelu(hidden).astype(bf16)
    final = resid + matmul(active, mlp_down)
    visual_in = final[:, 0].reshape(clip_count, local_frames, width)
    visual_low = layer_norm(visual_in, gains[2]).astype(bf16)
    visual_all = lax.all_gather(visual_low, "frame", axis=1, tiled=True)
    key_count = clip_count * frame_total
    visual_flat = visual_all.reshape(key_count, width)
    cap_local = caption_part.shape[0]
    positions = frame_index * cap_local + jnp.arange(cap_local, dtype=jnp.int32)
    ends = jnp.cumsum(length_part)
    document = jnp.sum((ends[None, :] <= positions[:, None]).astype(jnp.int32), axis=1)
    valid = (document < length_part.shape[0] - 1).astype(f32)
    token_clip = document % clip_count
    key_clip = jnp.arange(key_count, dtype=jnp.int32) // frame_total
    allowed = token_clip[:, None] == key_clip[None, :]
    pack = caption_part.astype(f32)
    cap_normed = layer_norm(pack, gains[3]).astype(bf16)
    cap_q = matmul(cap_normed, qkv_weights[2, 0]).astype(bf16).reshape(cap_local, HEADS, HEAD_DIM)
    cap_k = matmul(visual_flat, qkv_weights[2, 1]).astype(bf16).reshape(key_count, HEADS, HEAD_DIM)
    cap_v = matmul(visual_flat, qkv_weights[2, 2]).astype(bf16).reshape(key_count, HEADS, HEAD_DIM)
    cap_scores = jnp.einsum("thd,khd->htk", cap_q, cap_k, preferred_element_type=f32) * score_scale
    cap_scores = jnp.where(allowed[None], cap_scores, masked_score)
    cap_probs, _ = soft_stats(cap_scores)
    cap_probs_low = cap_probs.astype(bf16)
    cap_context = (
        jnp.einsum("htk,khd->thd", cap_probs_low, cap_v, preferred_element_type=f32)
        .astype(bf16)
        .reshape(cap_local, width)
    )
    caption_sum = pack + valid[:, None] * matmul(cap_context, out_weights[2])
    cap_cot = caption_cot_part.astype(f32)
    cap_branch = (cap_cot * valid[:, None]).astype(bf16)
    grad_cap_out = weight_grad(cap_context, cap_branch)
    d_cap_context = (
        matmul_back(cap_branch, out_weights[2]).astype(bf16).reshape(cap_local, HEADS, HEAD_DIM)
    )
    d_cap_v = jnp.einsum(
        "htk,thd->khd", cap_probs_low, d_cap_context, preferred_element_type=f32
    ).reshape(key_count, width)
    d_cap_probs = jnp.einsum("thd,khd->htk", d_cap_context, cap_v, preferred_element_type=f32)
    d_cap_scores = soft_back(cap_probs, d_cap_probs).astype(bf16)
    d_cap_q = (
        (jnp.einsum("htk,khd->thd", d_cap_scores, cap_k, preferred_element_type=f32) * score_scale)
        .astype(bf16)
        .reshape(cap_local, width)
    )
    d_cap_k = (
        jnp.einsum("htk,thd->khd", d_cap_scores, cap_q, preferred_element_type=f32) * score_scale
    ).reshape(key_count, width)
    grad_cap_q = weight_grad(cap_normed, d_cap_q)
    d_cap_normed = matmul_back(d_cap_q, qkv_weights[2, 0])
    d_pack_norm, grad_gain_cap = norm_back(pack, gains[3], d_cap_normed)
    caption_grad = cap_cot + d_pack_norm
    visual_f32 = visual_flat.astype(f32)
    grad_cap_k = precise_weight(visual_f32, d_cap_k)
    grad_cap_v = precise_weight(visual_f32, d_cap_v)
    d_visual_part = precise_back(d_cap_k, qkv_weights[2, 1].astype(f32)) + precise_back(
        d_cap_v, qkv_weights[2, 2].astype(f32)
    )
    d_visual = lax.psum_scatter(
        d_visual_part.reshape(clip_count, frame_total, width),
        "frame",
        scatter_dimension=1,
        tiled=True,
    )
    d_visual_in, grad_gain_visual = norm_back(visual_in, gains[2], d_visual)
    d_final = cot_part.astype(f32).reshape(row_count, patch_count, width)
    d_final = jnp.concatenate([d_final[:, :1] + d_visual_in, d_final[:, 1:]], axis=1)
    mlp_branch = d_final.astype(bf16)
    grad_down = weight_grad(active, mlp_branch)
    d_active = matmul_back(mlp_branch, mlp_down)
    _, gelu_pull = jax.vjp(quick_gelu, hidden)
    d_hidden = gelu_pull(d_active)[0].astype(bf16)
    grad_up = weight_grad(normed_two, d_hidden)
    d_normed_two = matmul_back(d_hidden, mlp_up)
    d_resid_norm, grad_gain_mlp = norm_back(resid, gains[1], d_normed_two)
    d_resid = d_final + d_resid_norm
    d_mixed = jnp.concatenate([d_resid, jnp.zeros((row_count, 1, width), f32)], axis=1)
    frame_branch = d_mixed.astype(bf16)
    grad_frame_out = weight_grad(frame_context, frame_branch)
    d_frame_context = matmul_back(frame_branch, out_weights[1]).astype(bf16).reshape(head_shape)
    again_scores = (
        jnp.einsum("nqhd,nkhd->nhqk", frame_q, frame_k, preferred_element_type=f32) * score_scale
    )
    again_probs = jnp.exp(again_scores - frame_lse)
    d_frame_v = jnp.einsum(
        "nhqk,nqhd->nkhd", again_probs.astype(bf16), d_frame_context, preferred_element_type=f32
    ).astype(bf16)
    d_frame_probs = jnp.einsum(
        "nqhd,nkhd->nhqk", d_frame_context, frame_v, preferred_element_type=f32
    )
    d_frame_scores = soft_back(again_probs, d_frame_probs).astype(bf16)
    d_frame_q = (
        jnp.einsum("nhqk,nkhd->nqhd", d_frame_scores, frame_k, preferred_element_type=f32)
        * score_scale
    ).astype(bf16)
    d_frame_k = (
        jnp.einsum("nhqk,nqhd->nkhd", d_frame_scores, frame_q, preferred_element_type=f32)
        * score_scale
    ).astype(bf16)
    row_shape = (row_count, token_count, width)
    d_frame_q = d_frame_q.reshape(row_shape)
    d_frame_k = d_frame_k.reshape(row_shape)
    d_frame_v = d_frame_v.reshape(row_shape)
    grad_frame_q = weight_grad(normed_one, d_frame_q)
    grad_frame_k = weight_grad(normed_one, d_frame_k)
    grad_frame_v = weight_grad(normed_one, d_frame_v)
    d_normed_one = (
        matmul_back(d_frame_q, qkv_weights[1, 0])
        + matmul_back(d_frame_k, qkv_weights[1, 1])
        + matmul_back(d_frame_v, qkv_weights[1, 2])
    )
    d_tokens_norm, grad_gain_frame = norm_back(tokens, gains[0], d_normed_one)
    d_tokens = (d_mixed + d_tokens_norm).reshape(clip_count, local_frames, token_count, width)
    d_message = d_tokens[:, :, patch_count]
    grad_msg_out = precise_weight(msg_context.astype(f32), d_message)
    d_msg_context = precise_back(d_message, out_weights[0].astype(f32)).reshape(
        clip_count, local_frames, HEADS, HEAD_DIM
    )
    d_msg_v = jnp.einsum(
        "chfg,cfhd->cghd", msg_probs_low.astype(f32), d_msg_context, precision=precise
    )
    d_msg_probs = jnp.einsum(
        "cfhd,cghd->chfg", d_msg_context, value_heads.astype(f32), precision=precise
    )
    d_msg_scores = soft_back(msg_probs, d_msg_probs) * score_scale
    d_msg_q = jnp.einsum(
        "chfg,cghd->cfhd", d_msg_scores, key_heads.astype(f32), precision=precise
    ).reshape(clip_count, local_frames, width)
    d_msg_k = jnp.einsum(
        "chfg,cfhd->cghd", d_msg_scores, query_heads.astype(f32), precision=precise
    ).reshape(clip_count, frame_total, width)
    d_msg_v = d_msg_v.reshape(clip_count, frame_total, width)
    grad_msg_q = precise_weight(normed_own.astype(f32), d_msg_q)
    d_normed_query = precise_back(d_msg_q, qkv_weights[0, 0].astype(f32))
    normed_f32 = normed_all.astype(f32)
    grad_msg_k = precise_weight(normed_f32, d_msg_k)
    grad_msg_v = precise_weight(normed_f32, d_msg_v)
    d_normed_all = precise_back(d_msg_k, qkv_weights[0, 1].astype(f32)) + precise_back(
        d_msg_v, qkv_weights[0, 2].astype(f32)
    )
    own_part = lax.dynamic_slice_in_dim(d_normed_all, first_frame, local_frames, 1) + d_normed_query
    d_normed_all = lax.dynamic_update_slice_in_dim(d_normed_all, own_part, first_frame, 1)
    d_start_part, grad_gain_msg = norm_back(gathered.astype(f32), message_gain, d_normed_all)
    d_start = (
        lax.psum_scatter(
            d_start_part.astype(jnp.bfloat16), "frame", scatter_dimension=1, tiled=True
        ).astype(jnp.float32)
        + d_message
    )
    grad_message = precise_weight(class_rows.astype(f32), d_start)
    d_class = precise_back(d_start, message_weight.astype(f32))
    d_video = d_tokens[:, :, :patch_count]
    d_video = jnp.concatenate([d_video[:, :, :1] + d_class[:, :, None], d_video[:, :, 1:]], axis=2)
    grads = (
        grad_message,
        grad_gain_msg,
        jnp.stack(
            [
                jnp.stack([grad_msg_q, grad_msg_k, grad_msg_v]),
                jnp.stack([grad_frame_q, grad_frame_k, grad_frame_v]),
                jnp.stack([grad_cap_q, grad_cap_k, grad_cap_v]),
            ]
        ),
        jnp.stack([grad_msg_out, grad_frame_out, grad_cap_out]),
        grad_up,
        grad_down,
        jnp.stack([grad_gain_frame, grad_gain_mlp, grad_gain_visual, grad_gain_cap]),
    )
    video_result = final.reshape(clip_count, local_frames, patch_count, width).astype(bf16)
    return (
        video_result,
        caption_sum.astype(bf16),
        d_video.astype(bf16),
        caption_grad.astype(bf16),
        grads,
    )


def local(
    video,
    captions,
    caption_lengths,
    message_weight,
    message_gain,
    qkv_weights,
    out_weights,
    mlp_up,
    mlp_down,
    gains,
    video_cot,
    caption_cot,
):
    micro_count = video.shape[0]
    frame_index = lax.axis_index("frame")
    frame_total = video.shape[2] * lax.axis_size("frame")
    params = (message_weight, message_gain, qkv_weights, out_weights, mlp_up, mlp_down, gains)
    totals = None
    video_rows = []
    caption_rows = []
    video_grads = []
    caption_grads = []
    for batch_index in range(micro_count):
        results = micro_batch(
            video[batch_index],
            captions[batch_index, 0],
            caption_lengths[batch_index, 0],
            video_cot[batch_index],
            caption_cot[batch_index, 0],
            params,
            frame_index,
            frame_total,
        )
        video_result, caption_result, video_grad, caption_grad, grads = results
        if totals is None:
            totals = tuple(grads)
        else:
            totals = tuple(
                jax.tree.map(lambda left, right: left + right, tuple(totals), tuple(grads))
            )
        video_rows.append(video_result)
        caption_rows.append(caption_result[None])
        video_grads.append(video_grad)
        caption_grads.append(caption_grad[None])
    totals = lax.psum(
        (totals[0], totals[1], totals[2], totals[3], totals[4], totals[5], totals[6]),
        ("clip", "frame", "seg"),
    )
    return (
        jnp.stack(video_rows),
        jnp.stack(caption_rows),
        jnp.stack(video_grads),
        jnp.stack(caption_grads),
        totals[0],
        totals[1],
        totals[2],
        totals[3],
        totals[4],
        totals[5],
        totals[6],
    )


def solution(mesh):
    placed = (
        P(None, ("clip", "seg"), "frame", None, None),
        P(None, ("clip", "seg"), "frame", None),
        P(None, ("clip", "seg"), None),
        P(),
        P(),
        P(),
        P(),
        P(),
        P(),
        P(),
        P(None, ("clip", "seg"), "frame", None, None),
        P(None, ("clip", "seg"), "frame", None),
    )
    return jax.shard_map(
        local,
        mesh=mesh,
        in_specs=placed,
        out_specs=(
            P(None, ("clip", "seg"), "frame", None, None),
            P(None, ("clip", "seg"), "frame", None),
            P(None, ("clip", "seg"), "frame", None, None),
            P(None, ("clip", "seg"), "frame", None),
            P(),
            P(),
            P(),
            P(),
            P(),
            P(),
            P(),
        ),
        check_vma=False,
    )
```

profile of v0, /device:TPU:0, one launch (start us, length us, event | category | flops | bytes accessed | tf_op | source)
XLA Modules:
  0.0 668.3 jit_solution(6832889343563072791)
XLA Ops:
  10.1 4.3 fusion.391
  16.7 9.6 %all-gather = bf16[5,1536]{1,0:T(8,128)(2,1)S(1)} all-gather(bf16[5,384]{1,0:T(8,128)(2,1)S(1)} %convolution_convert_fusion.25), channel_id=2, replica_groups=mesh['clip'=4,'frame'=4,'seg'=2] {'frame'}, dimensions={1}, use_global_device_ids=true | all-gather | bytes 19200 | tf_op jit(solution)/shard_map/all_gather | solution.py:94
  28.6 8.1 %all-gather.1 = bf16[5,1536]{1,0:T(8,128)(2,1)S(1)} all-gather(bf16[5,384]{1,0:T(8,128)(2,1)S(1)} %convolution_convert_fusion.23), channel_id=3, replica_groups=mesh['clip'=4,'frame'=4,'seg'=2] {'frame'}, dimensions={1}, use_global_device_ids=true | all-gather | bytes 19200 | tf_op jit(solution)/shard_map/all_gather | solution.py:94
  100.4 4.6 multiply_convert_fusion.3
  108.1 4.4 multiply_convert_fusion.2
  116.2 7.2 %all_gather.15 = bf16[5,4,384]{2,0,1:T(8,128)(2,1)S(1)} all-gather(bf16[5,1,384]{2,0,1:T(8,128)(2,1)S(1)} %copy.590), channel_id=1, replica_groups=mesh['clip'=4,'frame'=4,'seg'=2] {'frame'}, dimensions={1}, use_global_device_ids=true | all-gather | bytes 19200 | tf_op jit(solution)/shard_map/all_gather | solution.py:138
  125.7 8.1 %all_gather.14 = bf16[5,4,384]{2,0,1:T(8,128)(2,1)S(1)} all-gather(bf16[5,1,384]{2,0,1:T(8,128)(2,1)S(1)} %copy.584), channel_id=1, replica_groups=mesh['clip'=4,'frame'=4,'seg'=2] {'frame'}, dimensions={1}, use_global_device_ids=true | all-gather | bytes 19200 | tf_op jit(solution)/shard_map/all_gather | solution.py:138
  141.8 4.2 fusion.390
  169.8 16.9 %all-reduce.8 = (f32[5,4,384]{2,1,0:T(4,128)S(1)}, f32[5,4,384]{2,1,0:T(4,128)S(1)}) all-reduce(f32[5,4,384]{2,1,0:T(4,128)S(1)} %reshape.1744, f32[5,4,384]{2,1,0:T(4,128)} %reshape.1730), channel_id=6, replica_groups=mesh['clip'=4,'frame'=4,'seg'=2] {'frame'}, use_global_device_ids=true, to_apply=%region_50.51.clone | all-reduce | flops 15360 | bytes 122880
  191.8 6.8 %fusion.11 = bf16[5,197,1536]{2,1,0:T(8,128)(2,1)S(1)} fusion(f32[5,197,1536]{2,1,0:T(8,128)} %get-tuple-element.199, bf16[1536,384]{1,0:T(8,128)(2,1)} %param.20, f32[5,196,384]{2,1,0:T(8,128)} %slice.233, f32[5,1,384]{2,1,0:T(1,128)S(1)} %slice_add_fusion.5), kind=kOutput, calls=%fused_computation.13 | convolution fusion | flops 1181621760 | bytes 11770368 | tf_op jit(solution)/shard_map/dot_general | solution.py:36
  201.5 5.2 fusion.15
  219.9 5.1 fusion.48
  238.1 4.1 fusion.51
  284.9 5.7 convolution_bitcast_fusion
  295.0 3.0 convolution_bitcast_fusion.2
  308.8 3.5 fusion.35
  314.9 3.0 copy.656
  317.9 3.5 reshape_reshape.47
  324.4 3.6 reshape_reshape.46
  328.8 6.5 fusion.31
  340.0 3.1 fusion.30
  344.8 3.5 reshape_reshape.40
  348.4 3.0 copy.654
  351.4 3.7 reshape_reshape.45
  355.1 3.0 copy.649
  358.1 3.5 reshape_reshape.39
  367.5 3.5 reshape_reshape.38
  380.6 3.5 reshape_reshape.44
  390.0 3.0 reshape_reshape.43
  420.6 41.1 %all-reduce.6 = (f32[384]{0:T(512)}, f32[4,384]{1,0:T(4,128)}) all-reduce(f32[384]{0:T(512)S(1)} %add.372, f32[4,384]{1,0:T(4,128)S(1)} %maximum_add_fusion.2), channel_id=1, replica_groups=mesh['clip'=4,'frame'=4,'seg'=2] {'clip','frame','seg'}, use_global_device_ids=true, to_apply=%region_69.70 | all-reduce | flops 1920 | bytes 15360 | tf_op jit(solution)/shard_map/psum | solution.py:358
  469.9 177.8 %all-reduce.11.cloned.1.call-done = (f32[384,384]{0,1:T(8,128)}, f32[3,3,384,384]{3,2,1,0:T(8,128)}, f32[3,384,384]{2,1,0:T(8,128)}, f32[384,1536]{1,0:T(8,128)}, f32[1536,384]{1,0:T(8,128)}) async-done(((f32[384,384]{0,1:T(8,128)}, f32[3,3,384,384]{3,2,1,0:T(8,128)}, f32[3,384,384]{2,1,0:T(8,128)}, f32[384,1536]{1,0:T(8,128)}, f32[1536,384]{1,0:T(8,128)}), (f32[384,384]{0,1:T(8,128)}, ...) | async-done | bytes 12386320 | tf_op jit(solution)/shard_map/psum | solution.py:358
  649.8 5.4 copy.857
  (942 shorter events, 278.8 us)
Async XLA Ops:
  7.2 93.2 %copy-start = (bf16[384,1536]{1,0:T(8,128)(2,1)S(1)}, bf16[384,1536]{1,0:T(8,128)(2,1)}, u32[]{:S(2)}) copy-start(bf16[384,1536]{1,0:T(8,128)(2,1)} %param.19) | copy-start | bytes 3538948
  7.2 402.4 %reduce-scatter.9.cloned.1.call-start = ((), (), s32[]{:S(2)}) async-start(), calls=%async_computation.2 | async-start | bytes 30720
  27.7 20.6 %copy-start.186 = (bf16[5,1,1,384]{3,2,0,1:T(2,128)(2,1)}, bf16[5,1,1,384]{3,2,0,1:T(2,128)(2,1)S(1)}, u32[]{:S(2)}) copy-start(bf16[5,1,1,384]{3,2,0,1:T(2,128)(2,1)S(1)} %slice.227) | copy-start | bytes 11524
  99.4 111.0 %copy-start.4 = (f32[5,197,384]{2,1,0:T(8,128)}, f32[5,197,384]{2,1,0:T(8,128)S(1)}, u32[]{:S(2)}) copy-start(f32[5,197,384]{2,1,0:T(8,128)S(1)} %get-tuple-element.220) | copy-start | bytes 4538884
  99.4 111.0 %copy-start.131 = (f32[5,197]{1,0:T(8,128)}, f32[5,197]{1,0:T(8,128)S(1)}, u32[]{:S(2)}) copy-start(f32[5,197]{1,0:T(8,128)S(1)} %broadcast_multiply_fusion.1) | copy-start | bytes 11824
  99.9 110.5 %copy-start.129 = (f32[5,197]{1,0:T(8,128)}, f32[5,197]{1,0:T(8,128)S(1)}, u32[]{:S(2)}) copy-start(f32[5,197]{1,0:T(8,128)S(1)} %fusion.327) | copy-start | bytes 11824
  100.3 110.1 %copy-start.137 = (f32[5,197]{1,0:T(8,128)}, f32[5,197]{1,0:T(8,128)S(1)}, u32[]{:S(2)}) copy-start(f32[5,197]{1,0:T(8,128)S(1)} %fusion.325) | copy-start | bytes 11824
  114.3 21.9 %copy-start.104 = (bf16[2,1,32,384]{3,2,1,0:T(8,128)(2,1)S(1)}, bf16[2,1,32,384]{3,2,1,0:T(8,128)(2,1)}, u32[]{:S(2)}) copy-start(bf16[2,1,32,384]{3,2,1,0:T(8,128)(2,1)} %param.13) | copy-start | bytes 147460
  114.4 22.8 %copy-start.211 = (f32[384]{0:T(512)S(1)}, f32[384]{0:T(512)}, u32[]{:S(2)}) copy-start(f32[384]{0:T(512)} %get-tuple-element.114) | copy-start | bytes 4612
  114.4 25.2 %copy-start.139 = (bf16[2,1,32,384]{3,2,1,0:T(8,128)(2,1)S(1)}, bf16[2,1,32,384]{3,2,1,0:T(8,128)(2,1)}, u32[]{:S(2)}) copy-start(bf16[2,1,32,384]{3,2,1,0:T(8,128)(2,1)} %param.23) | copy-start | bytes 147460
  114.4 25.2 %copy-start.257 = (f32[32]{0:T(128)S(1)}, f32[32]{0:T(128)}, u32[]{:S(2)}) copy-start(f32[32]{0:T(128)} %get-tuple-element.223) | copy-start | bytes 388
  114.4 25.4 %copy-start.260 = (f32[32]{0:T(128)S(1)}, f32[32]{0:T(128)}, u32[]{:S(2)}) copy-start(f32[32]{0:T(128)} %get-tuple-element.224) | copy-start | bytes 388
  159.6 27.2 %copy-start.155 = (f32[5,1,384]{2,1,0:T(1,128)S(1)}, f32[5,1,384]{2,1,0:T(1,128)}, u32[]{:S(2)}) copy-start(f32[5,1,384]{2,1,0:T(1,128)} %copy-done.154) | copy-start | bytes 23044
  159.6 27.2 %copy-start.157 = (f32[5,1,384]{2,1,0:T(1,128)S(1)}, f32[5,1,384]{2,1,0:T(1,128)}, u32[]{:S(2)}) copy-start(f32[5,1,384]{2,1,0:T(1,128)} %copy-done.156) | copy-start | bytes 23044
  159.6 27.2 %copy-start.218 = (f32[384]{0:T(512)S(1)}, f32[384]{0:T(512)}, u32[]{:S(2)}) copy-start(f32[384]{0:T(512)} %get-tuple-element.117) | copy-start | bytes 4612
  159.6 27.2 %copy-start.244 = (f32[5]{0:T(128)S(1)}, f32[5]{0:T(128)}, u32[]{:S(2)}) copy-start(f32[5]{0:T(128)} %copy-done.243) | copy-start | bytes 64
  159.6 27.2 %copy-start.246 = (f32[5]{0:T(128)S(1)}, f32[5]{0:T(128)}, u32[]{:S(2)}) copy-start(f32[5]{0:T(128)} %copy-done.245) | copy-start | bytes 64
  161.4 27.4 %copy-start.223 = (f32[6,32]{1,0:T(8,128)}, f32[6,32]{1,0:T(8,128)S(1)}, u32[]{:S(2)}) copy-start(f32[6,32]{1,0:T(8,128)S(1)} %get-tuple-element.200) | copy-start | bytes 2308
  164.8 33.8 %copy-start.121 = (f32[20,384]{1,0:T(8,128)}, f32[20,384]{1,0:T(8,128)S(1)}, u32[]{:S(2)}) copy-start(f32[20,384]{1,0:T(8,128)S(1)} %reshape.1742) | copy-start | bytes 92164
  165.8 32.8 %copy-start.123 = (f32[20,384]{1,0:T(8,128)}, f32[20,384]{1,0:T(8,128)S(1)}, u32[]{:S(2)}) copy-start(f32[20,384]{1,0:T(8,128)S(1)} %reshape.1743) | copy-start | bytes 92164
  191.8 18.6 %copy-start.219 = (f32[5,1,384]{2,1,0:T(1,128)}, f32[5,1,384]{2,1,0:T(1,128)S(1)}, u32[]{:S(2)}) copy-start(f32[5,1,384]{2,1,0:T(1,128)S(1)} %slice_add_fusion.5) | copy-start | bytes 23044
  242.3 13.3 %copy-start.36 = (bf16[5,6,64,198]{3,2,1,0:T(8,128)(2,1)}, bf16[5,6,64,198]{3,2,1,0:T(8,128)(2,1)S(1)}, u32[]{:S(2)}) copy-start(bf16[5,6,64,198]{3,2,1,0:T(8,128)(2,1)S(1)} %fusion.51) | copy-start | bytes 2280964
  268.8 12.6 %copy-start.126 = (bf16[6,32,20]{1,2,0:T(8,128)(2,1)S(1)}, bf16[6,32,20]{1,2,0:T(8,128)(2,1)}, u32[]{:S(2)}) copy-start(bf16[6,32,20]{1,2,0:T(8,128)(2,1)} %copy-done.125) | copy-start | bytes 23044
  278.6 132.3 %reduce-scatter.11.cloned.1.call-start = ((), (), s32[]{:S(2)}) async-start(), calls=%async_computation.3 | async-start | bytes 30720
  279.5 368.1 %all-reduce.11.cloned.1.call-start = ((), (), s32[]{:S(2)}) async-start(), calls=%async_computation.4 | async-start | bytes 24772608 | tf_op jit(solution)/shard_map/psum | solution.py:358
  415.4 46.3 %copy-start.48 = (bf16[3,384,384]{2,1,0:T(8,128)(2,1)S(1)}, bf16[3,384,384]{2,1,0:T(8,128)(2,1)}, u32[]{:S(2)}) copy-start(bf16[3,384,384]{2,1,0:T(8,128)(2,1)} %param.18) | copy-start | bytes 2654212
  415.4 46.3 %copy-start.161 = (bf16[32,384]{1,0:T(8,128)(2,1)S(1)}, bf16[32,384]{1,0:T(8,128)(2,1)}, u32[]{:S(2)}) copy-start(bf16[32,384]{1,0:T(8,128)(2,1)} %copy-done.160) | copy-start | bytes 73732
  415.5 46.5 %copy-start.163 = (bf16[32,384]{1,0:T(8,128)(2,1)S(1)}, bf16[32,384]{1,0:T(8,128)(2,1)}, u32[]{:S(2)}) copy-start(bf16[32,384]{1,0:T(8,128)(2,1)} %copy-done.162) | copy-start | bytes 73732
  415.5 46.5 %copy-start.259 = (f32[32]{0:T(128)S(1)}, f32[32]{0:T(128)}, u32[]{:S(2)}) copy-start(f32[32]{0:T(128)} %get-tuple-element.223) | copy-start | bytes 388
  417.8 45.0 %copy-start.265 = (f32[32]{0:T(128)S(1)}, f32[32]{0:T(128)}, u32[]{:S(2)}) copy-start(f32[32]{0:T(128)} %copy-done.264) | copy-start | bytes 388
  417.8 45.0 %copy-start.263 = (f32[32]{0:T(128)S(1)}, f32[32]{0:T(128)}, u32[]{:S(2)}) copy-start(f32[32]{0:T(128)} %copy-done.262) | copy-start | bytes 388
  417.8 45.3 %copy-start.141 = (bf16[2,1,32,384]{3,2,1,0:T(8,128)(2,1)S(1)}, bf16[2,1,32,384]{3,2,1,0:T(8,128)(2,1)}, u32[]{:S(2)}) copy-start(bf16[2,1,32,384]{3,2,1,0:T(8,128)(2,1)} %param.23) | copy-start | bytes 147460
  (248 other events, 1088.9 us)
Sparse Core Ops, SparseCore 0:
  278.7 22.3 reduce-scatter.8
  304.1 22.9 reduce-scatter.10
  413.3 234.3 all-reduce.10
where the time goes:
time: 680 us; the launch traced here: 668 us
  waiting for transfers between devices  178 us (26%)
  matrix products  174 us (26%)
  local copies, waits for them, and re-layouts  149 us (22%)
  blocking collectives  91.1 us (13%)
  other arithmetic  58 us (9%)
  between operations  17.8 us (3%)
    psum x1, waiting for transfers between devices, local(): lax.psum((totals[0], totals[1], totals[2], totals[3], totals[4], totals[5...  178 us
    unnamed x562, local copies, waits for them, and re-layouts  51.2 us
    psum x1, blocking collectives, local(): lax.psum((totals[0], totals[1], totals[2], totals[3], totals[4], totals[5...  41.1 us
    dot_general x30, matrix products, matmul(): return jnp.dot(left, right, preferred_element_type=jnp.float32)  38.3 us
    dot_general x16, matrix products, weight_grad(): lax.dot_general(flat_in, flat_grad, (((0,), (0,)), ((), ())), preferred_e...  35.4 us
    dot_general x16, matrix products, matmul_back(): lax.dot_general(left, right, (((left.ndim - 1,), (right.ndim - 1,)), ((),...  31.4 us
    another operation x6, local copies, waits for them, and re-layouts, weight_grad(): flat_grad = grads.reshape(-1, grads.shape[-1])  20.9 us
    all_gather x2, blocking collectives, micro_batch(): gathered = lax.all_gather(start_message, 'frame', axis=1, tiled=True)  17.7 us
  transfers between devices with their start and end apart: 3, of which 1 were waited for; matrix products, arithmetic and copies ran while one was open for 20% of the time, Pallas kernels for 0%

commit v1 on v0

v1 whole, which is shorter than its diff:
```python
import functools

import jax
import jax.numpy as jnp
from jax import lax
from jax.experimental import pallas as pl
from jax.experimental.pallas import tpu as pltpu
from jax.sharding import PartitionSpec as P

HEADS = 6
HEAD_DIM = 64
EPS = 1e-05
SCALE = 0.125
MASKED = -1e30
BIG = 56 * 1024 * 1024

f32 = jnp.float32
bf16 = jnp.bfloat16


def nn(a, b):
    return lax.dot_general(a, b, (((1,), (0,)), ((), ())), preferred_element_type=f32)


def nt(a, b):
    return lax.dot_general(a, b, (((1,), (1,)), ((), ())), preferred_element_type=f32)


def tn(a, b):
    return lax.dot_general(a, b, (((0,), (0,)), ((), ())), preferred_element_type=f32)


def exact(a, b):
    return lax.dot_general(
        a, b, (((1,), (0,)), ((), ())), precision=lax.Precision.HIGHEST, preferred_element_type=f32
    )


def unit_norm(x):
    center = x - jnp.mean(x, axis=-1, keepdims=True)
    inv = lax.rsqrt(jnp.mean(center * center, axis=-1, keepdims=True) + EPS)
    return center * inv, inv


def norm_back(unit, inv, gain, dy):
    du = dy * gain
    mean_du = jnp.mean(du, axis=-1, keepdims=True)
    mean_dot = jnp.mean(du * unit, axis=-1, keepdims=True)
    return inv * (du - mean_du - unit * mean_dot)


def row_sum(x):
    return jnp.sum(x, axis=0, keepdims=True)


def sigmoid(x):
    return 1.0 / (1.0 + jnp.exp(-x))


def head_mask(shape, lane_dim, head):
    lane = lax.broadcasted_iota(jnp.int32, shape, lane_dim)
    return (lane >= head * HEAD_DIM) & (lane < (head + 1) * HEAD_DIM)


def head_columns(width):
    lane = lax.broadcasted_iota(jnp.int32, (width, 128), 0)
    col = lax.broadcasted_iota(jnp.int32, (width, 128), 1)
    return ((lane >= col * HEAD_DIM) & (lane < (col + 1) * HEAD_DIM)).astype(f32)


def head_rows(width):
    col = lax.broadcasted_iota(jnp.int32, (128, width), 0)
    lane = lax.broadcasted_iota(jnp.int32, (128, width), 1)
    return ((lane >= col * HEAD_DIM) & (lane < (col + 1) * HEAD_DIM)).astype(f32)


def pad_rows(x, rows):
    if x.shape[0] == rows:
        return x
    return jnp.concatenate([x, jnp.zeros((rows - x.shape[0], x.shape[1]), x.dtype)], axis=0)


def put_row(block, at, row):
    top = at // 16 * 16
    tail = block[top : top + 16]
    index = lax.broadcasted_iota(jnp.int32, tail.shape, 0)
    tail = jnp.where(index == at - top, row, tail)
    pieces = [tail]
    if top:
        pieces.insert(0, block[:top])
    if top + 16 < block.shape[0]:
        pieces.append(block[top + 16 :])
    return jnp.concatenate(pieces, axis=0) if len(pieces) > 1 else tail


def full(shape):
    return pl.BlockSpec(shape, lambda *_: (0,) * len(shape))


def frame_block(shape):
    return pl.BlockSpec((1,) + shape, lambda i, *_: (i, 0, 0))


def scalars():
    return pl.BlockSpec(memory_space=pltpu.SMEM)


def shape_of(shape, dtype):
    return jax.ShapeDtypeStruct(shape, dtype)


def params(limit=BIG):
    return pltpu.CompilerParams(vmem_limit_bytes=limit)


def cost(flops, nbytes):
    return pl.CostEstimate(flops=int(flops), bytes_accessed=int(nbytes), transcendentals=0)


def class_kernel(count, video_ref, out_ref):
    rows = [video_ref[i, 0:1, :].astype(f32) for i in range(count)]
    out_ref[...] = pad_rows(jnp.concatenate(rows, axis=0), out_ref.shape[0]).astype(bf16)


def class_rows(video, slots):
    count, _, width = video.shape
    return pl.pallas_call(
        functools.partial(class_kernel, count),
        grid=(1,),
        in_specs=[pl.BlockSpec((count, 16, width), lambda i: (0, 0, 0))],
        out_specs=full((slots, width)),
        out_shape=shape_of((slots, width), bf16),
        name="class_rows",
    )(video)


def norm_kernel(rows, video_ref, gains_ref, wk_ref, wv_ref, normed_ref, k_ref, vt_ref, wvt):
    @pl.when(pl.program_id(0) == 0)
    def _():
        wvt[...] = wv_ref[...].T

    unit, _ = unit_norm(video_ref[0].astype(f32))
    normed = pad_rows(unit * gains_ref[0:1, :], rows).astype(bf16)
    normed_ref[0] = normed
    k_ref[0] = nn(normed, wk_ref[...]).astype(bf16)
    vt_ref[0] = nt(wvt[...], normed).astype(bf16)


def norm_tokens(video, gains, wk, wv, rows):
    count, patch, width = video.shape
    return pl.pallas_call(
        functools.partial(norm_kernel, rows),
        grid=(count,),
        in_specs=[
            frame_block((patch, width)),
            full(gains.shape),
            full(wk.shape),
            full(wv.shape),
        ],
        out_specs=[
            frame_block((rows, width)),
            frame_block((rows, width)),
            frame_block((width, rows)),
        ],
        out_shape=[
            shape_of((count, rows, width), bf16),
            shape_of((count, rows, width), bf16),
            shape_of((count, width, rows), bf16),
        ],
        scratch_shapes=[pltpu.VMEM((width, width), bf16)],
        compiler_params=params(),
        cost_estimate=cost(4 * count * rows * width * width, 8 * count * rows * width),
        name="norm_tokens",
    )(video, gains, wk, wv)


def message_scores(query, keys, columns):
    return [exact(query.astype(f32) * key.astype(f32), columns) * SCALE for key in keys]


def message_probs(scores):
    top = functools.reduce(jnp.maximum, scores)
    expo = [jnp.exp(score - top) for score in scores]
    total = functools.reduce(jnp.add, expo)
    return [e / total for e in expo]


def first_kernel(
    pieces, count, tokens, *refs
):
    gathered = refs[:pieces]
    (
        mw_ref, mg_ref, qkv_ref, outw_ref, up_ref, down_ref, gains_ref, k_ref, vt_ref,
        message_ref, nmsg_ref, visual_ref, final_ref, ctx,
    ) = refs[pieces:]
    width = mw_ref.shape[0]
    slots = gathered[0].shape[0]
    rows = k_ref.shape[1]
    classes = jnp.concatenate([g[...] for g in gathered], axis=0)
    start = nn(classes, mw_ref[...]).astype(bf16)
    unit, _ = unit_norm(start.astype(f32))
    normed = (unit * mg_ref[...]).astype(bf16)
    keys = nn(normed, qkv_ref[0, 1]).astype(bf16)
    values = nn(normed, qkv_ref[0, 2]).astype(bf16)
    query = nn(normed[:slots], qkv_ref[0, 0]).astype(bf16)
    columns, spread = head_columns(width), head_rows(width).astype(bf16)
    cut = [slice(g * slots, (g + 1) * slots) for g in range(pieces)]
    probs = message_probs(message_scores(query, [keys[c] for c in cut], columns))
    context = functools.reduce(
        jnp.add,
        [nn(p.astype(bf16), spread) * values[c].astype(f32) for p, c in zip(probs, cut)],
    ).astype(bf16)
    message = start[:slots].astype(f32) + nn(context, outw_ref[0])
    message_ref[...] = message
    unit, _ = unit_norm(message)
    nmsg = (unit * gains_ref[0:1, :]).astype(bf16)
    nmsg_ref[...] = nmsg.astype(f32)
    kmsg = nn(nmsg, qkv_ref[1, 1]).astype(bf16).astype(f32)
    vmsg = nn(nmsg, qkv_ref[1, 2]).astype(bf16).astype(f32)

    own = gathered[0][...].astype(f32)
    unit, _ = unit_norm(own)
    qcls = nn((unit * gains_ref[0:1, :]).astype(bf16), qkv_ref[1, 0]).astype(bf16).astype(f32) * SCALE
    head = lax.broadcasted_iota(jnp.int32, (16, width), 0)
    lane = lax.broadcasted_iota(jnp.int32, (16, width), 1)
    mine = (lane >= head * HEAD_DIM) & (lane < (head + 1) * HEAD_DIM)
    token = lax.broadcasted_iota(jnp.int32, (16, rows), 1)
    ctx[...] = jnp.zeros(ctx.shape, f32)
    for i in range(count):
        queries = jnp.where(mine, qcls[i : i + 1], 0.0)
        scores = nt(queries.astype(bf16), k_ref[i])
        last = jnp.sum(queries * kmsg[i : i + 1], axis=1, keepdims=True)
        scores = jnp.where(token == tokens - 1, last, scores)
        scores = jnp.where(token < tokens, scores, MASKED)
        expo = jnp.exp(scores - jnp.max(scores, axis=1, keepdims=True))
        prob = (expo / jnp.sum(expo, axis=1, keepdims=True)).astype(bf16)
        extra = jnp.sum(
            jnp.where(token == tokens - 1, prob.astype(f32), 0.0), axis=1, keepdims=True
        )
        out = nt(prob, vt_ref[i]) + extra * vmsg[i : i + 1]
        ctx[i : i + 1, :] = row_sum(jnp.where(mine, out, 0.0))
    resid = own + nn(ctx[...].astype(bf16), outw_ref[1])
    unit, _ = unit_norm(resid)
    hidden = nn((unit * gains_ref[1:2, :]).astype(bf16), up_ref[...])
    active = (hidden * sigmoid(1.702 * hidden)).astype(bf16)
    final = resid + nn(active, down_ref[...])
    final_ref[...] = final
    unit, _ = unit_norm(final)
    visual_ref[...] = (unit * gains_ref[2:3, :]).astype(bf16)


def first_rows(gathered, mw, mg, qkv, outw, up, down, gains, keys, values_t, tokens):
    count, rows, width = keys.shape
    slots = gathered[0].shape[0]
    operands = list(gathered) + [mw, mg, qkv, outw, up, down, gains, keys, values_t]
    return pl.pallas_call(
        functools.partial(first_kernel, len(gathered), count, tokens),
        grid=(1,),
        in_specs=[full(x.shape) for x in operands],
        out_specs=[full((slots, width))] * 4,
        out_shape=[
            shape_of((slots, width), f32),
            shape_of((slots, width), f32),
            shape_of((slots, width), bf16),
            shape_of((slots, width), f32),
        ],
        scratch_shapes=[pltpu.VMEM((slots, width), f32)],
        compiler_params=params(),
        cost_estimate=cost(4e9, 12e6),
        name="first_rows",
    )(*operands)


def with_message(normed_ref, nmsg_ref, tokens):
    normed = normed_ref[0]
    top = (tokens - 1) // 16 * 16
    tail = normed[top : top + 16].astype(f32)
    index = lax.broadcasted_iota(jnp.int32, tail.shape, 0)
    row = nmsg_ref[pl.ds(pl.program_id(0), 1), :]
    tail = jnp.where(index == tokens - 1 - top, row, tail).astype(bf16)
    pieces = [normed[:top], tail]
    if top + 16 < normed.shape[0]:
        pieces.append(normed[top + 16 :])
    return jnp.concatenate(pieces, axis=0)


def masked_tail(scores, tokens):
    top = tokens // 16 * 16
    if top >= scores.shape[0]:
        return scores
    tail = scores[top:]
    index = lax.broadcasted_iota(jnp.int32, tail.shape, 0)
    return jnp.concatenate([scores[:top], jnp.where(index < tokens - top, tail, MASKED)], axis=0)


def half_pair(block_t, head):
    own = block_t[head * HEAD_DIM : (head + 1) * HEAD_DIM]
    none = jnp.zeros(own.shape, own.dtype)
    return jnp.concatenate([own, none] if head % 2 == 0 else [none, own], axis=0)


def pair_lanes(block, head):
    at = head // 2 * 2 * HEAD_DIM
    return block[:, at : at + 2 * HEAD_DIM]


def attend_kernel(
    tokens, normed_ref, video_ref, message_ref, nmsg_ref, wq_ref, wk_ref, wv_ref, wo_ref,
    resid_ref, ctx_ref, lse_ref, wqt, wvt,
):
    @pl.when(pl.program_id(0) == 0)
    def _():
        wqt[...] = wq_ref[...].T
        wvt[...] = wv_ref[...].T

    normed = with_message(normed_ref, nmsg_ref, tokens)
    rows = normed.shape[0]
    keys = nn(normed, wk_ref[...]).astype(bf16)
    queries_t = nt(wqt[...], normed).astype(bf16) * jnp.bfloat16(SCALE)
    values_t = nt(wvt[...], normed).astype(bf16)
    contexts, stats = [], []
    for head in range(HEADS):
        scores = nn(pair_lanes(keys, head), half_pair(queries_t, head))
        scores = masked_tail(scores, tokens)
        top = jnp.max(scores, axis=0, keepdims=True)
        expo = jnp.exp(scores - top)
        total = row_sum(expo)
        own = values_t[head * HEAD_DIM : (head + 1) * HEAD_DIM]
        contexts.append(nn(own, expo.astype(bf16)) * (1.0 / total))
        stats.append(top + jnp.log(total))
    context_t = jnp.concatenate(contexts, axis=0).astype(bf16)
    ctx_ref[0] = context_t
    lse_ref[0] = jnp.concatenate(stats + [jnp.zeros((8 - HEADS, rows), f32)], axis=0)
    row = message_ref[pl.ds(pl.program_id(0), 1), :]
    base = put_row(pad_rows(video_ref[0].astype(f32), rows), tokens - 1, row)
    resid_ref[0] = base + tn(context_t, wo_ref[...])


def attend(normed, video, message, nmsg, wq, wk, wv, wo, tokens):
    count, rows, width = normed.shape
    slots = message.shape[0]
    return pl.pallas_call(
        functools.partial(attend_kernel, tokens),
        grid=(count,),
        in_specs=[
            frame_block((rows, width)),
            frame_block(video.shape[1:]),
            full((slots, width)),
            full((slots, width)),
        ]
        + [full((width, width))] * 4,
        out_specs=[
            frame_block((rows, width)),
            frame_block((width, rows)),
            frame_block((8, rows)),
        ],
        out_shape=[
            shape_of((count, rows, width), f32),
            shape_of((count, width, rows), bf16),
            shape_of((count, 8, rows), f32),
        ],
        scratch_shapes=[pltpu.VMEM((width, width), bf16)] * 2,
        compiler_params=params(),
        cost_estimate=cost(14e9, 10e6),
        name="attend",
    )(normed, video, message, nmsg, wq, wk, wv, wo)


def caption_kernel(
    pieces, groups, clips, local, where_ref, lengths_ref, *refs
):
    gathered = refs[:pieces]
    caps_ref, cot_ref, qkv_ref, outw_ref, gains_ref = refs[pieces : pieces + 5]
    out_ref, grad_ref, gain_ref = refs[pieces + 5 : pieces + 8]
    part_refs = refs[pieces + 8 : pieces + 8 + pieces]
    keep_ref, send_ref, acc = refs[pieces + 8 + pieces :]
    width = caps_ref.shape[1]
    slots = gathered[0].shape[0]
    count = caps_ref.shape[0]
    keys_n = pieces * slots
    runs = lengths_ref.shape[1]

    token = lax.broadcasted_iota(jnp.int32, (count, keys_n), 0)
    key = lax.broadcasted_iota(jnp.int32, (count, keys_n), 1)
    slot = key % slots
    group = token // local
    position = token - group * local + where_ref[0] * local
    document = jnp.zeros((count, keys_n), jnp.int32)
    for m in range(groups):
        end = jnp.int32(0)
        for j in range(runs):
            end = end + lengths_ref[m, j]
            document = document + jnp.where((group == m) & (position >= end), 1, 0)
    allowed = slot == group * clips + document % clips
    valid = (document[:, 0:1] < runs - 1).astype(f32)

    pack = caps_ref[...].astype(f32)
    unit, inv = unit_norm(pack)
    gain = gains_ref[3:4, :]
    normed = (unit * gain).astype(bf16)
    visual = jnp.concatenate([g[...] for g in gathered], axis=0)
    queries = nn(normed, qkv_ref[2, 0]).astype(bf16)
    keys = nn(visual, qkv_ref[2, 1]).astype(bf16)
    values = nn(visual, qkv_ref[2, 2]).astype(bf16)

    masks = [head_mask((count, width), 1, h) for h in range(HEADS)]
    zero = jnp.zeros((count, width), bf16)

    def by_head(x):
        return jnp.concatenate([jnp.where(m, x, zero) for m in masks], axis=0)

    def merge(x):
        cut = [x[h * count : (h + 1) * count] for h in range(HEADS)]
        return functools.reduce(jnp.add, [jnp.where(m, c, 0.0) for m, c in zip(masks, cut)])

    allowed_all = jnp.concatenate([allowed.astype(jnp.int32)] * HEADS, axis=0) > 0
    split_q = by_head(queries)
    scores = jnp.where(allowed_all, nt(split_q, keys) * SCALE, MASKED)
    expo = jnp.exp(scores - jnp.max(scores, axis=1, keepdims=True))
    probs = expo / jnp.sum(expo, axis=1, keepdims=True)
    low = probs.astype(bf16)
    context = merge(nn(low, values)).astype(bf16)
    out_ref[...] = (pack + valid * nn(context, outw_ref[2])).astype(bf16)

    cot = cot_ref[...].astype(f32)
    branch = (cot * valid).astype(bf16)
    split_d = by_head(nt(branch, outw_ref[2]).astype(bf16))
    dvalues = tn(low, split_d)
    dprobs = nt(split_d, values)
    dscores = probs * (dprobs - jnp.sum(dprobs * probs, axis=1, keepdims=True))
    dscores = jnp.where(allowed_all, dscores, 0.0).astype(bf16)
    dqueries = (merge(nn(dscores, keys)) * SCALE).astype(bf16)
    dkeys = tn(dscores, split_q) * SCALE
    dnormed = nt(dqueries, qkv_ref[2, 0])
    grad_ref[...] = (cot + norm_back(unit, inv, gain, dnormed)).astype(bf16)
    gain_ref[...] = jnp.concatenate([row_sum(dnormed * unit), jnp.zeros((7, width), f32)], axis=0)
    low_k, low_v = dkeys.astype(bf16), dvalues.astype(bf16)
    part = nt(low_k, qkv_ref[2, 1]) + nt(low_v, qkv_ref[2, 2])
    for g in range(pieces):
        part_refs[g][...] = part[g * slots : (g + 1) * slots]
    if acc.shape[0] > 4 * width:
        acc[...] = jnp.zeros(acc.shape, f32)
    acc[0:width, :] = tn(normed, dqueries)
    acc[width : 2 * width, :] = tn(visual, low_k)
    acc[2 * width : 3 * width, :] = tn(visual, low_v)
    acc[3 * width : 4 * width, :] = tn(context, branch)
    emit(where_ref, acc, keep_ref, send_ref)


def captions_step(where, lengths, gathered, caps, cot, qkv, outw, gains, plan):
    count, width = caps.shape
    groups = lengths.shape[0]
    pieces = len(gathered)
    slots = gathered[0].shape[0]
    operands = list(gathered) + [caps, cot, qkv, outw, gains]
    acc_rows, packet_specs, packet_shapes = plan.packet(4 * width, width)
    return pl.pallas_call(
        functools.partial(caption_kernel, pieces, groups, plan.clips, count // groups),
        grid=(1,),
        in_specs=[scalars(), scalars()] + [full(x.shape) for x in operands],
        out_specs=[full((count, width))] * 2
        + [full((8, width))]
        + [full((slots, width))] * pieces
        + packet_specs,
        out_shape=[shape_of((count, width), bf16)] * 2
        + [shape_of((8, width), f32)]
        + [shape_of((slots, width), f32)] * pieces
        + packet_shapes,
        scratch_shapes=[pltpu.VMEM((acc_rows, width), f32)],
        compiler_params=params(),
        cost_estimate=cost(4e9, 8e6),
        name="captions_step",
    )(where, lengths, *operands)


def mlp_kernel(
    pieces, patch, ff, where_ref, resid_ref, cot_ref, final_ref, gains_ref, up_ref, down_ref, *refs
):
    parts = refs[:pieces]
    out_ref, dresid_ref, gain_ref, keep_ref, send_ref, acc, dcls = refs[pieces:]
    step = pl.program_id(0)
    rows, width = resid_ref.shape[1:]
    blocks = ff // width

    @pl.when(step == 0)
    def _():
        acc[...] = jnp.zeros(acc.shape, f32)
        dvisual = functools.reduce(jnp.add, [p[...] for p in parts])
        unit, inv = unit_norm(final_ref[...])
        dcls[...] = norm_back(unit, inv, gains_ref[2:3, :], dvisual)
        gain_ref[...] = jnp.concatenate(
            [jnp.zeros((1, width), f32), row_sum(dvisual * unit), jnp.zeros((6, width), f32)],
            axis=0,
        )

    resid = resid_ref[0]
    gain = gains_ref[1:2, :]
    unit, inv = unit_norm(resid)
    normed32 = unit * gain
    normed = normed32.astype(bf16)
    normed_t = normed32.T.astype(bf16)
    dfinal = pad_rows(cot_ref[0].astype(f32), rows)
    dfinal = put_row(dfinal, 0, dfinal[0:1] + dcls[pl.ds(step, 1), :])
    branch = dfinal.astype(bf16)
    branch_t = dfinal.T.astype(bf16)
    final = resid
    dnormed = jnp.zeros((rows, width), f32)
    for c in range(blocks):
        span = slice(c * width, (c + 1) * width)
        hidden = nn(normed, up_ref[:, span])
        gate = sigmoid(1.702 * hidden)
        active = (hidden * gate).astype(bf16)
        final = final + nn(active, down_ref[span, :])
        dactive = nt(branch, down_ref[span, :])
        dhidden = (dactive * gate * (1.0 + 1.702 * hidden * (1.0 - gate))).astype(bf16)
        dnormed = dnormed + nt(dhidden, up_ref[:, span])
        acc[span, :] += nn(normed_t, dhidden)
        acc[(blocks + c) * width : (blocks + c + 1) * width, :] += nn(branch_t, active)
    out_ref[0] = final[:patch].astype(bf16)
    dresid_ref[0] = dfinal + norm_back(unit, inv, gain, dnormed)
    gain_ref[0:1, :] += row_sum(dnormed * unit)

    @pl.when(step == pl.num_programs(0) - 1)
    def _():
        emit(where_ref, acc, keep_ref, send_ref)


def mlp_step(where, resid, cot, final, gains, up, down, parts, plan):
    count, rows, width = resid.shape
    patch = cot.shape[1]
    ff = up.shape[1]
    slots = final.shape[0]
    acc_rows, packet_specs, packet_shapes = plan.packet(2 * ff, width)
    return pl.pallas_call(
        functools.partial(mlp_kernel, len(parts), patch, ff),
        grid=(count,),
        in_specs=[
            scalars(),
            frame_block((rows, width)),
            frame_block((patch, width)),
            full((slots, width)),
            full(gains.shape),
            full(up.shape),
            full(down.shape),
        ]
        + [full((slots, width))] * len(parts),
        out_specs=[frame_block((patch, width)), frame_block((rows, width)), full((8, width))]
        + packet_specs,
        out_shape=[
            shape_of((count, patch, width), bf16),
            shape_of((count, rows, width), f32),
            shape_of((8, width), f32),
        ]
        + packet_shapes,
        scratch_shapes=[pltpu.VMEM((acc_rows, width), f32), pltpu.VMEM((slots, width), f32)],
        compiler_params=params(),
        cost_estimate=cost(20e9, 20e6),
        name="mlp_step",
    )(where, resid, cot, final, gains, up, down, *parts)


def attend_back_kernel(
    tokens, where_ref, normed_ref, video_ref, message_ref, nmsg_ref, ctx_ref, lse_ref, dresid_ref,
    gains_ref, wq_ref, wk_ref, wv_ref, wo_ref,
    grad_ref, dmsg_ref, dcls_ref, gain_ref, keep_ref, send_ref, acc, wqt, wkt, wall,
):
    step = pl.program_id(0)
    rows, width = dresid_ref.shape[1:]
    patch = tokens - 1

    @pl.when(step == 0)
    def _():
        acc[...] = jnp.zeros(acc.shape, f32)
        wqt[...] = wq_ref[...].T
        wkt[...] = wk_ref[...].T
        wall[:, 0:width] = wq_ref[...]
        wall[:, width : 2 * width] = wk_ref[...]
        wall[:, 2 * width : 3 * width] = wv_ref[...]
        dmsg_ref[...] = jnp.zeros(dmsg_ref.shape, f32)
        dcls_ref[...] = jnp.zeros(dcls_ref.shape, f32)
        gain_ref[...] = jnp.zeros(gain_ref.shape, f32)

    normed = with_message(normed_ref, nmsg_ref, tokens)
    keys = nn(normed, wk_ref[...]).astype(bf16)
    values = nn(normed, wv_ref[...]).astype(bf16)
    queries_t = nt(wqt[...], normed).astype(bf16) * jnp.bfloat16(SCALE)
    keys_t = nt(wkt[...], normed).astype(bf16)
    dmixed = dresid_ref[0]
    branch = dmixed.astype(bf16)
    context_t = ctx_ref[0]
    acc[3 * width : 4 * width, :] += nn(context_t, branch)
    dcontext_t = nt(wo_ref[...], branch).astype(bf16)
    dq, dk, dv = [], [], []
    for head in range(HEADS):
        own = slice(head * HEAD_DIM, (head + 1) * HEAD_DIM)
        scores = nn(pair_lanes(keys, head), half_pair(queries_t, head))
        probs = jnp.exp(masked_tail(scores, tokens) - lse_ref[0, head : head + 1, :])
        dprobs = nn(pair_lanes(values, head), half_pair(dcontext_t, head))
        dscores = (probs * (dprobs - row_sum(dprobs * probs))).astype(bf16)
        dv.append(nt(dcontext_t[own], probs.astype(bf16)))
        dq.append(nn(keys_t[own], dscores) * SCALE)
        dk.append(nt(queries_t[own], dscores))
    dall = jnp.concatenate(dq + dk + dv, axis=0).astype(bf16)
    acc[0 : 3 * width, :] += nn(dall, normed)
    dnormed = nn(wall[...], dall).T
    row = message_ref[pl.ds(step, 1), :]
    base = put_row(pad_rows(video_ref[0].astype(f32), rows), tokens - 1, row)
    unit, inv = unit_norm(base)
    dtokens = dmixed + norm_back(unit, inv, gains_ref[0:1, :], dnormed)
    gain_ref[0:1, :] += row_sum(dnormed * unit)
    grad_ref[0] = dtokens[:patch].astype(bf16)
    dcls_ref[pl.ds(step, 1), :] = dtokens[0:1]
    dmsg_ref[pl.ds(step, 1), :] = dtokens[patch : patch + 1]

    @pl.when(step == pl.num_programs(0) - 1)
    def _():
        emit(where_ref, acc, keep_ref, send_ref)


def attend_back(where, normed, video, message, nmsg, ctx, lse, dresid, gains, wq, wk, wv, wo, plan):
    count, rows, width = normed.shape
    patch = video.shape[1]
    slots = message.shape[0]
    acc_rows, packet_specs, packet_shapes = plan.packet(4 * width, width)
    return pl.pallas_call(
        functools.partial(attend_back_kernel, patch + 1),
        grid=(count,),
        in_specs=[
            scalars(),
            frame_block((rows, width)),
            frame_block((patch, width)),
            full((slots, width)),
            full((slots, width)),
            frame_block((width, rows)),
            frame_block((8, rows)),
            frame_block((rows, width)),
            full(gains.shape),
        ]
        + [full((width, width))] * 4,
        out_specs=[frame_block((patch, width))]
        + [full((slots, width))] * 2
        + [full((8, width))]
        + packet_specs,
        out_shape=[shape_of((count, patch, width), bf16)]
        + [shape_of((slots, width), f32)] * 2
        + [shape_of((8, width), f32)]
        + packet_shapes,
        scratch_shapes=[
            pltpu.VMEM((acc_rows, width), f32),
            pltpu.VMEM((width, width), bf16),
            pltpu.VMEM((width, width), bf16),
            pltpu.VMEM((width, 3 * width), bf16),
        ],
        compiler_params=params(),
        cost_estimate=cost(25e9, 20e6),
        name="attend_back",
    )(where, normed, video, message, nmsg, ctx, lse, dresid, gains, wq, wk, wv, wo)


def message_back_kernel(
    layout, together, where_ref, *refs
):
    segs, frames, clips = layout
    pieces = refs[: segs * frames]
    (
        mw_ref, mg_ref, qkv_ref, outw_ref, big_in, out_in,
        big_ref, out_ref, mwg_ref, gain_ref, gains_ref, dclass_ref,
        classes, dmsgs, keys, values, queries, context, dcontext, dq, dk, dv, dstart,
    ) = refs[segs * frames :]
    del big_in, out_in
    width = mw_ref.shape[0]
    slots = dclass_ref.shape[0]
    me_f, me_s, me_c = where_ref[0], where_ref[1], where_ref[2]
    total = together * slots
    rows = frames * total
    steps = segs * clips // together

    def row_of(s, f, c):
        group = s * clips + c
        step, inside = group // together, group % together
        return step, pl.multiple_of(f * total + inside * slots, 16)

    for a in range(segs):
        for b in range(frames):
            for d in range(clips):
                piece = pieces[a * frames + b][d]
                step, at = row_of(me_s ^ a, me_f ^ b, me_c ^ d)
                classes[step, pl.ds(at, slots), :] = piece[:slots]
                dmsgs[step, pl.ds(at, slots), :] = piece[slots : 2 * slots]
    gain_total = jnp.zeros((slots, width), f32)
    for i in range(frames * together):
        for step in range(steps):
            gain_total += dmsgs[step, i * slots : (i + 1) * slots, :].astype(f32)
    gains_ref[...] = gain_total[slots - 4 : slots]

    index = lax.broadcasted_iota(jnp.int32, (rows, 1), 0) % slots
    columns, spread = head_columns(width), head_rows(width)
    spread_low = spread.astype(bf16)
    cut = [slice(g * total, (g + 1) * total) for g in range(frames)]
    my_step, my_at = row_of(me_s, me_f, me_c)

    def batch(step, put):
        dm = jnp.where(index < slots - 6, dmsgs[step].astype(f32), 0.0).astype(bf16)
        cls = classes[step]
        start = nn(cls, mw_ref[...]).astype(bf16)
        unit, inv = unit_norm(start.astype(f32))
        normed = (unit * mg_ref[...]).astype(bf16)
        queries[...] = nn(normed, qkv_ref[0, 0]).astype(bf16)
        keys[...] = nn(normed, qkv_ref[0, 1]).astype(bf16)
        values[...] = nn(normed, qkv_ref[0, 2]).astype(bf16)
        dcontext[...] = nt(dm, outw_ref[0])
        dk[...] = jnp.zeros(dk.shape, f32)
        dv[...] = jnp.zeros(dv.shape, f32)

        @pl.loop(0, frames)
        def _(f):
            here = pl.ds(pl.multiple_of(f * total, 16), total)
            query = queries[here, :].astype(f32)
            dctx = dcontext[here, :]
            probs = message_probs(message_scores(query, [keys[c, :] for c in cut], columns))
            wide = [nn(p.astype(bf16), spread_low) for p in probs]
            context[here, :] = functools.reduce(
                jnp.add, [w * values[c, :].astype(f32) for w, c in zip(wide, cut)]
            ).astype(bf16)
            dprobs = [exact(dctx * values[c, :].astype(f32), columns) for c in cut]
            inner = functools.reduce(jnp.add, [p * d for p, d in zip(probs, dprobs)])
            total_dq = jnp.zeros((total, width), f32)
            for g in range(frames):
                dscore = exact(probs[g] * (dprobs[g] - inner) * SCALE, spread)
                total_dq = total_dq + dscore * keys[cut[g], :].astype(f32)
                dk[cut[g], :] += dscore * query
                dv[cut[g], :] += wide[g] * dctx
            dq[here, :] = total_dq

        low_q, low_k, low_v = dq[...].astype(bf16), dk[...].astype(bf16), dv[...].astype(bf16)
        put(big_ref, (0, 0), tn(normed, low_q))
        put(big_ref, (0, 1), tn(normed, low_k))
        put(big_ref, (0, 2), tn(normed, low_v))
        put(out_ref, 0, tn(context[...], dm))
        dnormed = nt(low_q, qkv_ref[0, 0]) + nt(low_k, qkv_ref[0, 1]) + nt(low_v, qkv_ref[0, 2])
        put(gain_ref, ..., row_sum(dnormed * unit))
        dstart[...] = norm_back(unit, inv, mg_ref[...], dnormed) + dm.astype(f32)
        put(mwg_ref, ..., tn(cls, dstart[...].astype(bf16)))

        @pl.when(my_step == step)
        def _():
            dclass_ref[...] = nt(dstart[pl.ds(my_at, slots), :].astype(bf16), mw_ref[...])

    def first(ref, at, value):
        ref[at] = value

    def more(ref, at, value):
        ref[at] += value

    batch(0, first)
    if steps > 1:
        pl.loop(1, steps)(lambda step: batch(step, more))


def message_back(where, pieces, mw, mg, qkv, outw, big, out, layout, slots):
    segs, frames, clips = layout
    width = mw.shape[0]
    groups = segs * clips
    together = max(1, min(groups, 512 // (frames * slots)))
    rows = frames * together * slots
    everyone = (groups // together, rows, width)
    operands = list(pieces) + [mw, mg, qkv, outw]
    where_big = 1 + len(operands)
    return pl.pallas_call(
        functools.partial(message_back_kernel, layout, together),
        grid=(1,),
        in_specs=[scalars()]
        + [full(x.shape) for x in operands]
        + [pl.BlockSpec(memory_space=pl.ANY)] * 2,
        out_specs=[
            pl.BlockSpec((1, 3, width, width), lambda i: (0, 0, 0, 0)),
            pl.BlockSpec((1, width, width), lambda i: (0, 0, 0)),
            full((width, width)),
            full((1, width)),
            full((4, width)),
            full((slots, width)),
        ],
        out_shape=[
            shape_of(big.shape, f32),
            shape_of(out.shape, f32),
            shape_of((width, width), f32),
            shape_of((1, width), f32),
            shape_of((4, width), f32),
            shape_of((slots, width), f32),
        ],
        input_output_aliases={where_big: 0, where_big + 1: 1},
        scratch_shapes=[pltpu.VMEM(everyone, bf16)] * 2
        + [pltpu.VMEM((rows, width), bf16)] * 4
        + [pltpu.VMEM((rows, width), f32)] * 5,
        compiler_params=params(),
        cost_estimate=cost(6e9, 12e6),
        name="message_back",
    )(where, *operands, big, out)


def class_fix_kernel(count, dclass_ref, dcls_ref, grad_in, grad_ref):
    fixed = dclass_ref[...] + dcls_ref[...]
    for i in range(count):
        block = grad_in[i].astype(f32)
        grad_ref[i] = put_row(block, 0, fixed[i : i + 1]).astype(bf16)


def class_fix(dclass, dcls, grad):
    count, _, width = grad.shape
    block = pl.BlockSpec((count, 16, width), lambda i: (0, 0, 0))
    return pl.pallas_call(
        functools.partial(class_fix_kernel, count),
        grid=(1,),
        in_specs=[full(dclass.shape), full(dcls.shape), block],
        out_specs=block,
        out_shape=shape_of(grad.shape, bf16),
        input_output_aliases={2: 0},
        name="class_fix",
    )(dclass, dcls, grad)


def emit(where_ref, acc, keep_ref, send_ref):
    frames, clips, chunk = keep_ref.shape[:3]
    me_f, me_s, me_c = where_ref[0], where_ref[1], where_ref[2]
    for a, out in enumerate((keep_ref, send_ref)):
        for b in range(frames):
            for d in range(clips):
                to = ((me_s ^ a) * frames + (me_f ^ b)) * clips + (me_c ^ d)
                at = pl.multiple_of(to * chunk, 16)
                out[b, d] = acc[pl.ds(at, chunk), :].astype(bf16)


class Plan:
    def __init__(self, clips):
        self.clips = clips
        self.segs = lax.axis_size("seg")
        self.frames = lax.axis_size("frame")
        self.rings = lax.axis_size("clip")
        self.layout = (self.segs, self.frames, self.rings)
        self.devices = self.segs * self.frames * self.rings

    def chunk(self, rows):
        share = -(-rows // self.devices)
        return -(-share // 16) * 16

    def packet(self, rows, width):
        chunk = self.chunk(rows)
        shape = (self.frames, self.rings, chunk, width)
        return chunk * self.devices, [full(shape)] * 2, [shape_of(shape, bf16)] * 2


def swap(x, axis, k):
    count = lax.axis_size(axis)
    return lax.ppermute(x, axis, [(i, i ^ k) for i in range(count)])


def add_first_kernel(keep_ref, got_ref, *outs):
    for b, out in enumerate(outs):
        out[...] = (keep_ref[b].astype(f32) + got_ref[b].astype(f32)).astype(bf16)


def add_first(keep, got):
    shape = keep.shape[1:]
    return pl.pallas_call(
        add_first_kernel,
        out_shape=[shape_of(shape, bf16)] * keep.shape[0],
        compiler_params=params(),
        cost_estimate=cost(keep.size, keep.size * 6),
        name="add_first",
    )(keep, got)


def add_split_kernel(count, *refs):
    terms, outs = refs[:count], refs[count:]
    for d, out in enumerate(outs):
        total = functools.reduce(jnp.add, [t[d].astype(f32) for t in terms])
        out[...] = total.astype(bf16)


def add_split(terms):
    shape = terms[0].shape[1:]
    return pl.pallas_call(
        functools.partial(add_split_kernel, len(terms)),
        out_shape=[shape_of(shape, bf16)] * terms[0].shape[0],
        compiler_params=params(),
        cost_estimate=cost(terms[0].size * len(terms), terms[0].size * 2 * (len(terms) + 1)),
        name="add_split",
    )(*terms)


def add_last_kernel(*refs):
    refs[-1][...] = functools.reduce(jnp.add, [t[...].astype(f32) for t in refs[:-1]]).astype(bf16)


def add_last(terms):
    return pl.pallas_call(
        add_last_kernel,
        out_shape=shape_of(terms[0].shape, bf16),
        compiler_params=params(),
        cost_estimate=cost(terms[0].size * len(terms), terms[0].size * 2 * (len(terms) + 1)),
        name="add_last",
    )(*terms)


def stack_kernel(*refs):
    for d, ref in enumerate(refs[:-1]):
        refs[-1][d] = ref[...]


def stack(parts):
    return pl.pallas_call(
        stack_kernel,
        out_shape=shape_of((len(parts),) + parts[0].shape, parts[0].dtype),
        compiler_params=params(),
        cost_estimate=cost(0, parts[0].size * 4 * len(parts)),
        name="stack",
    )(*parts)


def reduce_packet(keep, send):
    got = swap(send, "seg", 1)
    mine = add_first(keep, got)
    got = [swap(mine[b], "frame", b) for b in range(1, len(mine))]
    mine = add_split([mine[0]] + got)
    got = [swap(mine[d], "clip", d) for d in range(1, len(mine))]
    return add_last([mine[0]] + got)


def gather_packet(own):
    held = stack([own] + [swap(own, "clip", d) for d in range(1, lax.axis_size("clip"))])
    held = [held] + [swap(held, "frame", b) for b in range(1, lax.axis_size("frame"))]
    return held + [swap(h, "seg", 1) for h in held]


def place(layout, where_ref, pieces, whole):
    segs, frames, clips = layout
    chunk = pieces[0].shape[1]
    me_f, me_s, me_c = where_ref[0], where_ref[1], where_ref[2]
    for a in range(segs):
        for b in range(frames):
            for d in range(clips):
                of = ((me_s ^ a) * frames + (me_f ^ b)) * clips + (me_c ^ d)
                at = pl.multiple_of(of * chunk, 16)
                whole[pl.ds(at, chunk), :] = pieces[a * frames + b][d]


def unpack_mlp_kernel(layout, where_ref, *refs):
    count = layout[0] * layout[1]
    up_ref, down_ref, whole = refs[count:]
    width, ff = up_ref.shape
    place(layout, where_ref, refs[:count], whole)
    blocks = ff // width
    for c in range(blocks):
        span = slice(c * width, (c + 1) * width)
        up_ref[:, span] = whole[span, :].astype(f32)
        other = whole[(blocks + c) * width : (blocks + c + 1) * width, :]
        down_ref[span, :] = other.astype(f32).T


def unpack_mlp(where, pieces, width, ff, plan):
    whole = plan.devices * pieces[0].shape[1]
    return pl.pallas_call(
        functools.partial(unpack_mlp_kernel, plan.layout),
        grid=(1,),
        in_specs=[scalars()] + [full(x.shape) for x in pieces],
        out_specs=[full((width, ff)), full((ff, width))],
        out_shape=[shape_of((width, ff), f32), shape_of((ff, width), f32)],
        scratch_shapes=[pltpu.VMEM((whole, width), bf16)],
        compiler_params=params(),
        cost_estimate=cost(0, 8e6),
        name="unpack_mlp",
    )(where, *pieces)


def unpack_four_kernel(layout, flip, held, where_ref, *refs):
    count = layout[0] * layout[1]
    big_ref, out_ref, whole = refs[count + held :]
    width = out_ref.shape[-1]
    place(layout, where_ref, refs[:count], whole)
    for j in range(3):
        block = whole[j * width : (j + 1) * width, :].astype(f32)
        big_ref[0, j] = block.T if flip else block
    out_ref[0] = whole[3 * width : 4 * width, :].astype(f32)


def unpack_four(where, pieces, layer, flip, width, plan, held=()):
    whole = plan.devices * pieces[0].shape[1]
    at = 1 + len(pieces)
    return pl.pallas_call(
        functools.partial(unpack_four_kernel, plan.layout, flip, len(held)),
        grid=(1,),
        in_specs=[scalars()]
        + [full(x.shape) for x in pieces]
        + [pl.BlockSpec(memory_space=pl.ANY)] * len(held),
        out_specs=[
            pl.BlockSpec((1, 3, width, width), lambda i: (layer, 0, 0, 0)),
            pl.BlockSpec((1, width, width), lambda i: (layer, 0, 0)),
        ],
        out_shape=[shape_of((3, 3, width, width), f32), shape_of((3, width, width), f32)],
        input_output_aliases={at + i: i for i in range(len(held))},
        scratch_shapes=[pltpu.VMEM((whole, width), bf16)],
        compiler_params=params(),
        cost_estimate=cost(0, 5e6),
        name="unpack_four",
    )(where, *pieces, *held)


def last_rows_kernel(gain_a, gain_b, gain_c, dmsg_ref, classes_ref, out_ref):
    slots, width = dmsg_ref.shape
    filled = dmsg_ref[0 : slots - 6, :]
    rows = [
        filled,
        jnp.zeros((2, width), f32),
        gain_a[0:1, :],
        gain_b[0:1, :],
        gain_b[1:2, :],
        gain_c[0:1, :],
    ]
    out_ref[slots:, :] = jnp.concatenate(rows, axis=0).astype(bf16)
    out_ref[:slots, :] = classes_ref[...]


def last_rows(gain_a, gain_b, gain_c, dmsg, classes):
    slots, width = dmsg.shape
    return pl.pallas_call(
        last_rows_kernel,
        out_shape=shape_of((2 * slots, width), bf16),
        name="last_rows",
    )(gain_a, gain_b, gain_c, dmsg, classes)


def local(
    video, captions, caption_lengths, message_weight, message_gain, qkv_weights, out_weights,
    mlp_up, mlp_down, gains, video_cot, caption_cot,
):
    micro, clips, per_frame, patch, width = video.shape
    count = micro * clips * per_frame
    ff = mlp_up.shape[1]
    plan = Plan(clips)
    tokens = patch + 1
    rows = -(-tokens // 16) * 16
    slots = -(-(count + 6) // 16) * 16
    where = jnp.stack(
        [lax.axis_index("frame"), lax.axis_index("seg"), lax.axis_index("clip")]
    ).astype(jnp.int32)
    frames = video.reshape(count, patch, width)
    cots = video_cot.reshape(count, patch, width)
    caps = captions.reshape(-1, width)
    cap_cots = caption_cot.reshape(-1, width)
    lengths = caption_lengths.reshape(micro, -1)
    gain = message_gain.reshape(1, width)
    wq, wk, wv = qkv_weights[1, 0], qkv_weights[1, 1], qkv_weights[1, 2]
    wo = out_weights[1]

    classes = class_rows(frames, slots)
    gathered = [classes] + [swap(classes, "frame", b) for b in range(1, plan.frames)]
    normed, keys, values_t = norm_tokens(frames, gains, wk, wv, rows)
    message, nmsg, visual, final = first_rows(
        gathered, message_weight, gain, qkv_weights, out_weights, mlp_up, mlp_down, gains,
        keys, values_t, tokens,
    )
    visuals = [visual] + [swap(visual, "frame", b) for b in range(1, plan.frames)]
    resid, ctx, lse = attend(normed, frames, message, nmsg, wq, wk, wv, wo, tokens)
    results = captions_step(
        where, lengths, visuals, caps, cap_cots, qkv_weights, out_weights, gains, plan
    )
    caption_out, caption_grad, gain_c = results[:3]
    parts = list(results[3:-2])
    caption_packet = results[-2:]
    parts = [parts[0]] + [swap(parts[b], "frame", b) for b in range(1, plan.frames)]
    video_out, dresid, gain_b, keep, send = mlp_step(
        where, resid, cots, final, gains, mlp_up, mlp_down, parts, plan
    )
    caption_sum = gather_packet(reduce_packet(*caption_packet))
    mlp_sum = gather_packet(reduce_packet(keep, send))
    grad, dmsg, dcls, gain_a, keep, send = attend_back(
        where, normed, frames, message, nmsg, ctx, lse, dresid, gains, wq, wk, wv, wo, plan
    )
    rest = last_rows(gain_a, gain_b, gain_c, dmsg, classes)
    held = stack([rest] + [swap(rest, "clip", d) for d in range(1, plan.rings)])
    held = [held] + [swap(held, "frame", b) for b in range(1, plan.frames)]
    held = held + [swap(h, "seg", 1) for h in held]
    frame_sum = gather_packet(reduce_packet(keep, send))

    up_grad, down_grad = unpack_mlp(where, mlp_sum, width, ff, plan)
    big, out = unpack_four(where, caption_sum, 2, False, width, plan)
    big, out, mw_grad, mg_grad, gains_grad, dclass = message_back(
        where, held, message_weight, gain, qkv_weights, out_weights, big, out, plan.layout, slots
    )
    big, out = unpack_four(where, frame_sum, 1, True, width, plan, (big, out))
    grad = class_fix(dclass, dcls, grad)
    return (
        video_out.reshape(video.shape),
        caption_out.reshape(captions.shape),
        grad.reshape(video.shape),
        caption_grad.reshape(captions.shape),
        mw_grad,
        mg_grad.reshape(width),
        big,
        out,
        up_grad,
        down_grad,
        gains_grad,
    )


def solution(mesh):
    rows = P(None, ("clip", "seg"), "frame", None, None)
    caps = P(None, ("clip", "seg"), "frame", None)
    return jax.shard_map(
        local,
        mesh=mesh,
        in_specs=(rows, caps, P(None, ("clip", "seg"), None)) + (P(),) * 7 + (rows, caps),
        out_specs=(rows, caps, rows, caps) + (P(),) * 7,
        check_vma=False,
    )
```

time: 680 us -> 324 us (0.48); the launches traced: 668 us -> 323 us
  Pallas kernels: 0 us -> 190 us
  matrix products: 174 us -> 0 us
  waiting for transfers between devices: 178 us -> 35.7 us
  local copies, waits for them, and re-layouts: 149 us -> 20.7 us
  blocking collectives: 91.1 us -> 0 us
  starting transfers between devices: 0.12 us -> 73.4 us
  other arithmetic: 58 us -> 1.26 us
  between operations: 17.8 us -> 1.2 us
    pallas_call x0 -> x26, Pallas kernels: none -> 190 us  [the longest x1 44.4 us: mlp_step(): pl.pallas_call(functools.partial(mlp_kernel, len(parts), patch, ff), grid...]
    psum x1 -> x0, waiting for transfers between devices: 178 us -> none  [local(): lax.psum((totals[0], totals[1], totals[2], totals[3], totals[4], totals[5...]
    dot_general x122 -> x0, matrix products: 174 us -> none  [the longest x30 38.3 us: matmul(): return jnp.dot(left, right, preferred_element_type=jnp.float32)]
    ppermute x0 -> x70, starting transfers between devices: none -> 73.4 us  [swap(): return lax.ppermute(x, axis, [(i, i ^ k) for i in range(count)])]
    psum x1 -> x0, blocking collectives: 41.1 us -> none  [local(): lax.psum((totals[0], totals[1], totals[2], totals[3], totals[4], totals[5...]
    convert_element_type x32 -> x0, local copies, waits for them, and re-layouts: 37.7 us -> none  [the longest x2 5.99 us: micro_batch(): frame_context = jnp.einsum('nhqk,nkhd->nqhd', frame_probs.astype(bf16), f...]
    ppermute x0 -> x70, waiting for transfers between devices: none -> 35.7 us  [swap(): return lax.ppermute(x, axis, [(i, i ^ k) for i in range(count)])]
    unnamed x562 -> x150, local copies, waits for them, and re-layouts: 51.2 us -> 16.4 us
  transfers between devices with their start and end apart: 3 -> 70, of which waited for: 1 -> 15; matrix products, arithmetic and copies ran while one was open for 20% -> 4% of each run, Pallas kernels for 0% -> 52%
where the time goes in v1:
time: 324 us; the launch traced here: 323 us
  Pallas kernels  190 us (59%)
  starting transfers between devices  73.4 us (23%)
  waiting for transfers between devices  35.7 us (11%)
  local copies, waits for them, and re-layouts  20.7 us (6%)
    ppermute x70, starting transfers between devices, swap(): return lax.ppermute(x, axis, [(i, i ^ k) for i in range(count)])  73.4 us
    pallas_call x1, Pallas kernels, mlp_step(): pl.pallas_call(functools.partial(mlp_kernel, len(parts), patch, ff), grid...  44.4 us
    pallas_call x1, Pallas kernels, attend_back(): pl.pallas_call(functools.partial(attend_back_kernel, patch + 1), grid=(co...  37.1 us
    ppermute x70, waiting for transfers between devices, swap(): return lax.ppermute(x, axis, [(i, i ^ k) for i in range(count)])  35.7 us
    pallas_call x1, Pallas kernels, attend(): pl.pallas_call(functools.partial(attend_kernel, tokens), grid=(count,), i...  24.6 us
    pallas_call x1, Pallas kernels, message_back(): pl.pallas_call(functools.partial(message_back_kernel, layout, together),...  19 us
    unnamed x150, local copies, waits for them, and re-layouts  16.4 us
    pallas_call x1, Pallas kernels, first_rows(): pl.pallas_call(functools.partial(first_kernel, len(gathered), count, toke...  11.8 us
  transfers between devices with their start and end apart: 70, of which 15 were waited for; matrix products, arithmetic and copies ran while one was open for 4% of the time, Pallas kernels for 52%

profile of v1, /device:TPU:0, one launch (start us, length us, event | category | flops | bytes accessed | tf_op | source)
XLA Modules:
  0.0 322.6 jit_solution(12555007007825523669)
XLA Ops:
  0.6 2.8 copy.28
  5.0 2.9 collective-permute-start
  13.2 9.4 %norm_tokens.1 = (bf16[10,208,384]{2,1,0:T(8,128)(2,1)}, bf16[10,208,384]{2,1,0:T(8,128)(2,1)}, bf16[10,384,208]{2,1,0:T(8,128)(2,1)}) custom-call(bf16[10,197,384]{2,1,0:T(8,128)(2,1)} %bitcast.26, f32[4,384]{1,0:T(4,128)} %gains_ref.5, bf16[384,384]{1,0:T(8,128)(2,1)} %get-tuple-element.156.wk_ref, bf16[384,384]{1,0:T(8,128)(2,1)} %get-tuple-element.155.wv_ref), custom_call_target="tpu_custom_call" | custom-call | flops 1226833920 | bytes 6389760 | tf_op jit(solution)/shard_map/norm_tokens/pallas_call | solution.py:151
  23.9 11.8 %first_rows.1 = (f32[16,384]{1,0:T(8,128)}, f32[16,384]{1,0:T(8,128)}, bf16[16,384]{1,0:T(8,128)(2,1)}, f32[16,384]{1,0:T(8,128)}) custom-call(bf16[16,384]{1,0:T(8,128)(2,1)} %class_rows.1.refs_0_.classes_ref, bf16[16,384]{1,0:T(8,128)(2,1)} %copy-done.67, bf16[16,384]{1,0:T(8,128)(2,1)} %copy-done.68, bf16[16,384]{1,0:T(8,128)(2,1)} %copy-done.69, ...), custom_call_target="tpu_custom_call" | custom-call | flops 4000000000 | bytes 12000000 | tf_op jit(solution)/shard_map/first_rows/pallas_call | solution.py:256
  41.6 2.4 collective-permute-done.5.refs_3_
  44.6 5.7 %captions_step.1 = (bf16[64,384]{1,0:T(8,128)(2,1)}, bf16[64,384]{1,0:T(8,128)(2,1)}, f32[8,384]{1,0:T(8,128)}, f32[16,384]{1,0:T(8,128)}, f32[16,384]{1,0:T(8,1...) custom-call(s32[3]{0:T(128)} %pad_add_fusion.where_ref, ...), custom_call_target="tpu_custom_call" | custom-call | flops 4000000000 | bytes 8000000 | tf_op jit(solution)/shard_map/captions_step/pallas_call | solution.py:457
  51.0 2.8 collective-permute-start.8
  53.7 24.6 %attend.1 = (f32[10,208,384]{2,1,0:T(8,128)}, bf16[10,384,208]{2,1,0:T(8,128)(2,1)}, f32[10,8,208]{2,1,0:T(8,128)}) custom-call(bf16[10,208,384]{2,1,0:T(8,128)(2,1)} %get-tuple-element.77.normed_ref, bf16[10,197,384]{2,1,0:T(8,128)(2,1)} %bitcast.27, f32[16,384]{1,0:T(8,128)} %get-tuple-element.80.message_ref, f32[16,384]{1,0:T(8,128)} %get-tuple-element.81.nmsg_ref, ...), custom_call_target="tpu_custom_call" | custom-call | flops 14000000000 | bytes 10000000 | tf_op jit(solution)/shard_map/attend/pallas_call | solution.py:342
  79.1 44.4 %mlp_step.1 = (bf16[10,197,384]{2,1,0:T(8,128)(2,1)}, f32[10,208,384]{2,1,0:T(8,128)}, f32[8,384]{1,0:T(8,128)}, bf16[4,4,96,384]{3,2,1,0:T(8,128)(2,1)}, bf16[4,4,96,384]{3,2,1,0:T(8,128)(2,1)}) custom-call(s32[3]{0:T(128)} %pad_add_fusion.where_ref, f32[10,208,384]{2,1,0:T(8,128)} %get-tuple-element.82.resid_ref, bf16[10,197,384]{2,1,0:T(8,128)(2,1)} %bitcast.30, ...), custom_call_target="tpu_custom_call" | custom-call | flops 20000000000 | bytes 20000000 | tf_op jit(solution)/shard_map/mlp_step/pallas_call | solution.py:534
  124.0 37.1 %attend_back.1 = (bf16[10,197,384]{2,1,0:T(8,128)(2,1)}, f32[16,384]{1,0:T(8,128)}, f32[16,384]{1,0:T(8,128)}, f32[8,384]{1,0:T(8,128)}, bf16[4,4,48,384]{3,2,1,...) custom-call(s32[3]{0:T(128)} %pad_add_fusion.where_ref, bf16[10,208,384]{2,1,0:T(8,128)(2,1)} %get-tuple-element.77.normed_ref, ...), custom_call_target="tpu_custom_call" | custom-call | flops 24999999488 | bytes 20000000 | tf_op jit(solution)/shard_map/attend_back/pallas_call | solution.py:625
  164.2 2.6 collective-permute-start.10
  166.8 3.5 %collective-permute-start.11 = (bf16[32,384]{1,0:T(8,128)(2,1)}, bf16[32,384]{1,0:T(8,128)(2,1)S(1)}, u32[]{:S(2)}, u32[]{:S(2)}) collective-permute-start(bf16[32,384]{1,0:T(8,128)(2,1)} %last_rows.1.refs_0_), channel_id=1, source_target_pairs={{0,24},{8,16},{16,8},{24,0},{1,25},{9,17},{17,9},{25,1},{2,26},{10... | collective-permute-start | bytes 73736 | tf_op jit(solution)/shard_map/ppermute | solution.py:854
  170.2 2.4 collective-permute-done.11.refs_3_
  175.7 2.5 collective-permute-start.14
  190.9 2.7 add_first.5
  199.1 4.2 %collective-permute-start.24 = (bf16[48,384]{1,0:T(8,128)(2,1)}, bf16[48,384]{1,0:T(8,128)(2,1)S(1)}, u32[]{:S(2)}, u32[]{:S(2)}) collective-permute-start(bf16[48,384]{1,0:T(8,128)(2,1)} %get-tuple-element.106), channel_id=1, source_target_pairs={{0,16},{8,24},{16,0},{24,8},{1,17},{9,25},{17,1},{25,9},{2,18},{10... | collective-permute-start | bytes 110600 | tf_op jit(solution)/shard_map/ppermute | solution.py:854
  203.3 3.6 %collective-permute-start.25 = (bf16[48,384]{1,0:T(8,128)(2,1)}, bf16[48,384]{1,0:T(8,128)(2,1)S(1)}, u32[]{:S(2)}, u32[]{:S(2)}) collective-permute-start(bf16[48,384]{1,0:T(8,128)(2,1)} %get-tuple-element.107), channel_id=1, source_target_pairs={{0,24},{8,16},{16,8},{24,0},{1,25},{9,17},{17,9},{25,1},{2,26},{10... | collective-permute-start | bytes 110600 | tf_op jit(solution)/shard_map/ppermute | solution.py:854
  209.6 3.7 %collective-permute-done.40.refs_1_ = bf16[48,384]{1,0:T(8,128)(2,1)S(1)} collective-permute-done((bf16[48,384]{1,0:T(8,128)(2,1)}, bf16[48,384]{1,0:T(8,128)(2,1)S(1)}, u32[]{:S(2)}, u32[]{:S(2)}) %collective-permute-start.40) | collective-permute-done | bytes 36896 | tf_op jit(solution)/shard_map/ppermute | solution.py:854
  215.9 3.5 %collective-permute-done.42.refs_3_ = bf16[48,384]{1,0:T(8,128)(2,1)S(1)} collective-permute-done((bf16[48,384]{1,0:T(8,128)(2,1)}, bf16[48,384]{1,0:T(8,128)(2,1)S(1)}, u32[]{:S(2)}, u32[]{:S(2)}) %collective-permute-start.42) | collective-permute-done | bytes 36896 | tf_op jit(solution)/shard_map/ppermute | solution.py:854
  219.7 3.1 collective-permute-start.28
  237.3 3.0 collective-permute-start.45
  240.3 3.6 %collective-permute-done.44.refs_2_ = bf16[48,384]{1,0:T(8,128)(2,1)S(1)} collective-permute-done((bf16[48,384]{1,0:T(8,128)(2,1)}, bf16[48,384]{1,0:T(8,128)(2,1)S(1)}, u32[]{:S(2)}, u32[]{:S(2)}) %collective-permute-start.44) | collective-permute-done | bytes 36896 | tf_op jit(solution)/shard_map/ppermute | solution.py:854
  243.9 3.0 collective-permute-start.59
  256.2 2.4 collective-permute-start.48
  261.5 5.7 %collective-permute-done.61.refs_2_ = bf16[96,384]{1,0:T(8,128)(2,1)S(1)} collective-permute-done((bf16[96,384]{1,0:T(8,128)(2,1)}, bf16[96,384]{1,0:T(8,128)(2,1)S(1)}, u32[]{:S(2)}, u32[]{:S(2)}) %collective-permute-start.61) | collective-permute-done | bytes 73760 | tf_op jit(solution)/shard_map/ppermute | solution.py:854
  273.7 2.3 copy.30
  276.1 3.0 unpack_four.2
  279.8 7.5 %collective-permute-done.64.refs_2_ = bf16[4,96,384]{2,1,0:T(8,128)(2,1)S(1)} collective-permute-done((bf16[4,96,384]{2,1,0:T(8,128)(2,1)}, bf16[4,96,384]{2,1,0:T(8,128)(2,1)S(1)}, u32[]{:S(2)}, u32[]{:S(2)}) %collective-permute-start.64) | collective-permute-done | bytes 294944 | tf_op jit(solution)/shard_map/ppermute | solution.py:854
  287.8 19.0 %message_back.1 = (f32[3,3,384,384]{3,2,1,0:T(8,128)}, f32[3,384,384]{2,1,0:T(8,128)}, f32[384,384]{1,0:T(8,128)}, f32[1,384]{1,0:T(1,128)}, f32[4,384]{1,0:T(4,128)}, /*index=5*/f32[16,384]{1,0:T(8,128)}) custom-call(s32[3]{0:T(128)} %pad_add_fusion.where_ref, bf16[4,32,384]{2,1,0:T(8,128)(2,1)} %stack.20.refs_0_, ...), custom_call_target="tpu_custom_call", output_to_operand_aliasing={{0}: (13, {}), {1}: (14, {})} | custom-call | flops 6000000000 | bytes 12000000 | tf_op jit(solution)/shard_map/message_back/pallas_call | solution.py:769
  308.5 3.7 %copy.32 = bf16[2,5,1,197,384]{4,0,3,2,1:T(2,128)(2,1)} copy(bf16[2,5,1,197,384]{4,3,1,0,2:T(8,128)(2,1)} %bitcast.24) | data formatting | bytes 3025920
  313.4 3.1 unpack_four.3
  318.2 4.4 %unpack_mlp.1 = (f32[384,1536]{1,0:T(8,128)}, f32[1536,384]{1,0:T(8,128)}) custom-call(s32[3]{0:T(128)} %pad_add_fusion.where_ref, bf16[4,96,384]{2,1,0:T(8,128)(2,1)} %stack.23.refs_0_, bf16[4,96,384]{2,1,0:T(8,128)(2,1)} %copy-done.7, bf16[4,96,384]{2,1,0:T(8,128)(2,1)} %copy-done.8, bf16[4,96,384]{2,1,0:T(8,128)(2,1)} %copy-done.9, ...), custom_call_target="tpu_custom_call" | custom-call | bytes 8000000 | tf_op jit(solution)/shard_map/unpack_mlp/pallas_call | solution.py:962
  (289 shorter events, 85.2 us)
Async XLA Ops:
  5.0 18.2 %collective-permute-start = (bf16[16,384]{1,0:T(8,128)(2,1)}, bf16[16,384]{1,0:T(8,128)(2,1)S(1)}, u32[]{:S(2)}, u32[]{:S(2)}) collective-permute-start(bf16[16,384]{1,0:T(8,128)(2,1)} %class_rows.1.refs_0_.classes_ref), channel_id=1, source_target_pairs={{0,2},{2,0},{4,6},{6,4},{1,3},{3,1},{5,7},{7,5},{8,10},{10,8},{12,... | collective-permute-start | bytes 36872 | tf_op jit(solution)/shard_map/ppermute | solution.py:854
  7.9 15.3 %collective-permute-start.1 = (bf16[16,384]{1,0:T(8,128)(2,1)}, bf16[16,384]{1,0:T(8,128)(2,1)S(1)}, u32[]{:S(2)}, u32[]{:S(2)}) collective-permute-start(bf16[16,384]{1,0:T(8,128)(2,1)} %class_rows.1.refs_0_.classes_ref), channel_id=1, source_target_pairs={{0,4},{2,6},{4,0},{6,2},{1,5},{3,7},{5,1},{7,3},{8,12},{10,14},{12... | collective-permute-start | bytes 36872 | tf_op jit(solution)/shard_map/ppermute | solution.py:854
  9.4 13.8 %collective-permute-start.2 = (bf16[16,384]{1,0:T(8,128)(2,1)}, bf16[16,384]{1,0:T(8,128)(2,1)S(1)}, u32[]{:S(2)}, u32[]{:S(2)}) collective-permute-start(bf16[16,384]{1,0:T(8,128)(2,1)} %class_rows.1.refs_0_.classes_ref), channel_id=1, source_target_pairs={{0,6},{2,4},{4,2},{6,0},{1,7},{3,5},{5,3},{7,1},{8,14},{10,12},{12... | collective-permute-start | bytes 36872 | tf_op jit(solution)/shard_map/ppermute | solution.py:854
  50.3 28.2 %collective-permute-start.6 = (f32[16,384]{1,0:T(8,128)}, f32[16,384]{1,0:T(8,128)S(1)}, u32[]{:S(2)}, u32[]{:S(2)}) collective-permute-start(f32[16,384]{1,0:T(8,128)} %get-tuple-element.86), channel_id=1, source_target_pairs={{0,2},{2,0},{4,6},{6,4},{1,3},{3,1},{5,7},{7,5},{8,10},{10,8},{12,... | collective-permute-start | bytes 73736 | tf_op jit(solution)/shard_map/ppermute | solution.py:854
  50.8 27.7 %collective-permute-start.7 = (f32[16,384]{1,0:T(8,128)}, f32[16,384]{1,0:T(8,128)S(1)}, u32[]{:S(2)}, u32[]{:S(2)}) collective-permute-start(f32[16,384]{1,0:T(8,128)} %get-tuple-element.87), channel_id=1, source_target_pairs={{0,4},{2,6},{4,0},{6,2},{1,5},{3,7},{5,1},{7,3},{8,12},{10,14},{12... | collective-permute-start | bytes 73736 | tf_op jit(solution)/shard_map/ppermute | solution.py:854
  51.0 27.5 %collective-permute-start.8 = (f32[16,384]{1,0:T(8,128)}, f32[16,384]{1,0:T(8,128)S(1)}, u32[]{:S(2)}, u32[]{:S(2)}) collective-permute-start(f32[16,384]{1,0:T(8,128)} %get-tuple-element.88), channel_id=1, source_target_pairs={{0,6},{2,4},{4,2},{6,0},{1,7},{3,5},{5,3},{7,1},{8,14},{10,12},{12... | collective-permute-start | bytes 73736 | tf_op jit(solution)/shard_map/ppermute | solution.py:854
  78.4 97.3 %collective-permute-start.19 = (bf16[4,4,48,384]{3,2,1,0:T(8,128)(2,1)S(1)}, bf16[4,4,48,384]{3,2,1,0:T(8,128)(2,1)S(1)}, u32[]{:S(2)}, u32[]{:S(2)}) collective-permute-start(bf16[4,4,48,384]{3,2,1,0:T(8,128)(2,1)S(1)} %copy-done.60), channel_id=1, source_target_pairs={{0,1},{1,0},{2,3},{3,2},{4,5},{5,4},{6,7},{7,6},{8,9},{9,8},{10,11... | collective-permute-start | bytes 1769480 | tf_op jit(solution)/shard_map/ppermute | solution.py:854
  123.5 65.7 %collective-permute-start.53 = (bf16[4,4,96,384]{3,2,1,0:T(8,128)(2,1)}, bf16[4,4,96,384]{3,2,1,0:T(8,128)(2,1)S(1)}, u32[]{:S(2)}, u32[]{:S(2)}) collective-permute-start(bf16[4,4,96,384]{3,2,1,0:T(8,128)(2,1)} %get-tuple-element.131), channel_id=1, source_target_pairs={{0,1},{1,0},{2,3},{3,2},{4,5},{5,4},{6,7},{7,6},{8,9},{9,8},{10,11... | collective-permute-start | bytes 3538952 | tf_op jit(solution)/shard_map/ppermute | solution.py:854
  161.1 22.5 %collective-permute-start.36 = (bf16[4,4,48,384]{3,2,1,0:T(8,128)(2,1)}, bf16[4,4,48,384]{3,2,1,0:T(8,128)(2,1)S(1)}, u32[]{:S(2)}, u32[]{:S(2)}) collective-permute-start(bf16[4,4,48,384]{3,2,1,0:T(8,128)(2,1)} %get-tuple-element.117), channel_id=1, source_target_pairs={{0,1},{1,0},{2,3},{3,2},{4,5},{5,4},{6,7},{7,6},{8,9},{9,8},{10,11... | collective-permute-start | bytes 1769480 | tf_op jit(solution)/shard_map/ppermute | solution.py:854
  182.1 11.5 %collective-permute-start.21 = (bf16[4,48,384]{2,1,0:T(8,128)(2,1)}, bf16[4,48,384]{2,1,0:T(8,128)(2,1)S(1)}, u32[]{:S(2)}, u32[]{:S(2)}) collective-permute-start(bf16[4,48,384]{2,1,0:T(8,128)(2,1)} %get-tuple-element.102), channel_id=1, source_target_pairs={{0,4},{2,6},{4,0},{6,2},{1,5},{3,7},{5,1},{7,3},{8,12},{10,14},{12... | collective-permute-start | bytes 442376 | tf_op jit(solution)/shard_map/ppermute | solution.py:854
  183.6 11.3 %collective-permute-start.22 = (bf16[4,48,384]{2,1,0:T(8,128)(2,1)}, bf16[4,48,384]{2,1,0:T(8,128)(2,1)S(1)}, u32[]{:S(2)}, u32[]{:S(2)}) collective-permute-start(bf16[4,48,384]{2,1,0:T(8,128)(2,1)} %get-tuple-element.103), channel_id=1, source_target_pairs={{0,6},{2,4},{4,2},{6,0},{1,7},{3,5},{5,3},{7,1},{8,14},{10,12},{12... | collective-permute-start | bytes 442376 | tf_op jit(solution)/shard_map/ppermute | solution.py:854
  188.5 10.6 %collective-permute-start.38 = (bf16[4,48,384]{2,1,0:T(8,128)(2,1)}, bf16[4,48,384]{2,1,0:T(8,128)(2,1)S(1)}, u32[]{:S(2)}, u32[]{:S(2)}) collective-permute-start(bf16[4,48,384]{2,1,0:T(8,128)(2,1)} %get-tuple-element.120), channel_id=1, source_target_pairs={{0,4},{2,6},{4,0},{6,2},{1,5},{3,7},{5,1},{7,3},{8,12},{10,14},{12... | collective-permute-start | bytes 442376 | tf_op jit(solution)/shard_map/ppermute | solution.py:854
  189.2 9.8 %collective-permute-start.39 = (bf16[4,48,384]{2,1,0:T(8,128)(2,1)}, bf16[4,48,384]{2,1,0:T(8,128)(2,1)S(1)}, u32[]{:S(2)}, u32[]{:S(2)}) collective-permute-start(bf16[4,48,384]{2,1,0:T(8,128)(2,1)} %get-tuple-element.121), channel_id=1, source_target_pairs={{0,6},{2,4},{4,2},{6,0},{1,7},{3,5},{5,3},{7,1},{8,14},{10,12},{12... | collective-permute-start | bytes 442376 | tf_op jit(solution)/shard_map/ppermute | solution.py:854
  193.6 34.1 %collective-permute-start.54 = (bf16[4,96,384]{2,1,0:T(8,128)(2,1)}, bf16[4,96,384]{2,1,0:T(8,128)(2,1)S(1)}, u32[]{:S(2)}, u32[]{:S(2)}) collective-permute-start(bf16[4,96,384]{2,1,0:T(8,128)(2,1)} %get-tuple-element.133), channel_id=1, source_target_pairs={{0,2},{2,0},{4,6},{6,4},{1,3},{3,1},{5,7},{7,5},{8,10},{10,8},{12,... | collective-permute-start | bytes 884744 | tf_op jit(solution)/shard_map/ppermute | solution.py:854
  194.9 33.7 %collective-permute-start.55 = (bf16[4,96,384]{2,1,0:T(8,128)(2,1)}, bf16[4,96,384]{2,1,0:T(8,128)(2,1)S(1)}, u32[]{:S(2)}, u32[]{:S(2)}) collective-permute-start(bf16[4,96,384]{2,1,0:T(8,128)(2,1)} %get-tuple-element.134), channel_id=1, source_target_pairs={{0,4},{2,6},{4,0},{6,2},{1,5},{3,7},{5,1},{7,3},{8,12},{10,14},{12... | collective-permute-start | bytes 884744 | tf_op jit(solution)/shard_map/ppermute | solution.py:854
  195.5 34.7 %collective-permute-start.56 = (bf16[4,96,384]{2,1,0:T(8,128)(2,1)}, bf16[4,96,384]{2,1,0:T(8,128)(2,1)S(1)}, u32[]{:S(2)}, u32[]{:S(2)}) collective-permute-start(bf16[4,96,384]{2,1,0:T(8,128)(2,1)} %get-tuple-element.135), channel_id=1, source_target_pairs={{0,6},{2,4},{4,2},{6,0},{1,7},{3,5},{5,3},{7,1},{8,14},{10,12},{12... | collective-permute-start | bytes 884744 | tf_op jit(solution)/shard_map/ppermute | solution.py:854
  199.1 9.6 %collective-permute-start.24 = (bf16[48,384]{1,0:T(8,128)(2,1)}, bf16[48,384]{1,0:T(8,128)(2,1)S(1)}, u32[]{:S(2)}, u32[]{:S(2)}) collective-permute-start(bf16[48,384]{1,0:T(8,128)(2,1)} %get-tuple-element.106), channel_id=1, source_target_pairs={{0,16},{8,24},{16,0},{24,8},{1,17},{9,25},{17,1},{25,9},{2,18},{10... | collective-permute-start | bytes 110600 | tf_op jit(solution)/shard_map/ppermute | solution.py:854
  227.7 22.0 %collective-permute-start.29 = (bf16[4,48,384]{2,1,0:T(8,128)(2,1)}, bf16[4,48,384]{2,1,0:T(8,128)(2,1)S(1)}, u32[]{:S(2)}, u32[]{:S(2)}) collective-permute-start(bf16[4,48,384]{2,1,0:T(8,128)(2,1)} %stack.21.refs_0_), channel_id=1, source_target_pairs={{0,2},{2,0},{4,6},{6,4},{1,3},{3,1},{5,7},{7,5},{8,10},{10,8},{12,... | collective-permute-start | bytes 442376 | tf_op jit(solution)/shard_map/ppermute | solution.py:854
  233.0 18.4 %collective-permute-start.57 = (bf16[96,384]{1,0:T(8,128)(2,1)}, bf16[96,384]{1,0:T(8,128)(2,1)S(1)}, u32[]{:S(2)}, u32[]{:S(2)}) collective-permute-start(bf16[96,384]{1,0:T(8,128)(2,1)} %get-tuple-element.137), channel_id=1, source_target_pairs={{0,8},{8,0},{16,24},{24,16},{1,9},{9,1},{17,25},{25,17},{2,10},{10... | collective-permute-start | bytes 221192 | tf_op jit(solution)/shard_map/ppermute | solution.py:854
  234.3 17.0 %collective-permute-start.58 = (bf16[96,384]{1,0:T(8,128)(2,1)}, bf16[96,384]{1,0:T(8,128)(2,1)S(1)}, u32[]{:S(2)}, u32[]{:S(2)}) collective-permute-start(bf16[96,384]{1,0:T(8,128)(2,1)} %get-tuple-element.138), channel_id=1, source_target_pairs={{0,16},{8,24},{16,0},{24,8},{1,17},{9,25},{17,1},{25,9},{2,18},{10... | collective-permute-start | bytes 221192 | tf_op jit(solution)/shard_map/ppermute | solution.py:854
  237.3 9.6 %collective-permute-start.45 = (bf16[48,384]{1,0:T(8,128)(2,1)}, bf16[48,384]{1,0:T(8,128)(2,1)S(1)}, u32[]{:S(2)}, u32[]{:S(2)}) collective-permute-start(bf16[48,384]{1,0:T(8,128)(2,1)} %add_last.4.refs_0_), channel_id=1, source_target_pairs={{0,24},{8,16},{16,8},{24,0},{1,25},{9,17},{17,9},{25,1},{2,26},{10... | collective-permute-start | bytes 110600 | tf_op jit(solution)/shard_map/ppermute | solution.py:854
  256.2 13.4 %collective-permute-start.48 = (bf16[4,48,384]{2,1,0:T(8,128)(2,1)}, bf16[4,48,384]{2,1,0:T(8,128)(2,1)S(1)}, u32[]{:S(2)}, u32[]{:S(2)}) collective-permute-start(bf16[4,48,384]{2,1,0:T(8,128)(2,1)} %stack.22.refs_0_), channel_id=1, source_target_pairs={{0,6},{2,4},{4,2},{6,0},{1,7},{3,5},{5,3},{7,1},{8,14},{10,12},{12... | collective-permute-start | bytes 442376 | tf_op jit(solution)/shard_map/ppermute | solution.py:854
  258.6 13.0 %collective-permute-start.49 = (bf16[4,48,384]{2,1,0:T(8,128)(2,1)}, bf16[4,48,384]{2,1,0:T(8,128)(2,1)S(1)}, u32[]{:S(2)}, u32[]{:S(2)}) collective-permute-start(bf16[4,48,384]{2,1,0:T(8,128)(2,1)} %stack.22.refs_0_), channel_id=1, source_target_pairs={{0,1},{1,0},{2,3},{3,2},{4,5},{5,4},{6,7},{7,6},{8,9},{9,8},{10,11... | collective-permute-start | bytes 442376 | tf_op jit(solution)/shard_map/ppermute | solution.py:854
  258.7 14.3 %collective-permute-start.33 = (bf16[4,48,384]{2,1,0:T(8,128)(2,1)S(1)}, bf16[4,48,384]{2,1,0:T(8,128)(2,1)S(1)}, u32[]{:S(2)}, u32[]{:S(2)}) collective-permute-start(bf16[4,48,384]{2,1,0:T(8,128)(2,1)S(1)} %collective-permute-done.29.refs_1_), channel_id=1, source_target_pairs={{0,1},{1,0},{2,3},{3,2},{4,5},{5,4},{6,7},{7,6},{8,9},{9,8},{10,11... | collective-permute-start | bytes 442376 | tf_op jit(solution)/shard_map/ppermute | solution.py:854
  269.6 10.1 %collective-permute-start.63 = (bf16[4,96,384]{2,1,0:T(8,128)(2,1)}, bf16[4,96,384]{2,1,0:T(8,128)(2,1)S(1)}, u32[]{:S(2)}, u32[]{:S(2)}) collective-permute-start(bf16[4,96,384]{2,1,0:T(8,128)(2,1)} %stack.23.refs_0_), channel_id=1, source_target_pairs={{0,2},{2,0},{4,6},{6,4},{1,3},{3,1},{5,7},{7,5},{8,10},{10,8},{12,... | collective-permute-start | bytes 884744 | tf_op jit(solution)/shard_map/ppermute | solution.py:854
  271.7 15.7 %collective-permute-start.64 = (bf16[4,96,384]{2,1,0:T(8,128)(2,1)}, bf16[4,96,384]{2,1,0:T(8,128)(2,1)S(1)}, u32[]{:S(2)}, u32[]{:S(2)}) collective-permute-start(bf16[4,96,384]{2,1,0:T(8,128)(2,1)} %stack.23.refs_0_), channel_id=1, source_target_pairs={{0,4},{2,6},{4,0},{6,2},{1,5},{3,7},{5,1},{7,3},{8,12},{10,14},{12... | collective-permute-start | bytes 884744 | tf_op jit(solution)/shard_map/ppermute | solution.py:854
  273.0 14.3 %collective-permute-start.65 = (bf16[4,96,384]{2,1,0:T(8,128)(2,1)}, bf16[4,96,384]{2,1,0:T(8,128)(2,1)S(1)}, u32[]{:S(2)}, u32[]{:S(2)}) collective-permute-start(bf16[4,96,384]{2,1,0:T(8,128)(2,1)} %stack.23.refs_0_), channel_id=1, source_target_pairs={{0,6},{2,4},{4,2},{6,0},{1,7},{3,5},{5,3},{7,1},{8,14},{10,12},{12... | collective-permute-start | bytes 884744 | tf_op jit(solution)/shard_map/ppermute | solution.py:854
  279.1 33.7 %collective-permute-start.52 = (bf16[4,48,384]{2,1,0:T(8,128)(2,1)S(1)}, bf16[4,48,384]{2,1,0:T(8,128)(2,1)S(1)}, u32[]{:S(2)}, u32[]{:S(2)}) collective-permute-start(bf16[4,48,384]{2,1,0:T(8,128)(2,1)S(1)} %collective-permute-done.48.refs_3_), channel_id=1, source_target_pairs={{0,1},{1,0},{2,3},{3,2},{4,5},{5,4},{6,7},{7,6},{8,9},{9,8},{10,11... | collective-permute-start | bytes 442376 | tf_op jit(solution)/shard_map/ppermute | solution.py:854
  279.3 37.3 %collective-permute-start.66 = (bf16[4,96,384]{2,1,0:T(8,128)(2,1)S(1)}, bf16[4,96,384]{2,1,0:T(8,128)(2,1)S(1)}, u32[]{:S(2)}, u32[]{:S(2)}) collective-permute-start(bf16[4,96,384]{2,1,0:T(8,128)(2,1)S(1)} %copy-done.2), channel_id=1, source_target_pairs={{0,1},{1,0},{2,3},{3,2},{4,5},{5,4},{6,7},{7,6},{8,9},{9,8},{10,11... | collective-permute-start | bytes 884744 | tf_op jit(solution)/shard_map/ppermute | solution.py:854
  279.7 36.8 %collective-permute-start.67 = (bf16[4,96,384]{2,1,0:T(8,128)(2,1)S(1)}, bf16[4,96,384]{2,1,0:T(8,128)(2,1)S(1)}, u32[]{:S(2)}, u32[]{:S(2)}) collective-permute-start(bf16[4,96,384]{2,1,0:T(8,128)(2,1)S(1)} %collective-permute-done.63.refs_1_), channel_id=1, source_target_pairs={{0,1},{1,0},{2,3},{3,2},{4,5},{5,4},{6,7},{7,6},{8,9},{9,8},{10,11... | collective-permute-start | bytes 884744 | tf_op jit(solution)/shard_map/ppermute | solution.py:854
  287.3 29.3 %collective-permute-start.68 = (bf16[4,96,384]{2,1,0:T(8,128)(2,1)S(1)}, bf16[4,96,384]{2,1,0:T(8,128)(2,1)S(1)}, u32[]{:S(2)}, u32[]{:S(2)}) collective-permute-start(bf16[4,96,384]{2,1,0:T(8,128)(2,1)S(1)} %collective-permute-done.64.refs_2_), channel_id=1, source_target_pairs={{0,1},{1,0},{2,3},{3,2},{4,5},{5,4},{6,7},{7,6},{8,9},{9,8},{10,11... | collective-permute-start | bytes 884744 | tf_op jit(solution)/shard_map/ppermute | solution.py:854
  287.3 29.3 %collective-permute-start.69 = (bf16[4,96,384]{2,1,0:T(8,128)(2,1)S(1)}, bf16[4,96,384]{2,1,0:T(8,128)(2,1)S(1)}, u32[]{:S(2)}, u32[]{:S(2)}) collective-permute-start(bf16[4,96,384]{2,1,0:T(8,128)(2,1)S(1)} %collective-permute-done.65.refs_3_), channel_id=1, source_target_pairs={{0,1},{1,0},{2,3},{3,2},{4,5},{5,4},{6,7},{7,6},{8,9},{9,8},{10,11... | collective-permute-start | bytes 884744 | tf_op jit(solution)/shard_map/ppermute | solution.py:854
  (111 other events, 984.2 us)

commit v2 on v1

v2 whole, which is shorter than its diff:
```python
import functools

import jax
import jax.numpy as jnp
from jax import lax
from jax.experimental import pallas as pl
from jax.experimental.pallas import tpu as pltpu
from jax.sharding import PartitionSpec as P

HEADS = 6
HEAD_DIM = 64
EPS = 1e-05
SCALE = 0.125
MASKED = -1e30
BIG = 56 * 1024 * 1024

f32 = jnp.float32
bf16 = jnp.bfloat16


def nn(a, b):
    return lax.dot_general(a, b, (((1,), (0,)), ((), ())), preferred_element_type=f32)


def nt(a, b):
    return lax.dot_general(a, b, (((1,), (1,)), ((), ())), preferred_element_type=f32)


def tn(a, b):
    return lax.dot_general(a, b, (((0,), (0,)), ((), ())), preferred_element_type=f32)


def exact(a, b):
    return lax.dot_general(
        a, b, (((1,), (0,)), ((), ())), precision=lax.Precision.HIGHEST, preferred_element_type=f32
    )


def unit_norm(x):
    center = x - jnp.mean(x, axis=-1, keepdims=True)
    inv = lax.rsqrt(jnp.mean(center * center, axis=-1, keepdims=True) + EPS)
    return center * inv, inv


def norm_back(unit, inv, gain, dy):
    du = dy * gain
    mean_du = jnp.mean(du, axis=-1, keepdims=True)
    mean_dot = jnp.mean(du * unit, axis=-1, keepdims=True)
    return inv * (du - mean_du - unit * mean_dot)


def row_sum(x):
    return jnp.sum(x, axis=0, keepdims=True)


def sigmoid(x):
    return 0.5 + 0.5 * jnp.tanh(0.5 * x)


def head_mask(shape, lane_dim, head):
    lane = lax.broadcasted_iota(jnp.int32, shape, lane_dim)
    return (lane >= head * HEAD_DIM) & (lane < (head + 1) * HEAD_DIM)


def head_columns(width):
    lane = lax.broadcasted_iota(jnp.int32, (width, 128), 0)
    col = lax.broadcasted_iota(jnp.int32, (width, 128), 1)
    return ((lane >= col * HEAD_DIM) & (lane < (col + 1) * HEAD_DIM)).astype(f32)


def head_rows(width):
    col = lax.broadcasted_iota(jnp.int32, (128, width), 0)
    lane = lax.broadcasted_iota(jnp.int32, (128, width), 1)
    return ((lane >= col * HEAD_DIM) & (lane < (col + 1) * HEAD_DIM)).astype(f32)


def pad_rows(x, rows):
    if x.shape[0] == rows:
        return x
    return jnp.concatenate([x, jnp.zeros((rows - x.shape[0], x.shape[1]), x.dtype)], axis=0)


def put_row(block, at, row):
    top = at // 16 * 16
    tail = block[top : top + 16]
    index = lax.broadcasted_iota(jnp.int32, tail.shape, 0)
    tail = jnp.where(index == at - top, row, tail)
    pieces = [tail]
    if top:
        pieces.insert(0, block[:top])
    if top + 16 < block.shape[0]:
        pieces.append(block[top + 16 :])
    return jnp.concatenate(pieces, axis=0) if len(pieces) > 1 else tail


def full(shape):
    return pl.BlockSpec(shape, lambda *_: (0,) * len(shape))


def frame_block(shape):
    return pl.BlockSpec((1,) + shape, lambda i, *_: (i, 0, 0))


def frames_block(batch, shape):
    return pl.BlockSpec((batch,) + shape, lambda i, *_: (i, 0, 0))


def stagger(jobs, stages, gap):
    for at in range(len(jobs) + (len(stages) - 1) * gap):
        for k, stage in enumerate(stages):
            j = at - k * gap
            if 0 <= j < len(jobs):
                stage(jobs[j])


def share_of(count, most):
    return max(b for b in range(1, most + 1) if count % b == 0)


def square(width, *at):
    return pl.BlockSpec((None,) * len(at) + (width, width), lambda *_: at + (0, 0))


def scalars():
    return pl.BlockSpec(memory_space=pltpu.SMEM)


def shape_of(shape, dtype):
    return jax.ShapeDtypeStruct(shape, dtype)


def params(limit=BIG):
    return pltpu.CompilerParams(vmem_limit_bytes=limit)


def cost(flops, nbytes):
    return pl.CostEstimate(flops=int(flops), bytes_accessed=int(nbytes), transcendentals=0)


def class_kernel(video_ref, out_ref):
    clips, _, micro, width = video_ref.shape
    rows = [video_ref[c, 0, m : m + 1, :].astype(f32) for m in range(micro) for c in range(clips)]
    out_ref[...] = pad_rows(jnp.concatenate(rows, axis=0), out_ref.shape[0]).astype(bf16)


def class_rows(video, slots):
    micro, clips, per_frame, patch, width = video.shape
    turned = video.transpose(1, 2, 3, 0, 4).reshape(clips * per_frame, patch, micro, width)
    return pl.pallas_call(
        class_kernel,
        grid=(1,),
        in_specs=[pl.BlockSpec((clips * per_frame, 1, micro, width), lambda i: (0, 0, 0, 0))],
        out_specs=full((slots, width)),
        out_shape=shape_of((slots, width), bf16),
        name="class_rows",
    )(turned)


def norm_kernel(video_ref, gains_ref, wk_ref, wv_ref, normed_ref, kv_ref, wkv):
    batch, rows, width = normed_ref.shape

    @pl.when(pl.program_id(0) == 0)
    def _():
        wkv[:, :width] = wk_ref[...]
        wkv[:, width:] = wv_ref[...]

    parts = []
    for i in range(batch):
        unit, _ = unit_norm(video_ref[i].astype(f32))
        parts.append(pad_rows(unit * gains_ref[0:1, :], rows).astype(bf16))
        normed_ref[i] = parts[i]
    normed = jnp.concatenate(parts, axis=0)
    kv_ref[...] = nn(normed, wkv[...]).astype(bf16).reshape(batch, rows, 2 * width)


def norm_tokens(video, gains, qkv, rows):
    count, patch, width = video.shape
    batch = share_of(count, 5)
    return pl.pallas_call(
        norm_kernel,
        grid=(count // batch,),
        in_specs=[
            frames_block(batch, (patch, width)),
            full(gains.shape),
            square(width, 1, 1),
            square(width, 1, 2),
        ],
        out_specs=[
            frames_block(batch, (rows, width)),
            frames_block(batch, (rows, 2 * width)),
        ],
        out_shape=[
            shape_of((count, rows, width), bf16),
            shape_of((count, rows, 2 * width), bf16),
        ],
        scratch_shapes=[pltpu.VMEM((width, 2 * width), bf16)],
        compiler_params=params(),
        cost_estimate=cost(4 * count * rows * width * width, 8 * count * rows * width),
        name="norm_tokens",
    )(video, gains, qkv, qkv)


def message_scores(query, keys, columns):
    return [exact(query.astype(f32) * key.astype(f32), columns) * SCALE for key in keys]


def message_probs(scores):
    top = functools.reduce(jnp.maximum, scores)
    expo = [jnp.exp(score - top) for score in scores]
    total = functools.reduce(jnp.add, expo)
    return [e / total for e in expo]


def first_kernel(
    pieces, count, tokens, *refs
):
    gathered = refs[:pieces]
    (
        mw_ref, mg_ref, qkv_ref, outw_ref, up_ref, down_ref, gains_ref, kv_ref,
        message_ref, nmsg_ref, kvmsg_ref, visual_ref, final_ref, ctx,
    ) = refs[pieces:]
    width = mw_ref.shape[0]
    slots = gathered[0].shape[0]
    rows = kv_ref.shape[1]
    classes = jnp.concatenate([g[...] for g in gathered], axis=0)
    start = nn(classes, mw_ref[...]).astype(bf16)
    unit, _ = unit_norm(start.astype(f32))
    normed = (unit * mg_ref[...]).astype(bf16)
    keys = nn(normed, qkv_ref[0, 1]).astype(bf16)
    values = nn(normed, qkv_ref[0, 2]).astype(bf16)
    query = nn(normed[:slots], qkv_ref[0, 0]).astype(bf16)
    columns, spread = head_columns(width), head_rows(width).astype(bf16)
    cut = [slice(g * slots, (g + 1) * slots) for g in range(pieces)]
    probs = message_probs(message_scores(query, [keys[c] for c in cut], columns))
    context = functools.reduce(
        jnp.add,
        [nn(p.astype(bf16), spread) * values[c].astype(f32) for p, c in zip(probs, cut)],
    ).astype(bf16)
    message = start[:slots].astype(f32) + nn(context, outw_ref[0])
    message_ref[...] = message
    unit, _ = unit_norm(message)
    nmsg = (unit * gains_ref[0:1, :]).astype(bf16)
    nmsg_ref[...] = nmsg.astype(f32)
    kmsg = nn(nmsg, qkv_ref[1, 1]).astype(bf16).astype(f32)
    vmsg = nn(nmsg, qkv_ref[1, 2]).astype(bf16).astype(f32)

    own = gathered[0][...].astype(f32)
    unit, _ = unit_norm(own)
    qcls = nn((unit * gains_ref[0:1, :]).astype(bf16), qkv_ref[1, 0]).astype(bf16).astype(f32) * SCALE
    head = lax.broadcasted_iota(jnp.int32, (16, width), 0)
    lane = lax.broadcasted_iota(jnp.int32, (16, width), 1)
    mine = (lane >= head * HEAD_DIM) & (lane < (head + 1) * HEAD_DIM)
    token = lax.broadcasted_iota(jnp.int32, (16, rows), 1)
    ctx[...] = jnp.zeros(ctx.shape, f32)
    kvmsg_ref[:, :width] = kmsg
    kvmsg_ref[:, width:] = vmsg
    queries = [jnp.where(mine, qcls[i : i + 1], 0.0) for i in range(count)]
    scores = [nt(queries[i].astype(bf16), kv_ref[i, :, :width]) for i in range(count)]
    probs = []
    for i in range(count):
        last = jnp.sum(queries[i] * kmsg[i : i + 1], axis=1, keepdims=True)
        score = jnp.where(token == tokens - 1, last, scores[i])
        score = jnp.where(token < tokens, score, MASKED)
        expo = jnp.exp(score - jnp.max(score, axis=1, keepdims=True))
        probs.append((expo / jnp.sum(expo, axis=1, keepdims=True)).astype(bf16))
    outs = [nn(probs[i], kv_ref[i, :, width:]) for i in range(count)]
    for i in range(count):
        extra = jnp.sum(
            jnp.where(token == tokens - 1, probs[i].astype(f32), 0.0), axis=1, keepdims=True
        )
        out = outs[i] + extra * vmsg[i : i + 1]
        ctx[i : i + 1, :] = row_sum(jnp.where(mine, out, 0.0))
    resid = own + nn(ctx[...].astype(bf16), outw_ref[1])
    unit, _ = unit_norm(resid)
    hidden = nn((unit * gains_ref[1:2, :]).astype(bf16), up_ref[...])
    active = (hidden * sigmoid(1.702 * hidden)).astype(bf16)
    final = resid + nn(active, down_ref[...])
    final_ref[...] = final
    unit, _ = unit_norm(final)
    visual_ref[...] = (unit * gains_ref[2:3, :]).astype(bf16)


def first_rows(gathered, mw, mg, qkv, outw, up, down, gains, kv, tokens):
    count, width = kv.shape[0], mw.shape[0]
    slots = gathered[0].shape[0]
    operands = list(gathered) + [mw, mg, qkv, outw, up, down, gains, kv]
    return pl.pallas_call(
        functools.partial(first_kernel, len(gathered), count, tokens),
        grid=(1,),
        in_specs=[full(x.shape) for x in operands],
        out_specs=[full((slots, width))] * 2 + [full((slots, 2 * width))] + [full((slots, width))] * 2,
        out_shape=[
            shape_of((slots, width), f32),
            shape_of((slots, width), f32),
            shape_of((slots, 2 * width), f32),
            shape_of((slots, width), bf16),
            shape_of((slots, width), f32),
        ],
        scratch_shapes=[pltpu.VMEM((slots, width), f32)],
        compiler_params=params(),
        cost_estimate=cost(4e9, 12e6),
        name="first_rows",
    )(*operands)


def with_message(block, rows_ref, tokens, frame):
    top = (tokens - 1) // 16 * 16
    tail = block[top : top + 16].astype(f32)
    index = lax.broadcasted_iota(jnp.int32, tail.shape, 0)
    tail = jnp.where(index == tokens - 1 - top, rows_ref[pl.ds(frame, 1), :], tail).astype(bf16)
    pieces = [block[:top], tail]
    if top + 16 < block.shape[0]:
        pieces.append(block[top + 16 :])
    return jnp.concatenate(pieces, axis=0)


def masked_tail(scores, tokens):
    top = tokens // 16 * 16
    if top >= scores.shape[0]:
        return scores
    tail = scores[top:]
    index = lax.broadcasted_iota(jnp.int32, tail.shape, 0)
    return jnp.concatenate([scores[:top], jnp.where(index < tokens - top, tail, MASKED)], axis=0)


def half_pair(block_t, head):
    own = block_t[head * HEAD_DIM : (head + 1) * HEAD_DIM]
    none = jnp.zeros(own.shape, own.dtype)
    return jnp.concatenate([own, none] if head % 2 == 0 else [none, own], axis=0)


def pair_lanes(block, head):
    at = head // 2 * 2 * HEAD_DIM
    return block[:, at : at + 2 * HEAD_DIM]


def attend_kernel(
    tokens, normed_ref, kv_ref, video_ref, message_ref, nmsg_ref, kvmsg_ref, wq_ref, wv_ref, wo_ref,
    resid_ref, ctx_ref, lse_ref, wqt, wvt,
):
    step = pl.program_id(0)

    @pl.when(step == 0)
    def _():
        wqt[...] = wq_ref[...].T
        wvt[...] = wv_ref[...].T

    batch, rows, width = normed_ref.shape
    normed, keys = [], []
    for i in range(batch):
        frame = step * batch + i
        normed.append(with_message(normed_ref[i], nmsg_ref, tokens, frame))
        keys.append(with_message(kv_ref[i], kvmsg_ref, tokens, frame))
    queries_t = [nt(wqt[...], n).astype(bf16) * jnp.bfloat16(SCALE) for n in normed]
    values_t = [nt(wvt[...], n).astype(bf16) for n in normed]
    jobs = [(i, h) for i in range(batch) for h in range(HEADS)]
    contexts, stats, scores, expos, totals = {}, {}, {}, {}, {}

    def score(job):
        i, head = job
        scores[job] = nn(pair_lanes(keys[i], head), half_pair(queries_t[i], head))

    def soften(job):
        one = masked_tail(scores.pop(job), tokens)
        top = jnp.max(one, axis=0, keepdims=True)
        expo = jnp.exp(one - top)
        totals[job] = row_sum(expo)
        expos[job] = expo.astype(bf16)
        stats[job] = top + jnp.log(totals[job])

    def mix(job):
        i, head = job
        own = values_t[i][head * HEAD_DIM : (head + 1) * HEAD_DIM]
        contexts[job] = nn(own, expos.pop(job)) * (1.0 / totals[job])

    stagger(jobs, [score, soften, mix], 3)
    for i in range(batch):
        context_t = jnp.concatenate([contexts[i, h] for h in range(HEADS)], axis=0).astype(bf16)
        ctx_ref[i] = context_t
        pad = [jnp.zeros((8 - HEADS, rows), f32)]
        lse_ref[i] = jnp.concatenate([stats[i, h] for h in range(HEADS)] + pad, axis=0)
        row = message_ref[pl.ds(step * batch + i, 1), :]
        base = put_row(pad_rows(video_ref[i].astype(f32), rows), tokens - 1, row)
        resid_ref[i] = base + tn(context_t, wo_ref[...])


def attend(normed, kv, video, message, nmsg, kvmsg, qkv, outw, tokens):
    count, rows, width = normed.shape
    slots = message.shape[0]
    batch = share_of(count, 2)
    return pl.pallas_call(
        functools.partial(attend_kernel, tokens),
        grid=(count // batch,),
        in_specs=[
            frames_block(batch, (rows, width)),
            frames_block(batch, (rows, 2 * width)),
            frames_block(batch, video.shape[1:]),
            full((slots, width)),
            full((slots, width)),
            full((slots, 2 * width)),
            square(width, 1, 0),
            square(width, 1, 2),
            square(width, 1),
        ],
        out_specs=[
            frames_block(batch, (rows, width)),
            frames_block(batch, (width, rows)),
            frames_block(batch, (8, rows)),
        ],
        out_shape=[
            shape_of((count, rows, width), f32),
            shape_of((count, width, rows), bf16),
            shape_of((count, 8, rows), f32),
        ],
        scratch_shapes=[pltpu.VMEM((width, width), bf16)] * 2,
        compiler_params=params(),
        cost_estimate=cost(14e9, 10e6),
        name="attend",
    )(normed, kv, video, message, nmsg, kvmsg, qkv, qkv, outw)


def caption_kernel(
    pieces, groups, clips, local, where_ref, lengths_ref, *refs
):
    gathered = refs[:pieces]
    caps_ref, cot_ref, qkv_ref, outw_ref, gains_ref = refs[pieces : pieces + 5]
    out_ref, grad_ref, gain_ref = refs[pieces + 5 : pieces + 8]
    part_refs = refs[pieces + 8 : pieces + 8 + pieces]
    keep_ref, send_ref, acc = refs[pieces + 8 + pieces :]
    width = caps_ref.shape[1]
    slots = gathered[0].shape[0]
    count = caps_ref.shape[0]
    keys_n = pieces * slots
    runs = lengths_ref.shape[1]

    token = lax.broadcasted_iota(jnp.int32, (count, keys_n), 0)
    key = lax.broadcasted_iota(jnp.int32, (count, keys_n), 1)
    slot = key % slots
    group = token // local
    position = token - group * local + where_ref[0] * local
    document = jnp.zeros((count, keys_n), jnp.int32)
    for m in range(groups):
        end = jnp.int32(0)
        for j in range(runs):
            end = end + lengths_ref[m, j]
            document = document + jnp.where((group == m) & (position >= end), 1, 0)
    allowed = slot == group * clips + document % clips
    valid = (document[:, 0:1] < runs - 1).astype(f32)

    pack = caps_ref[...].astype(f32)
    unit, inv = unit_norm(pack)
    gain = gains_ref[3:4, :]
    normed = (unit * gain).astype(bf16)
    visual = jnp.concatenate([g[...] for g in gathered], axis=0)
    queries = nn(normed, qkv_ref[2, 0]).astype(bf16)
    keys = nn(visual, qkv_ref[2, 1]).astype(bf16)
    values = nn(visual, qkv_ref[2, 2]).astype(bf16)

    masks = [head_mask((count, width), 1, h) for h in range(HEADS)]
    zero = jnp.zeros((count, width), bf16)

    def by_head(x):
        return jnp.concatenate([jnp.where(m, x, zero) for m in masks], axis=0)

    def merge(x):
        cut = [x[h * count : (h + 1) * count] for h in range(HEADS)]
        return functools.reduce(jnp.add, [jnp.where(m, c, 0.0) for m, c in zip(masks, cut)])

    allowed_all = jnp.concatenate([allowed.astype(jnp.int32)] * HEADS, axis=0) > 0
    split_q = by_head(queries)
    scores = jnp.where(allowed_all, nt(split_q, keys) * SCALE, MASKED)
    expo = jnp.exp(scores - jnp.max(scores, axis=1, keepdims=True))
    probs = expo / jnp.sum(expo, axis=1, keepdims=True)
    low = probs.astype(bf16)
    context = merge(nn(low, values)).astype(bf16)
    out_ref[...] = (pack + valid * nn(context, outw_ref[2])).astype(bf16)

    cot = cot_ref[...].astype(f32)
    branch = (cot * valid).astype(bf16)
    split_d = by_head(nt(branch, outw_ref[2]).astype(bf16))
    dvalues = tn(low, split_d)
    dprobs = nt(split_d, values)
    dscores = probs * (dprobs - jnp.sum(dprobs * probs, axis=1, keepdims=True))
    dscores = jnp.where(allowed_all, dscores, 0.0).astype(bf16)
    dqueries = (merge(nn(dscores, keys)) * SCALE).astype(bf16)
    dkeys = tn(dscores, split_q) * SCALE
    dnormed = nt(dqueries, qkv_ref[2, 0])
    grad_ref[...] = (cot + norm_back(unit, inv, gain, dnormed)).astype(bf16)
    gain_ref[...] = jnp.concatenate([row_sum(dnormed * unit), jnp.zeros((7, width), f32)], axis=0)
    low_k, low_v = dkeys.astype(bf16), dvalues.astype(bf16)
    part = nt(low_k, qkv_ref[2, 1]) + nt(low_v, qkv_ref[2, 2])
    for g in range(pieces):
        part_refs[g][...] = part[g * slots : (g + 1) * slots]
    if acc.shape[0] > 4 * width:
        acc[...] = jnp.zeros(acc.shape, f32)
    acc[0:width, :] = tn(normed, dqueries)
    acc[width : 2 * width, :] = tn(visual, low_k)
    acc[2 * width : 3 * width, :] = tn(visual, low_v)
    acc[3 * width : 4 * width, :] = tn(context, branch)
    emit(where_ref, acc, keep_ref, send_ref)


def captions_step(where, lengths, gathered, caps, cot, qkv, outw, gains, plan):
    count, width = caps.shape
    groups = lengths.shape[0]
    pieces = len(gathered)
    slots = gathered[0].shape[0]
    operands = list(gathered) + [caps, cot, qkv, outw, gains]
    acc_rows, packet_specs, packet_shapes = plan.packet(4 * width, width)
    return pl.pallas_call(
        functools.partial(caption_kernel, pieces, groups, plan.clips, count // groups),
        grid=(1,),
        in_specs=[scalars(), scalars()] + [full(x.shape) for x in operands],
        out_specs=[full((count, width))] * 2
        + [full((8, width))]
        + [full((slots, width))] * pieces
        + packet_specs,
        out_shape=[shape_of((count, width), bf16)] * 2
        + [shape_of((8, width), f32)]
        + [shape_of((slots, width), f32)] * pieces
        + packet_shapes,
        scratch_shapes=[pltpu.VMEM((acc_rows, width), f32)],
        compiler_params=params(),
        cost_estimate=cost(4e9, 8e6),
        name="captions_step",
    )(where, lengths, *operands)


def mlp_kernel(
    pieces, patch, ff, where_ref, resid_ref, cot_ref, final_ref, gains_ref, up_ref, down_ref, *refs
):
    parts = refs[:pieces]
    more_keep, more_send, out_ref, dresid_ref, gain_ref, keep_ref, send_ref, acc, dcls = refs[pieces:]
    step = pl.program_id(0)
    batch, rows, width = resid_ref.shape
    wide = acc.shape[1]
    blocks = ff // wide

    @pl.when(step == 0)
    def _():
        acc[...] = jnp.zeros(acc.shape, f32)
        dvisual = functools.reduce(jnp.add, [p[...] for p in parts])
        unit, inv = unit_norm(final_ref[...])
        dcls[...] = norm_back(unit, inv, gains_ref[2:3, :], dvisual)
        gain_ref[...] = jnp.concatenate(
            [jnp.zeros((1, width), f32), row_sum(dvisual * unit), jnp.zeros((6, width), f32)],
            axis=0,
        )

    resid = resid_ref[...].reshape(batch * rows, width)
    gain = gains_ref[1:2, :]
    unit, inv = unit_norm(resid)
    normed32 = unit * gain
    normed = normed32.astype(bf16)
    normed_t = normed32.T.astype(bf16)
    pieces_d = []
    for i in range(batch):
        one = pad_rows(cot_ref[i].astype(f32), rows)
        pieces_d.append(put_row(one, 0, one[0:1] + dcls[pl.ds(step * batch + i, 1), :]))
    dfinal = jnp.concatenate(pieces_d, axis=0)
    branch = dfinal.astype(bf16)
    branch_t = dfinal.T.astype(bf16)
    final = resid
    dnormed = jnp.zeros((batch * rows, width), f32)
    for c in range(blocks):
        span = slice(c * wide, (c + 1) * wide)
        hidden = nn(normed, up_ref[:, span])
        gate = sigmoid(1.702 * hidden)
        active = (hidden * gate).astype(bf16)
        final = final + nn(active, down_ref[span, :])
        dactive = nt(branch, down_ref[span, :])
        dhidden = (dactive * gate * (1.0 + 1.702 * hidden * (1.0 - gate))).astype(bf16)
        dnormed = dnormed + nt(dhidden, up_ref[:, span])
        acc[c * width : (c + 1) * width, :] += nn(normed_t, dhidden)
        acc[(blocks + c) * width : (blocks + c + 1) * width, :] += nn(branch_t, active)
    for i in range(batch):
        out_ref[i] = final[i * rows : i * rows + patch].astype(bf16)
    dresid = dfinal + norm_back(unit, inv, gain, dnormed)
    dresid_ref[...] = dresid.reshape(batch, rows, width)
    gain_ref[0:1, :] += row_sum(dnormed * unit)

    @pl.when(step == pl.num_programs(0) - 1)
    def _():
        emit(where_ref, acc, keep_ref, send_ref, more_keep, more_send)


def mlp_step(where, resid, cot, final, gains, up, down, parts, more, plan):
    count, rows, width = resid.shape
    patch = cot.shape[1]
    ff = up.shape[1]
    slots = final.shape[0]
    batch = share_of(count, 2)
    wide = 2 * width
    acc_rows, packet_specs, packet_shapes = plan.packet(
        2 * ff * width // wide, wide, more[0].shape[-1]
    )
    return pl.pallas_call(
        functools.partial(mlp_kernel, len(parts), patch, ff),
        grid=(count // batch,),
        in_specs=[
            scalars(),
            frames_block(batch, (rows, width)),
            frames_block(batch, (patch, width)),
            full((slots, width)),
            full(gains.shape),
            full(up.shape),
            full(down.shape),
        ]
        + [full((slots, width))] * len(parts)
        + [full(x.shape) for x in more],
        out_specs=[
            frames_block(batch, (patch, width)),
            frames_block(batch, (rows, width)),
            full((8, width)),
        ]
        + packet_specs,
        out_shape=[
            shape_of((count, patch, width), bf16),
            shape_of((count, rows, width), f32),
            shape_of((8, width), f32),
        ]
        + packet_shapes,
        scratch_shapes=[pltpu.VMEM((acc_rows, wide), f32), pltpu.VMEM((slots, width), f32)],
        compiler_params=params(),
        cost_estimate=cost(20e9, 20e6),
        name="mlp_step",
    )(where, resid, cot, final, gains, up, down, *parts, *more)


def attend_back_kernel(tokens, first, last, waits, where_ref, normed_ref, kv_ref, *refs):
    (
        video_ref, message_ref, nmsg_ref, kvmsg_ref, ctx_ref, lse_ref, dresid_ref, gains_ref,
        wq_ref, wk_ref, wv_ref, wo_ref,
    ) = refs[:12]
    refs = refs[12:]
    if first:
        carried, refs = refs[1:5], refs[5:]
    refs = refs[waits:]
    outs = refs[: 6 if last else 5]
    grad_ref, dmsg_ref, dcls_ref, gain_ref = outs[:4]
    acc, wqt, wkt, wall = refs[len(outs) :]
    here = pl.program_id(0)
    step = here + first
    batch, rows, width = dresid_ref.shape
    patch = tokens - 1

    @pl.when(here == 0)
    def _():
        wqt[...] = wq_ref[...].T
        wkt[...] = wk_ref[...].T
        wall[:, 0:width] = wq_ref[...]
        wall[:, width : 2 * width] = wk_ref[...]
        wall[:, 2 * width : 3 * width] = wv_ref[...]
        for k, ref in enumerate((dmsg_ref, dcls_ref, gain_ref, acc)):
            ref[...] = carried[k][...] if first else jnp.zeros(ref.shape, f32)

    frames = range(batch)
    normed, kv = [], []
    for i in frames:
        normed.append(with_message(normed_ref[i], nmsg_ref, tokens, step * batch + i))
        kv.append(with_message(kv_ref[i], kvmsg_ref, tokens, step * batch + i))
    branch = [dresid_ref[i].astype(bf16) for i in frames]
    queries_t = [nt(wqt[...], n).astype(bf16) * jnp.bfloat16(SCALE) for n in normed]
    dcontext_t = [nt(wo_ref[...], b).astype(bf16) for b in branch]
    keys_t = [nt(wkt[...], n).astype(bf16) for n in normed]
    acc[3 * width : 4 * width, :] += functools.reduce(
        jnp.add, [nn(ctx_ref[i], branch[i]) for i in frames]
    )
    jobs = [(i, h) for i in frames for h in range(HEADS)]
    own = [slice(h * HEAD_DIM, (h + 1) * HEAD_DIM) for h in range(HEADS)]
    scores, dprobs, low, dscores, dq, dk, dv = {}, {}, {}, {}, {}, {}, {}

    def score(job):
        i, h = job
        scores[job] = nn(pair_lanes(kv[i], h), half_pair(queries_t[i], h))
        dprobs[job] = nn(pair_lanes(kv[i], HEADS + h), half_pair(dcontext_t[i], h))

    def soften(job):
        i, h = job
        probs = jnp.exp(masked_tail(scores.pop(job), tokens) - lse_ref[i, h : h + 1, :])
        low[job] = probs.astype(bf16)
        weighted = dprobs.pop(job) * probs
        dscores[job] = (weighted - probs * row_sum(weighted)).astype(bf16)

    def mix(job):
        i, h = job
        dq[job] = nn(keys_t[i][own[h]], dscores[job]) * SCALE
        dk[job] = nt(queries_t[i][own[h]], dscores.pop(job))
        dv[job] = nt(dcontext_t[i][own[h]], low.pop(job))

    stagger(jobs, [score, soften, mix], 2)
    dall = []
    for i in frames:
        parts = [d[i, h] for d in (dq, dk, dv) for h in range(HEADS)]
        dall.append(jnp.concatenate(parts, axis=0).astype(bf16))
    acc[0 : 3 * width, :] += functools.reduce(
        jnp.add, [nn(dall[i], normed[i]) for i in frames]
    )
    gain_sum = jnp.zeros((1, width), f32)
    for i in frames:
        dnormed = nn(wall[...], dall[i]).T
        at = pl.ds(step * batch + i, 1)
        base = put_row(pad_rows(video_ref[i].astype(f32), rows), tokens - 1, message_ref[at, :])
        unit, inv = unit_norm(base)
        dtokens = dresid_ref[i] + norm_back(unit, inv, gains_ref[0:1, :], dnormed)
        gain_sum = gain_sum + row_sum(dnormed * unit)
        grad_ref[i] = dtokens[:patch].astype(bf16)
        dcls_ref[at, :] = dtokens[0:1]
        dmsg_ref[at, :] = dtokens[patch : patch + 1]
    gain_ref[0:1, :] += gain_sum

    @pl.when(here == pl.num_programs(0) - 1)
    def _():
        if last:
            emit(where_ref, acc, *outs[4:])
        else:
            outs[4][...] = acc[...]


def attend_back(
    where, normed, kv, video, message, nmsg, kvmsg, ctx, lse, dresid, gains, qkv, outw, plan,
    batch, first, steps, carried=(), after=(),
):
    count, rows, width = normed.shape
    patch = video.shape[1]
    slots = message.shape[0]
    last = (first + steps) * batch == count
    acc_rows, packet_specs, packet_shapes = plan.packet(4 * width, width)
    if not last:
        packet_specs, packet_shapes = [full((acc_rows, width))], [shape_of((acc_rows, width), f32)]

    def block(shape):
        return pl.BlockSpec((batch,) + shape, lambda i, *_: (i + first, 0, 0))

    anywhere = pl.BlockSpec(memory_space=pl.ANY)
    carry_specs = [anywhere] + [full(x.shape) for x in carried[1:]] if carried else []
    return pl.pallas_call(
        functools.partial(attend_back_kernel, patch + 1, first, last, len(after)),
        grid=(steps,),
        in_specs=[
            scalars(),
            block((rows, width)),
            block((rows, 2 * width)),
            block((patch, width)),
            full((slots, width)),
            full((slots, width)),
            full((slots, 2 * width)),
            block((width, rows)),
            block((8, rows)),
            block((rows, width)),
            full(gains.shape),
            square(width, 1, 0),
            square(width, 1, 1),
            square(width, 1, 2),
            square(width, 1),
        ]
        + carry_specs
        + [anywhere] * len(after),
        out_specs=[block((patch, width))]
        + [full((slots, width))] * 2
        + [full((8, width))]
        + packet_specs,
        out_shape=[shape_of((count, patch, width), bf16)]
        + [shape_of((slots, width), f32)] * 2
        + [shape_of((8, width), f32)]
        + packet_shapes,
        input_output_aliases={15: 0} if carried else {},
        scratch_shapes=[
            pltpu.VMEM((acc_rows, width), f32),
            pltpu.VMEM((width, width), bf16),
            pltpu.VMEM((width, width), bf16),
            pltpu.VMEM((width, 3 * width), bf16),
        ],
        compiler_params=params(),
        cost_estimate=cost(4.5e9 * steps, 4e6 * steps),
        name="attend_back",
    )(
        where, normed, kv, video, message, nmsg, kvmsg, ctx, lse, dresid, gains, qkv, qkv, qkv,
        outw, *carried, *after,
    )


def message_back_kernel(
    layout, together, where_ref, *refs
):
    segs, frames, clips = layout
    pieces = refs[: segs * frames]
    (
        mw_ref, mg_ref, qkv_ref, outw_ref, big_in, out_in,
        big_ref, out_ref, mwg_ref, gain_ref, gains_ref, dclass_ref,
        whole, classes, dmsgs, keys, values, queries, context, dcontext, dq, dk, dv, dstart,
    ) = refs[segs * frames :]
    del big_in, out_in
    width = mw_ref.shape[0]
    slots = dclass_ref.shape[0]
    chunk = pieces[0].shape[1] - 2 * slots
    place(layout, where_ref, pieces, whole, slice(0, chunk), slice(0, width))
    for j in range(3):
        big_ref[1, j] = whole[j * width : (j + 1) * width, :].astype(f32).T
    out_ref[1] = whole[3 * width : 4 * width, :].astype(f32)
    me_f, me_s, me_c = where_ref[0], where_ref[1], where_ref[2]
    total = together * slots
    rows = frames * total
    steps = segs * clips // together

    def row_of(s, f, c):
        group = s * clips + c
        step, inside = group // together, group % together
        return step, pl.multiple_of(f * total + inside * slots, 16)

    for a in range(segs):
        for b in range(frames):
            for d in range(clips):
                piece = pieces[a * frames + b][d]
                step, at = row_of(me_s ^ a, me_f ^ b, me_c ^ d)
                classes[step, pl.ds(at, slots), :] = piece[chunk : chunk + slots]
                dmsgs[step, pl.ds(at, slots), :] = piece[chunk + slots :]
    gain_total = jnp.zeros((slots, width), f32)
    for i in range(frames * together):
        for step in range(steps):
            gain_total += dmsgs[step, i * slots : (i + 1) * slots, :].astype(f32)
    gains_ref[...] = gain_total[slots - 4 : slots]

    index = lax.broadcasted_iota(jnp.int32, (rows, 1), 0) % slots
    columns, spread = head_columns(width), head_rows(width)
    spread_low = spread.astype(bf16)
    cut = [slice(g * total, (g + 1) * total) for g in range(frames)]
    my_step, my_at = row_of(me_s, me_f, me_c)

    def batch(step, put):
        dm = jnp.where(index < slots - 6, dmsgs[step].astype(f32), 0.0).astype(bf16)
        cls = classes[step]
        start = nn(cls, mw_ref[...]).astype(bf16)
        unit, inv = unit_norm(start.astype(f32))
        normed = (unit * mg_ref[...]).astype(bf16)
        queries[...] = nn(normed, qkv_ref[0, 0]).astype(bf16)
        keys[...] = nn(normed, qkv_ref[0, 1]).astype(bf16)
        values[...] = nn(normed, qkv_ref[0, 2]).astype(bf16)
        dcontext[...] = nt(dm, outw_ref[0])
        dk[...] = jnp.zeros(dk.shape, f32)
        dv[...] = jnp.zeros(dv.shape, f32)

        @pl.loop(0, frames)
        def _(f):
            here = pl.ds(pl.multiple_of(f * total, 16), total)
            query = queries[here, :].astype(f32)
            dctx = dcontext[here, :]
            probs = message_probs(message_scores(query, [keys[c, :] for c in cut], columns))
            wide = [nn(p.astype(bf16), spread_low) for p in probs]
            context[here, :] = functools.reduce(
                jnp.add, [w * values[c, :].astype(f32) for w, c in zip(wide, cut)]
            ).astype(bf16)
            dprobs = [exact(dctx * values[c, :].astype(f32), columns) for c in cut]
            inner = functools.reduce(jnp.add, [p * d for p, d in zip(probs, dprobs)])
            total_dq = jnp.zeros((total, width), f32)
            for g in range(frames):
                dscore = exact(probs[g] * (dprobs[g] - inner) * SCALE, spread)
                total_dq = total_dq + dscore * keys[cut[g], :].astype(f32)
                dk[cut[g], :] += dscore * query
                dv[cut[g], :] += wide[g] * dctx
            dq[here, :] = total_dq

        low_q, low_k, low_v = dq[...].astype(bf16), dk[...].astype(bf16), dv[...].astype(bf16)
        put(big_ref, (0, 0), tn(normed, low_q))
        put(big_ref, (0, 1), tn(normed, low_k))
        put(big_ref, (0, 2), tn(normed, low_v))
        put(out_ref, 0, tn(context[...], dm))
        dnormed = nt(low_q, qkv_ref[0, 0]) + nt(low_k, qkv_ref[0, 1]) + nt(low_v, qkv_ref[0, 2])
        put(gain_ref, ..., row_sum(dnormed * unit))
        dstart[...] = norm_back(unit, inv, mg_ref[...], dnormed) + dm.astype(f32)
        put(mwg_ref, ..., tn(cls, dstart[...].astype(bf16)))

        @pl.when(my_step == step)
        def _():
            dclass_ref[...] = nt(dstart[pl.ds(my_at, slots), :].astype(bf16), mw_ref[...])

    def first(ref, at, value):
        ref[at] = value

    def more(ref, at, value):
        ref[at] += value

    batch(0, first)
    if steps > 1:
        pl.loop(1, steps)(lambda step: batch(step, more))


def message_back(where, pieces, mw, mg, qkv, outw, big, out, layout, slots):
    segs, frames, clips = layout
    width = mw.shape[0]
    groups = segs * clips
    together = max(1, min(groups, 512 // (frames * slots)))
    rows = frames * together * slots
    everyone = (groups // together, rows, width)
    operands = list(pieces) + [mw, mg, qkv, outw]
    where_big = 1 + len(operands)
    return pl.pallas_call(
        functools.partial(message_back_kernel, layout, together),
        grid=(1,),
        in_specs=[scalars()]
        + [full(x.shape) for x in operands]
        + [pl.BlockSpec(memory_space=pl.ANY)] * 2,
        out_specs=[
            pl.BlockSpec((2, 3, width, width), lambda i: (0, 0, 0, 0)),
            pl.BlockSpec((2, width, width), lambda i: (0, 0, 0)),
            full((width, width)),
            full((1, width)),
            full((4, width)),
            full((slots, width)),
        ],
        out_shape=[
            shape_of(big.shape, f32),
            shape_of(out.shape, f32),
            shape_of((width, width), f32),
            shape_of((1, width), f32),
            shape_of((4, width), f32),
            shape_of((slots, width), f32),
        ],
        input_output_aliases={where_big: 0, where_big + 1: 1},
        scratch_shapes=[
            pltpu.VMEM((groups * frames * (pieces[0].shape[1] - 2 * slots), width), bf16)
        ]
        + [pltpu.VMEM(everyone, bf16)] * 2
        + [pltpu.VMEM((rows, width), bf16)] * 4
        + [pltpu.VMEM((rows, width), f32)] * 5,
        compiler_params=params(),
        cost_estimate=cost(6e9, 12e6),
        name="message_back",
    )(where, *operands, big, out)


def emit(where_ref, acc, keep_ref, send_ref, more_keep=None, more_send=None):
    frames, clips, chunk = keep_ref.shape[:3]
    width = acc.shape[1]
    me_f, me_s, me_c = where_ref[0], where_ref[1], where_ref[2]
    for a, out in enumerate((keep_ref, send_ref)):
        more = (more_keep, more_send)[a]
        for b in range(frames):
            for d in range(clips):
                to = ((me_s ^ a) * frames + (me_f ^ b)) * clips + (me_c ^ d)
                at = pl.multiple_of(to * chunk, 16)
                out[b, d, :, :width] = acc[pl.ds(at, chunk), :].astype(bf16)
                if more is not None:
                    out[b, d, :, width:] = more[b, d]


class Plan:
    def __init__(self, clips):
        self.clips = clips
        self.segs = lax.axis_size("seg")
        self.frames = lax.axis_size("frame")
        self.rings = lax.axis_size("clip")
        self.layout = (self.segs, self.frames, self.rings)
        self.devices = self.segs * self.frames * self.rings

    def chunk(self, rows):
        share = -(-rows // self.devices)
        return -(-share // 16) * 16

    def packet(self, rows, width, more=0):
        chunk = self.chunk(rows)
        shape = (self.frames, self.rings, chunk, width + more)
        return chunk * self.devices, [full(shape)] * 2, [shape_of(shape, bf16)] * 2


def swap(x, axis, k):
    count = lax.axis_size(axis)
    return lax.ppermute(x, axis, [(i, i ^ k) for i in range(count)])


def total(terms):
    return functools.reduce(jnp.add, [t.astype(f32) for t in terms]).astype(bf16)


def reduce_seg(keep, send):
    return [keep, swap(send, "seg", 1)]


def frame_sends(terms):
    return [total([t[b] for t in terms]) for b in range(1, terms[0].shape[0])]


def reduce_frame(terms, sends):
    return [t[0] for t in terms] + [swap(x, "frame", b + 1) for b, x in enumerate(sends)]


def reduce_clip(terms):
    count = lax.axis_size("clip")
    bit = 1
    while bit < count:
        paired = [t.reshape((-1, 2) + t.shape[1:]) for t in terms]
        send = total([p[:, 1] for p in paired])
        terms = [p[:, 0] for p in paired] + [swap(send, "clip", bit)]
        bit *= 2
    return total([t[0] for t in terms])


def gather_clip(own):
    held = own[None]
    bit = lax.axis_size("clip") // 2
    while bit:
        held = jnp.stack([held, swap(held, "clip", bit)], axis=1)
        held = held.reshape((-1,) + own.shape)
        bit //= 2
    return held


def gather_frame(held):
    return [held] + [swap(held, "frame", b) for b in range(1, lax.axis_size("frame"))]


def gather_seg(held):
    return held + [swap(h, "seg", 1) for h in held]


def place(layout, where_ref, pieces, whole, rows, lanes):
    segs, frames, clips = layout
    chunk = rows.stop - rows.start
    me_f, me_s, me_c = where_ref[0], where_ref[1], where_ref[2]
    for a in range(segs):
        for b in range(frames):
            for d in range(clips):
                of = ((me_s ^ a) * frames + (me_f ^ b)) * clips + (me_c ^ d)
                at = pl.multiple_of(of * chunk, 16)
                whole[pl.ds(at, chunk), :] = pieces[a * frames + b][d, rows, lanes]


def unpack_kernel(layout, where_ref, *refs):
    count = layout[0] * layout[1]
    pieces = refs[:count]
    up_ref, down_ref, big_ref, out_ref, whole, more = refs[count:]
    width, ff = up_ref.shape
    wide = whole.shape[1]
    rows = slice(0, pieces[0].shape[1])
    place(layout, where_ref, pieces, whole, rows, slice(0, wide))
    place(layout, where_ref, pieces, more, rows, slice(wide, wide + width))
    blocks = ff // wide
    for c in range(blocks):
        span = slice(c * wide, (c + 1) * wide)
        up_ref[:, span] = whole[c * width : (c + 1) * width, :].astype(f32)
        other = whole[(blocks + c) * width : (blocks + c + 1) * width, :]
        down_ref[span, :] = other.astype(f32).T
    for j in range(3):
        big_ref[0, j] = more[j * width : (j + 1) * width, :].astype(f32)
    out_ref[0] = more[3 * width : 4 * width, :].astype(f32)


def unpack(where, pieces, width, ff, plan):
    chunk, wide = pieces[0].shape[1:]
    everything = plan.devices * chunk
    return pl.pallas_call(
        functools.partial(unpack_kernel, plan.layout),
        grid=(1,),
        in_specs=[scalars()] + [full(x.shape) for x in pieces],
        out_specs=[
            full((width, ff)),
            full((ff, width)),
            pl.BlockSpec((1, 3, width, width), lambda i: (2, 0, 0, 0)),
            pl.BlockSpec((1, width, width), lambda i: (2, 0, 0)),
        ],
        out_shape=[
            shape_of((width, ff), f32),
            shape_of((ff, width), f32),
            shape_of((3, 3, width, width), f32),
            shape_of((3, width, width), f32),
        ],
        scratch_shapes=[
            pltpu.VMEM((everything, wide - width), bf16),
            pltpu.VMEM((everything, width), bf16),
        ],
        compiler_params=params(),
        cost_estimate=cost(2e9, 12e6),
        name="unpack",
    )(where, *pieces)


def last_rows_kernel(gain_a, gain_b, gain_c, dmsg_ref, classes_ref, out_ref):
    slots, width = dmsg_ref.shape
    filled = dmsg_ref[0 : slots - 6, :]
    rows = [
        filled,
        jnp.zeros((2, width), f32),
        gain_a[0:1, :],
        gain_b[0:1, :],
        gain_b[1:2, :],
        gain_c[0:1, :],
    ]
    out_ref[slots:, :] = jnp.concatenate(rows, axis=0).astype(bf16)
    out_ref[:slots, :] = classes_ref[...]


def last_rows(gain_a, gain_b, gain_c, dmsg, classes):
    slots, width = dmsg.shape
    return pl.pallas_call(
        last_rows_kernel,
        out_shape=shape_of((2 * slots, width), bf16),
        name="last_rows",
    )(gain_a, gain_b, gain_c, dmsg, classes)


def local(
    video, captions, caption_lengths, message_weight, message_gain, qkv_weights, out_weights,
    mlp_up, mlp_down, gains, video_cot, caption_cot,
):
    micro, clips, per_frame, patch, width = video.shape
    count = micro * clips * per_frame
    ff = mlp_up.shape[1]
    plan = Plan(clips)
    tokens = patch + 1
    rows = -(-tokens // 16) * 16
    slots = -(-(count + 6) // 16) * 16
    where = jnp.stack(
        [lax.axis_index("frame"), lax.axis_index("seg"), lax.axis_index("clip")]
    ).astype(jnp.int32)
    frames = video.reshape(count, patch, width)
    cots = video_cot.reshape(count, patch, width)
    caps = captions.reshape(-1, width)
    cap_cots = caption_cot.reshape(-1, width)
    lengths = caption_lengths.reshape(micro, -1)
    gain = message_gain.reshape(1, width)

    classes = class_rows(video, slots)
    gathered = gather_frame(classes)
    normed, kv = norm_tokens(frames, gains, qkv_weights, rows)
    message, nmsg, kvmsg, visual, final = first_rows(
        gathered, message_weight, gain, qkv_weights, out_weights, mlp_up, mlp_down, gains,
        kv, tokens,
    )
    visuals = gather_frame(visual)
    resid, ctx, lse = attend(
        normed, kv, frames, message, nmsg, kvmsg, qkv_weights, out_weights, tokens
    )
    results = captions_step(
        where, lengths, visuals, caps, cap_cots, qkv_weights, out_weights, gains, plan
    )
    caption_out, caption_grad, gain_c = results[:3]
    parts = list(results[3:-2])
    parts = [parts[0]] + [swap(parts[b], "frame", b) for b in range(1, plan.frames)]
    video_out, dresid, gain_b, keep, send = mlp_step(
        where, resid, cots, final, gains, mlp_up, mlp_down, parts, results[-2:], plan
    )
    terms = reduce_seg(keep, send)
    batch = share_of(count, 2)
    steps = count // batch
    early = min(1, steps - 1)
    back = functools.partial(
        attend_back, where, normed, kv, frames, message, nmsg, kvmsg, ctx, lse, dresid, gains,
        qkv_weights, out_weights, plan, batch,
    )
    carried = back(0, early) if early else ()
    sends = frame_sends(terms)
    grad, dmsg, dcls, gain_a, keep, send = back(early, steps - early, carried, sends)
    terms = reduce_frame(terms, sends)
    rest = last_rows(gain_a, gain_b, gain_c, dmsg, classes)
    late = reduce_seg(keep, send)
    mlp_own = reduce_clip(terms)
    late = reduce_frame(late, frame_sends(late))
    mlp_held = gather_clip(mlp_own)
    late_own = reduce_clip(late)
    mlp_all = gather_seg(gather_frame(mlp_held))
    late_all = gather_seg(gather_frame(gather_clip(jnp.concatenate([late_own, rest], axis=0))))

    up_grad, down_grad, big, out = unpack(where, mlp_all, width, ff, plan)
    big, out, mw_grad, mg_grad, gains_grad, dclass = message_back(
        where, late_all, message_weight, gain, qkv_weights, out_weights, big, out, plan.layout, slots
    )
    fixed = (dclass + dcls)[:count].astype(bf16).reshape(micro, clips, per_frame, 1, width)
    grad = lax.dynamic_update_slice(grad.reshape(video.shape), fixed, (0, 0, 0, 0, 0))
    return (
        video_out.reshape(video.shape),
        caption_out.reshape(captions.shape),
        grad,
        caption_grad.reshape(captions.shape),
        mw_grad,
        mg_grad.reshape(width),
        big,
        out,
        up_grad,
        down_grad,
        gains_grad,
    )


def solution(mesh):
    rows = P(None, ("clip", "seg"), "frame", None, None)
    caps = P(None, ("clip", "seg"), "frame", None)
    return jax.shard_map(
        local,
        mesh=mesh,
        in_specs=(rows, caps, P(None, ("clip", "seg"), None)) + (P(),) * 7 + (rows, caps),
        out_specs=(rows, caps, rows, caps) + (P(),) * 7,
        check_vma=False,
    )
```

time: 324 us -> 229 us (0.71)
  Pallas kernels: 190 us -> 116 us
  starting transfers between devices: 73.4 us -> 44.1 us
  waiting for transfers between devices: 35.7 us -> 46.5 us
  local copies, waits for them, and re-layouts: 20.7 us -> 14.3 us
  other arithmetic: 1.26 us -> 5.8 us
    pallas_call x21 -> x6, Pallas kernels: 108 us -> 52.4 us  [the longest x2 28.3 us: attend_back(): pl.pallas_call(functools.partial(attend_back_kernel, patch + 1, first, la...]
    ppermute x70 -> x39, starting transfers between devices: 73.4 us -> 44.1 us  [swap(): return lax.ppermute(x, axis, [(i, i ^ k) for i in range(count)])]
    pallas_call x1, Pallas kernels: 44.4 us -> 28.4 us  [mlp_step(): pl.pallas_call(functools.partial(mlp_kernel, len(parts), patch, ff), grid...]
    ppermute x70 -> x39, waiting for transfers between devices: 35.7 us -> 46.5 us  [swap(): return lax.ppermute(x, axis, [(i, i ^ k) for i in range(count)])]
    unnamed x150 -> x73, local copies, waits for them, and re-layouts: 16.4 us -> 8.5 us
    squeeze x2 -> x0, local copies, waits for them, and re-layouts: 3.8 us -> none  [the longest x1 2.09 us: local(): wq, wk, wv = (qkv_weights[1, 0], qkv_weights[1, 1], qkv_weights[1, 2])]
    pallas_call x1, Pallas kernels: 11.8 us -> 8.31 us  [first_rows(): pl.pallas_call(functools.partial(first_kernel, len(gathered), count, toke...]
  transfers between devices with their start and end apart: 70 -> 39, of which waited for: 15 -> 12; matrix products, arithmetic and copies ran while one was open for 4% -> 6% of each run, Pallas kernels for 52% -> 23%
where the time goes in v2:
time: 229 us; the launch traced here: 228 us
  Pallas kernels  116 us (51%)
  waiting for transfers between devices  46.5 us (20%)
  starting transfers between devices  44.1 us (19%)
  local copies, waits for them, and re-layouts  14.3 us (6%)
  other arithmetic  5.8 us (3%)
    ppermute x39, waiting for transfers between devices, swap(): return lax.ppermute(x, axis, [(i, i ^ k) for i in range(count)])  46.5 us
    ppermute x39, starting transfers between devices, swap(): return lax.ppermute(x, axis, [(i, i ^ k) for i in range(count)])  44.1 us
    pallas_call x1, Pallas kernels, mlp_step(): pl.pallas_call(functools.partial(mlp_kernel, len(parts), patch, ff), grid...  28.4 us
    pallas_call x2, Pallas kernels, attend_back(): pl.pallas_call(functools.partial(attend_back_kernel, patch + 1, first, la...  28.3 us
    pallas_call x1, Pallas kernels, message_back(): pl.pallas_call(functools.partial(message_back_kernel, layout, together),...  20.1 us
    pallas_call x1, Pallas kernels, attend(): pl.pallas_call(functools.partial(attend_kernel, tokens), grid=(count // b...  11.7 us
    unnamed x73, local copies, waits for them, and re-layouts  8.5 us
    pallas_call x1, Pallas kernels, first_rows(): pl.pallas_call(functools.partial(first_kernel, len(gathered), count, toke...  8.31 us
  transfers between devices with their start and end apart: 39, of which 12 were waited for; matrix products, arithmetic and copies ran while one was open for 6% of the time, Pallas kernels for 23%

profile of v2, /device:TPU:0, one launch (start us, length us, event | category | flops | bytes accessed | tf_op | source)
XLA Modules:
  0.0 228.2 jit_solution(5492425682669554368)
XLA Ops:
  2.1 3.9 %collective-permute-start.2 = (bf16[16,384]{1,0:T(8,128)(2,1)}, bf16[16,384]{1,0:T(8,128)(2,1)S(1)}, u32[]{:S(2)}, u32[]{:S(2)}) collective-permute-start(bf16[16,384]{1,0:T(8,128)(2,1)} %class_rows.1.refs_0_.classes_ref), channel_id=1, source_target_pairs={{0,6},{2,4},{4,2},{6,0},{1,7},{3,5},{5,3},{7,1},{8,14},{10,12},{12... | collective-permute-start | bytes 36872 | tf_op jit(solution)/shard_map/ppermute | solution.py:968
  7.9 5.5 %norm_tokens.1 = (bf16[10,208,384]{2,1,0:T(8,128)(2,1)}, bf16[10,208,768]{2,1,0:T(8,128)(2,1)}) custom-call(bf16[10,197,384]{2,1,0:T(8,128)(2,1)} %bitcast.168, f32[4,384]{1,0:T(4,128)} %refs_7_.7, bf16[3,3,384,384]{3,2,1,0:T(8,128)(2,1)} %refs_10_.7, bf16[3,3,384,384]{3,2,1,0:T(8,128)(2,1)} %refs_10_.7), custom_call_target="tpu_custom_call" | custom-call | flops 1226833920 | bytes 6389760 | tf_op jit(solution)/shard_map/norm_tokens/pallas_call | solution.py:179
  14.6 8.3 %first_rows.1 = (f32[16,384]{1,0:T(8,128)}, f32[16,384]{1,0:T(8,128)}, f32[16,768]{1,0:T(8,128)}, bf16[16,384]{1,0:T(8,128)(2,1)}, f32[16,384]{1,0:T(8,128)}) custom-call(bf16[16,384]{1,0:T(8,128)(2,1)} %class_rows.1.refs_0_.classes_ref, bf16[16,384]{1,0:T(8,128)(2,1)} %copy-done.31, bf16[16,384]{1,0:T(8,128)(2,1)} %copy-done.30, ...), custom_call_target="tpu_custom_call" | custom-call | flops 4000000000 | bytes 12000000 | tf_op jit(solution)/shard_map/first_rows/pallas_call | solution.py:287
  22.9 2.9 %collective-permute-start.5 = (bf16[16,384]{1,0:T(8,128)(2,1)}, bf16[16,384]{1,0:T(8,128)(2,1)S(1)}, u32[]{:S(2)}, u32[]{:S(2)}) collective-permute-start(bf16[16,384]{1,0:T(8,128)(2,1)} %get-tuple-element.63.refs_0_), channel_id=1, source_target_pairs={{0,6},{2,4},{4,2},{6,0},{1,7},{3,5},{5,3},{7,1},{8,14},{10,12},{12... | collective-permute-start | bytes 36872 | tf_op jit(solution)/shard_map/ppermute | solution.py:968
  30.9 5.7 %captions_step.1 = (bf16[64,384]{1,0:T(8,128)(2,1)}, bf16[64,384]{1,0:T(8,128)(2,1)}, f32[8,384]{1,0:T(8,128)}, f32[16,384]{1,0:T(8,128)}, f32[16,384]{1,0:T(8,1...) custom-call(s32[3]{0:T(128)} %pad_add_fusion.where_ref, ...), custom_call_target="tpu_custom_call" | custom-call | flops 4000000000 | bytes 8000000 | tf_op jit(solution)/shard_map/captions_step/pallas_call | solution.py:510
  36.7 1.9 collective-permute-start.7
  40.0 11.7 %attend.1 = (f32[10,208,384]{2,1,0:T(8,128)}, bf16[10,384,208]{2,1,0:T(8,128)(2,1)}, f32[10,8,208]{2,1,0:T(8,128)}) custom-call(bf16[10,208,384]{2,1,0:T(8,128)(2,1)} %get-tuple-element.56.normed_ref, bf16[10,208,768]{2,1,0:T(8,128)(2,1)} %get-tuple-element.57.refs_11_.kv_ref, bf16[10,197,384]{2,1,0:T(8,128)(2,1)} %bitcast.169, ...), custom_call_target="tpu_custom_call" | custom-call | flops 14000000000 | bytes 10000000 | tf_op jit(solution)/shard_map/attend/pallas_call | solution.py:391
  52.4 28.4 %mlp_step.1 = (bf16[10,197,384]{2,1,0:T(8,128)(2,1)}, f32[10,208,384]{2,1,0:T(8,128)}, f32[8,384]{1,0:T(8,128)}, bf16[4,4,48,1152]{3,2,1,0:T(8,128)(2,1)}, bf16[4,4,48,1152]{3,2,1,0:T(8,128)(2,1)}) custom-call(s32[3]{0:T(128)} %pad_add_fusion.where_ref, f32[10,208,384]{2,1,0:T(8,128)} %get-tuple-element.61.resid_ref, bf16[10,197,384]{2,1,0:T(8,128)(2,1)} %bitcast.178, ...), custom_call_target="tpu_custom_call" | custom-call | flops 20000000000 | bytes 20000000 | tf_op jit(solution)/shard_map/mlp_step/pallas_call | solution.py:597
  82.0 7.5 %attend_back.2 = (bf16[10,197,384]{2,1,0:T(8,128)(2,1)}, f32[16,384]{1,0:T(8,128)}, f32[16,384]{1,0:T(8,128)}, f32[8,384]{1,0:T(8,128)}, f32[1536,384]{1,0:T(8,128)}) custom-call(s32[3]{0:T(128)} %pad_add_fusion.where_ref, bf16[10,208,384]{2,1,0:T(8,128)(2,1)} %get-tuple-element.56.normed_ref, bf16[10,208,768]{2,1,0:T(8,128)(2,1)} %get-tuple-element.57.refs_11_.kv_ref, ...), custom_call_target="tpu_custom_call" | custom-call | flops 4499999744 | bytes 4000000 | tf_op jit(solution)/shard_map/attend_back/pallas_call | solution.py:737
  92.3 1.9 collective-permute-start.25
  94.2 20.8 %attend_back.3 = (bf16[10,197,384]{2,1,0:T(8,128)(2,1)}, f32[16,384]{1,0:T(8,128)}, f32[16,384]{1,0:T(8,128)}, f32[8,384]{1,0:T(8,128)}, bf16[4,4,48,384]{3,2,1,...) custom-call(s32[3]{0:T(128)} %pad_add_fusion.where_ref, ...), custom_call_target="tpu_custom_call", output_to_operand_aliasing={{0}: (15, {})} | custom-call | flops 17999998976 | bytes 16000000 | tf_op jit(solution)/shard_map/attend_back/pallas_call | solution.py:737
  119.8 1.6 collective-permute-start.28
  123.1 2.5 %collective-permute-start.13 = (bf16[4,48,384]{2,1,0:T(8,128)(2,1)S(1)}, bf16[4,48,384]{2,1,0:T(8,128)(2,1)S(1)}, u32[]{:S(2)}, u32[]{:S(2)}) collective-permute-start(bf16[4,48,384]{2,1,0:T(8,128)(2,1)S(1)} %get-tuple-element.127), channel_id=1, source_target_pairs={{0,6},{2,4},{4,2},{6,0},{1,7},{3,5},{5,3},{7,1},{8,14},{10,12},{12... | collective-permute-start | bytes 442376 | tf_op jit(solution)/shard_map/ppermute | solution.py:968
  126.2 1.6 collective-permute-done.28
  127.8 2.6 %collective-permute-start.29 = (bf16[1,48,1152]{2,1,0:T(8,128)(2,1)S(1)}, bf16[1,48,1152]{2,1,0:T(8,128)(2,1)S(1)}, u32[]{:S(2)}, u32[]{:S(2)}) collective-permute-start(bf16[1,48,1152]{2,1,0:T(8,128)(2,1)S(1)} %fusion.12), channel_id=1, source_target_pairs={{0,16},{8,24},{16,0},{24,8},{1,17},{9,25},{17,1},{25,9},{2,18},{10... | collective-permute-start | bytes 331784 | tf_op jit(solution)/shard_map/ppermute | solution.py:968
  130.5 2.3 %collective-permute-done.13 = bf16[4,48,384]{2,1,0:T(8,128)(2,1)S(1)} collective-permute-done((bf16[4,48,384]{2,1,0:T(8,128)(2,1)S(1)}, bf16[4,48,384]{2,1,0:T(8,128)(2,1)S(1)}, u32[]{:S(2)}, u32[]{:S(2)}) %collective-permute-start.13) | collective-permute-done | bytes 147488 | tf_op jit(solution)/shard_map/ppermute | solution.py:968
  135.9 1.6 collective-permute-start.30
  137.5 2.3 %collective-permute-done.14 = bf16[2,48,384]{2,1,0:T(8,128)(2,1)S(1)} collective-permute-done((bf16[2,48,384]{2,1,0:T(8,128)(2,1)S(1)}, bf16[2,48,384]{2,1,0:T(8,128)(2,1)S(1)}, u32[]{:S(2)}, u32[]{:S(2)}) %collective-permute-start.14) | collective-permute-done | bytes 73760 | tf_op jit(solution)/shard_map/ppermute | solution.py:968
  139.9 1.9 collective-permute-start.15
  141.9 3.3 %collective-permute-done.15 = bf16[1,48,384]{2,1,0:T(8,128)(2,1)S(1)} collective-permute-done((bf16[1,48,384]{2,1,0:T(8,128)(2,1)S(1)}, bf16[1,48,384]{2,1,0:T(8,128)(2,1)S(1)}, u32[]{:S(2)}, u32[]{:S(2)}) %collective-permute-start.15) | collective-permute-done | bytes 36896 | tf_op jit(solution)/shard_map/ppermute | solution.py:968
  145.4 3.4 %collective-permute-start.16 = (bf16[1,80,384]{2,1,0:T(8,128)(2,1)S(1)}, bf16[1,80,384]{2,1,0:T(8,128)(2,1)S(1)}, u32[]{:S(2)}, u32[]{:S(2)}) collective-permute-start(bf16[1,80,384]{2,1,0:T(8,128)(2,1)S(1)} %get-tuple-element.134), channel_id=1, source_target_pairs={{0,16},{8,24},{16,0},{24,8},{1,17},{9,25},{17,1},{25,9},{2,18},{10... | collective-permute-start | bytes 184328 | tf_op jit(solution)/shard_map/ppermute | solution.py:968
  148.8 2.3 collective-permute-done.16
  151.1 4.7 %collective-permute-start.17 = (bf16[2,80,384]{2,1,0:T(8,128)(2,1)S(1)}, bf16[2,80,384]{2,1,0:T(8,128)(2,1)S(1)}, u32[]{:S(2)}, u32[]{:S(2)}) collective-permute-start(bf16[2,80,384]{2,1,0:T(8,128)(2,1)S(1)} %get-tuple-element.132), channel_id=1, source_target_pairs={{0,8},{8,0},{16,24},{24,16},{1,9},{9,1},{17,25},{25,17},{2,10},{10... | collective-permute-start | bytes 368648 | tf_op jit(solution)/shard_map/ppermute | solution.py:968
  155.9 2.0 collective-permute-start.33
  157.9 1.5 collective-permute-start.32
  159.6 1.9 collective-permute-start.19
  161.5 21.0 %collective-permute-done.20.refs_3_ = bf16[4,80,384]{2,1,0:T(8,128)(2,1)S(1)} collective-permute-done((bf16[4,80,384]{2,1,0:T(8,128)(2,1)S(1)}, bf16[4,80,384]{2,1,0:T(8,128)(2,1)S(1)}, u32[]{:S(2)}, u32[]{:S(2)}) %collective-permute-start.20) | collective-permute-done | bytes 245792 | tf_op jit(solution)/shard_map/ppermute | solution.py:968
  183.5 3.3 %collective-permute-done.19.refs_2_ = bf16[4,80,384]{2,1,0:T(8,128)(2,1)S(1)} collective-permute-done((bf16[4,80,384]{2,1,0:T(8,128)(2,1)S(1)}, bf16[4,80,384]{2,1,0:T(8,128)(2,1)S(1)}, u32[]{:S(2)}, u32[]{:S(2)}) %collective-permute-start.19) | collective-permute-done | bytes 245792 | tf_op jit(solution)/shard_map/ppermute | solution.py:968
  188.1 6.1 %collective-permute-done.18.refs_1_ = bf16[4,80,384]{2,1,0:T(8,128)(2,1)S(1)} collective-permute-done((bf16[4,80,384]{2,1,0:T(8,128)(2,1)S(1)}, bf16[4,80,384]{2,1,0:T(8,128)(2,1)S(1)}, u32[]{:S(2)}, u32[]{:S(2)}) %collective-permute-start.18) | collective-permute-done | bytes 245792 | tf_op jit(solution)/shard_map/ppermute | solution.py:968
  195.3 2.3 %copy.83 = bf16[2,5,1,197,384]{4,0,3,2,1:T(2,128)(2,1)} copy(bf16[2,5,1,197,384]{4,3,1,0,2:T(8,128)(2,1)S(1)} %bitcast.177) | data formatting | bytes 3025920
  199.6 5.4 %unpack.1 = (f32[384,1536]{1,0:T(8,128)}, f32[1536,384]{1,0:T(8,128)}, f32[3,3,384,384]{3,2,1,0:T(8,128)}, f32[3,384,384]{2,1,0:T(8,128)}) custom-call(s32[3]{0:T(128)} %pad_add_fusion.where_ref, bf16[4,48,1152]{2,1,0:T(8,128)(2,1)} %bitcast.191, bf16[4,48,1152]{2,1,0:T(8,128)(2,1)} %copy-done.14, bf16[4,48,1152]{2,1,0:T(8,128)(2,1)} %copy-done.13, ...), custom_call_target="tpu_custom_call" | custom-call | flops 2000000000 | bytes 12000000 | tf_op jit(solution)/shard_map/unpack/pallas_call | solution.py:1051
  206.0 20.1 %message_back.1 = (f32[3,3,384,384]{3,2,1,0:T(8,128)}, f32[3,384,384]{2,1,0:T(8,128)}, f32[384,384]{1,0:T(8,128)}, f32[1,384]{1,0:T(1,128)}, f32[4,384]{1,0:T(4,128)}, /*index=5*/f32[16,384]{1,0:T(8,128)}) custom-call(s32[3]{0:T(128)} %pad_add_fusion.where_ref, bf16[4,80,384]{2,1,0:T(8,128)(2,1)} %bitcast.198, ...), custom_call_target="tpu_custom_call", output_to_operand_aliasing={{0}: (13, {}), {1}: (14, {})} | custom-call | flops 6000000000 | bytes 12000000 | tf_op jit(solution)/shard_map/message_back/pallas_call | solution.py:897
  (163 shorter events, 34.7 us)
Async XLA Ops:
  2.1 11.9 %collective-permute-start.2 = (bf16[16,384]{1,0:T(8,128)(2,1)}, bf16[16,384]{1,0:T(8,128)(2,1)S(1)}, u32[]{:S(2)}, u32[]{:S(2)}) collective-permute-start(bf16[16,384]{1,0:T(8,128)(2,1)} %class_rows.1.refs_0_.classes_ref), channel_id=1, source_target_pairs={{0,6},{2,4},{4,2},{6,0},{1,7},{3,5},{5,3},{7,1},{8,14},{10,12},{12... | collective-permute-start | bytes 36872 | tf_op jit(solution)/shard_map/ppermute | solution.py:968
  6.0 8.0 %collective-permute-start.1 = (bf16[16,384]{1,0:T(8,128)(2,1)}, bf16[16,384]{1,0:T(8,128)(2,1)S(1)}, u32[]{:S(2)}, u32[]{:S(2)}) collective-permute-start(bf16[16,384]{1,0:T(8,128)(2,1)} %class_rows.1.refs_0_.classes_ref), channel_id=1, source_target_pairs={{0,4},{2,6},{4,0},{6,2},{1,5},{3,7},{5,1},{7,3},{8,12},{10,14},{12... | collective-permute-start | bytes 36872 | tf_op jit(solution)/shard_map/ppermute | solution.py:968
  6.5 7.5 %collective-permute-start = (bf16[16,384]{1,0:T(8,128)(2,1)}, bf16[16,384]{1,0:T(8,128)(2,1)S(1)}, u32[]{:S(2)}, u32[]{:S(2)}) collective-permute-start(bf16[16,384]{1,0:T(8,128)(2,1)} %class_rows.1.refs_0_.classes_ref), channel_id=1, source_target_pairs={{0,2},{2,0},{4,6},{6,4},{1,3},{3,1},{5,7},{7,5},{8,10},{10,8},{12,... | collective-permute-start | bytes 36872 | tf_op jit(solution)/shard_map/ppermute | solution.py:968
  36.5 15.2 %collective-permute-start.6 = (f32[16,384]{1,0:T(8,128)}, f32[16,384]{1,0:T(8,128)S(1)}, u32[]{:S(2)}, u32[]{:S(2)}) collective-permute-start(f32[16,384]{1,0:T(8,128)} %get-tuple-element.65), channel_id=1, source_target_pairs={{0,2},{2,0},{4,6},{6,4},{1,3},{3,1},{5,7},{7,5},{8,10},{10,8},{12,... | collective-permute-start | bytes 73736 | tf_op jit(solution)/shard_map/ppermute | solution.py:968
  36.7 15.1 %collective-permute-start.7 = (f32[16,384]{1,0:T(8,128)}, f32[16,384]{1,0:T(8,128)S(1)}, u32[]{:S(2)}, u32[]{:S(2)}) collective-permute-start(f32[16,384]{1,0:T(8,128)} %get-tuple-element.66), channel_id=1, source_target_pairs={{0,4},{2,6},{4,0},{6,2},{1,5},{3,7},{5,1},{7,3},{8,12},{10,14},{12... | collective-permute-start | bytes 73736 | tf_op jit(solution)/shard_map/ppermute | solution.py:968
  38.6 13.2 %collective-permute-start.8 = (f32[16,384]{1,0:T(8,128)}, f32[16,384]{1,0:T(8,128)S(1)}, u32[]{:S(2)}, u32[]{:S(2)}) collective-permute-start(f32[16,384]{1,0:T(8,128)} %get-tuple-element.67), channel_id=1, source_target_pairs={{0,6},{2,4},{4,2},{6,0},{1,7},{3,5},{5,3},{7,1},{8,14},{10,12},{12... | collective-permute-start | bytes 73736 | tf_op jit(solution)/shard_map/ppermute | solution.py:968
  80.8 8.7 %collective-permute-start.9 = (bf16[4,4,48,1152]{3,2,1,0:T(8,128)(2,1)}, bf16[4,4,48,1152]{3,2,1,0:T(8,128)(2,1)S(1)}, u32[]{:S(2)}, u32[]{:S(2)}) collective-permute-start(bf16[4,4,48,1152]{3,2,1,0:T(8,128)(2,1)} %get-tuple-element.81), channel_id=1, source_target_pairs={{0,1},{1,0},{2,3},{3,2},{4,5},{5,4},{6,7},{7,6},{8,9},{9,8},{10,11... | collective-permute-start | bytes 5308424 | tf_op jit(solution)/shard_map/ppermute | solution.py:968
  90.7 26.8 %collective-permute-start.27 = (bf16[4,48,1152]{2,1,0:T(8,128)(2,1)}, bf16[4,48,1152]{2,1,0:T(8,128)(2,1)S(1)}, u32[]{:S(2)}, u32[]{:S(2)}) collective-permute-start(bf16[4,48,1152]{2,1,0:T(8,128)(2,1)} %get-tuple-element.123.refs_19_), channel_id=1, source_target_pairs={{0,6},{2,4},{4,2},{6,0},{1,7},{3,5},{5,3},{7,1},{8,14},{10,12},{12... | collective-permute-start | bytes 1327112 | tf_op jit(solution)/shard_map/ppermute | solution.py:968
  92.2 25.3 %collective-permute-start.26 = (bf16[4,48,1152]{2,1,0:T(8,128)(2,1)}, bf16[4,48,1152]{2,1,0:T(8,128)(2,1)}, u32[]{:S(2)}, u32[]{:S(2)}) collective-permute-start(bf16[4,48,1152]{2,1,0:T(8,128)(2,1)} %get-tuple-element.124.refs_18_), channel_id=1, source_target_pairs={{0,4},{2,6},{4,0},{6,2},{1,5},{3,7},{5,1},{7,3},{8,12},{10,14},{12... | collective-permute-start | bytes 1327112 | tf_op jit(solution)/shard_map/ppermute | solution.py:968
  92.3 25.3 %collective-permute-start.25 = (bf16[4,48,1152]{2,1,0:T(8,128)(2,1)}, bf16[4,48,1152]{2,1,0:T(8,128)(2,1)}, u32[]{:S(2)}, u32[]{:S(2)}) collective-permute-start(bf16[4,48,1152]{2,1,0:T(8,128)(2,1)} %get-tuple-element.125.refs_17_), channel_id=1, source_target_pairs={{0,2},{2,0},{4,6},{6,4},{1,3},{3,1},{5,7},{7,5},{8,10},{10,8},{12,... | collective-permute-start | bytes 1327112 | tf_op jit(solution)/shard_map/ppermute | solution.py:968
  119.8 7.9 %collective-permute-start.28 = (bf16[2,48,1152]{2,1,0:T(8,128)(2,1)S(1)}, bf16[2,48,1152]{2,1,0:T(8,128)(2,1)S(1)}, u32[]{:S(2)}, u32[]{:S(2)}) collective-permute-start(bf16[2,48,1152]{2,1,0:T(8,128)(2,1)S(1)} %fusion.6), channel_id=1, source_target_pairs={{0,8},{8,0},{16,24},{24,16},{1,9},{9,1},{17,25},{25,17},{2,10},{10... | collective-permute-start | bytes 663560 | tf_op jit(solution)/shard_map/ppermute | solution.py:968
  122.6 7.9 %collective-permute-start.11 = (bf16[4,48,384]{2,1,0:T(8,128)(2,1)S(1)}, bf16[4,48,384]{2,1,0:T(8,128)(2,1)S(1)}, u32[]{:S(2)}, u32[]{:S(2)}) collective-permute-start(bf16[4,48,384]{2,1,0:T(8,128)(2,1)S(1)} %get-tuple-element.126), channel_id=1, source_target_pairs={{0,2},{2,0},{4,6},{6,4},{1,3},{3,1},{5,7},{7,5},{8,10},{10,8},{12,... | collective-permute-start | bytes 442376 | tf_op jit(solution)/shard_map/ppermute | solution.py:968
  123.1 9.7 %collective-permute-start.13 = (bf16[4,48,384]{2,1,0:T(8,128)(2,1)S(1)}, bf16[4,48,384]{2,1,0:T(8,128)(2,1)S(1)}, u32[]{:S(2)}, u32[]{:S(2)}) collective-permute-start(bf16[4,48,384]{2,1,0:T(8,128)(2,1)S(1)} %get-tuple-element.127), channel_id=1, source_target_pairs={{0,6},{2,4},{4,2},{6,0},{1,7},{3,5},{5,3},{7,1},{8,14},{10,12},{12... | collective-permute-start | bytes 442376 | tf_op jit(solution)/shard_map/ppermute | solution.py:968
  125.6 8.6 %collective-permute-start.12 = (bf16[4,48,384]{2,1,0:T(8,128)(2,1)S(1)}, bf16[4,48,384]{2,1,0:T(8,128)(2,1)S(1)}, u32[]{:S(2)}, u32[]{:S(2)}) collective-permute-start(bf16[4,48,384]{2,1,0:T(8,128)(2,1)S(1)} %get-tuple-element.128), channel_id=1, source_target_pairs={{0,4},{2,6},{4,0},{6,2},{1,5},{3,7},{5,1},{7,3},{8,12},{10,14},{12... | collective-permute-start | bytes 442376 | tf_op jit(solution)/shard_map/ppermute | solution.py:968
  127.8 8.0 %collective-permute-start.29 = (bf16[1,48,1152]{2,1,0:T(8,128)(2,1)S(1)}, bf16[1,48,1152]{2,1,0:T(8,128)(2,1)S(1)}, u32[]{:S(2)}, u32[]{:S(2)}) collective-permute-start(bf16[1,48,1152]{2,1,0:T(8,128)(2,1)S(1)} %fusion.12), channel_id=1, source_target_pairs={{0,16},{8,24},{16,0},{24,8},{1,17},{9,25},{17,1},{25,9},{2,18},{10... | collective-permute-start | bytes 331784 | tf_op jit(solution)/shard_map/ppermute | solution.py:968
  135.9 9.3 %collective-permute-start.30 = (bf16[1,48,1152]{2,1,0:T(8,128)(2,1)S(1)}, bf16[1,48,1152]{2,1,0:T(8,128)(2,1)S(1)}, u32[]{:S(2)}, u32[]{:S(2)}) collective-permute-start(bf16[1,48,1152]{2,1,0:T(8,128)(2,1)S(1)} %fusion.5), channel_id=1, source_target_pairs={{0,16},{8,24},{16,0},{24,8},{1,17},{9,25},{17,1},{25,9},{2,18},{10... | collective-permute-start | bytes 331784 | tf_op jit(solution)/shard_map/ppermute | solution.py:968
  145.3 10.5 %collective-permute-start.31 = (bf16[2,48,1152]{2,1,0:T(8,128)(2,1)S(1)}, bf16[2,48,1152]{2,1,0:T(8,128)(2,1)S(1)}, u32[]{:S(2)}, u32[]{:S(2)}) collective-permute-start(bf16[2,48,1152]{2,1,0:T(8,128)(2,1)S(1)} %get-tuple-element.130), channel_id=1, source_target_pairs={{0,8},{8,0},{16,24},{24,16},{1,9},{9,1},{17,25},{25,17},{2,10},{10... | collective-permute-start | bytes 663560 | tf_op jit(solution)/shard_map/ppermute | solution.py:968
  151.1 8.3 %collective-permute-start.17 = (bf16[2,80,384]{2,1,0:T(8,128)(2,1)S(1)}, bf16[2,80,384]{2,1,0:T(8,128)(2,1)S(1)}, u32[]{:S(2)}, u32[]{:S(2)}) collective-permute-start(bf16[2,80,384]{2,1,0:T(8,128)(2,1)S(1)} %get-tuple-element.132), channel_id=1, source_target_pairs={{0,8},{8,0},{16,24},{24,16},{1,9},{9,1},{17,25},{25,17},{2,10},{10... | collective-permute-start | bytes 368648 | tf_op jit(solution)/shard_map/ppermute | solution.py:968
  155.8 26.7 %collective-permute-start.34 = (bf16[4,48,1152]{2,1,0:T(8,128)(2,1)S(1)}, bf16[4,48,1152]{2,1,0:T(8,128)(2,1)S(1)}, u32[]{:S(2)}, u32[]{:S(2)}) collective-permute-start(bf16[4,48,1152]{2,1,0:T(8,128)(2,1)S(1)} %bitcast.187), channel_id=1, source_target_pairs={{0,6},{2,4},{4,2},{6,0},{1,7},{3,5},{5,3},{7,1},{8,14},{10,12},{12... | collective-permute-start | bytes 1327112 | tf_op jit(solution)/shard_map/ppermute | solution.py:968
  155.9 27.1 %collective-permute-start.33 = (bf16[4,48,1152]{2,1,0:T(8,128)(2,1)S(1)}, bf16[4,48,1152]{2,1,0:T(8,128)(2,1)S(1)}, u32[]{:S(2)}, u32[]{:S(2)}) collective-permute-start(bf16[4,48,1152]{2,1,0:T(8,128)(2,1)S(1)} %bitcast.188), channel_id=1, source_target_pairs={{0,4},{2,6},{4,0},{6,2},{1,5},{3,7},{5,1},{7,3},{8,12},{10,14},{12... | collective-permute-start | bytes 1327112 | tf_op jit(solution)/shard_map/ppermute | solution.py:968
  157.9 25.2 %collective-permute-start.32 = (bf16[4,48,1152]{2,1,0:T(8,128)(2,1)S(1)}, bf16[4,48,1152]{2,1,0:T(8,128)(2,1)S(1)}, u32[]{:S(2)}, u32[]{:S(2)}) collective-permute-start(bf16[4,48,1152]{2,1,0:T(8,128)(2,1)S(1)} %bitcast.189), channel_id=1, source_target_pairs={{0,2},{2,0},{4,6},{6,4},{1,3},{3,1},{5,7},{7,5},{8,10},{10,8},{12,... | collective-permute-start | bytes 1327112 | tf_op jit(solution)/shard_map/ppermute | solution.py:968
  159.4 23.0 %collective-permute-start.20 = (bf16[4,80,384]{2,1,0:T(8,128)(2,1)S(1)}, bf16[4,80,384]{2,1,0:T(8,128)(2,1)S(1)}, u32[]{:S(2)}, u32[]{:S(2)}) collective-permute-start(bf16[4,80,384]{2,1,0:T(8,128)(2,1)S(1)} %bitcast.194), channel_id=1, source_target_pairs={{0,6},{2,4},{4,2},{6,0},{1,7},{3,5},{5,3},{7,1},{8,14},{10,12},{12... | collective-permute-start | bytes 737288 | tf_op jit(solution)/shard_map/ppermute | solution.py:968
  159.6 27.2 %collective-permute-start.19 = (bf16[4,80,384]{2,1,0:T(8,128)(2,1)S(1)}, bf16[4,80,384]{2,1,0:T(8,128)(2,1)S(1)}, u32[]{:S(2)}, u32[]{:S(2)}) collective-permute-start(bf16[4,80,384]{2,1,0:T(8,128)(2,1)S(1)} %bitcast.195), channel_id=1, source_target_pairs={{0,4},{2,6},{4,0},{6,2},{1,5},{3,7},{5,1},{7,3},{8,12},{10,14},{12... | collective-permute-start | bytes 737288 | tf_op jit(solution)/shard_map/ppermute | solution.py:968
  182.5 11.8 %collective-permute-start.35 = (bf16[4,48,1152]{2,1,0:T(8,128)(2,1)S(1)}, bf16[4,48,1152]{2,1,0:T(8,128)(2,1)S(1)}, u32[]{:S(2)}, u32[]{:S(2)}) collective-permute-start(bf16[4,48,1152]{2,1,0:T(8,128)(2,1)S(1)} %bitcast.190), channel_id=1, source_target_pairs={{0,1},{1,0},{2,3},{3,2},{4,5},{5,4},{6,7},{7,6},{8,9},{9,8},{10,11... | collective-permute-start | bytes 1327112 | tf_op jit(solution)/shard_map/ppermute | solution.py:968
  182.5 12.2 %collective-permute-start.38 = (bf16[4,48,1152]{2,1,0:T(8,128)(2,1)S(1)}, bf16[4,48,1152]{2,1,0:T(8,128)(2,1)S(1)}, u32[]{:S(2)}, u32[]{:S(2)}) collective-permute-start(bf16[4,48,1152]{2,1,0:T(8,128)(2,1)S(1)} %collective-permute-done.34.refs_3_), channel_id=1, source_target_pairs={{0,1},{1,0},{2,3},{3,2},{4,5},{5,4},{6,7},{7,6},{8,9},{9,8},{10,11... | collective-permute-start | bytes 1327112 | tf_op jit(solution)/shard_map/ppermute | solution.py:968
  183.0 11.8 %collective-permute-start.37 = (bf16[4,48,1152]{2,1,0:T(8,128)(2,1)S(1)}, bf16[4,48,1152]{2,1,0:T(8,128)(2,1)S(1)}, u32[]{:S(2)}, u32[]{:S(2)}) collective-permute-start(bf16[4,48,1152]{2,1,0:T(8,128)(2,1)S(1)} %collective-permute-done.33.refs_2_), channel_id=1, source_target_pairs={{0,1},{1,0},{2,3},{3,2},{4,5},{5,4},{6,7},{7,6},{8,9},{9,8},{10,11... | collective-permute-start | bytes 1327112 | tf_op jit(solution)/shard_map/ppermute | solution.py:968
  183.1 15.8 %collective-permute-start.36 = (bf16[4,48,1152]{2,1,0:T(8,128)(2,1)S(1)}, bf16[4,48,1152]{2,1,0:T(8,128)(2,1)S(1)}, u32[]{:S(2)}, u32[]{:S(2)}) collective-permute-start(bf16[4,48,1152]{2,1,0:T(8,128)(2,1)S(1)} %collective-permute-done.32.refs_1_), channel_id=1, source_target_pairs={{0,1},{1,0},{2,3},{3,2},{4,5},{5,4},{6,7},{7,6},{8,9},{9,8},{10,11... | collective-permute-start | bytes 1327112 | tf_op jit(solution)/shard_map/ppermute | solution.py:968
  186.8 7.5 %collective-permute-start.18 = (bf16[4,80,384]{2,1,0:T(8,128)(2,1)S(1)}, bf16[4,80,384]{2,1,0:T(8,128)(2,1)S(1)}, u32[]{:S(2)}, u32[]{:S(2)}) collective-permute-start(bf16[4,80,384]{2,1,0:T(8,128)(2,1)S(1)} %bitcast.196), channel_id=1, source_target_pairs={{0,2},{2,0},{4,6},{6,4},{1,3},{3,1},{5,7},{7,5},{8,10},{10,8},{12,... | collective-permute-start | bytes 737288 | tf_op jit(solution)/shard_map/ppermute | solution.py:968
  194.2 10.8 %collective-permute-start.21 = (bf16[4,80,384]{2,1,0:T(8,128)(2,1)S(1)}, bf16[4,80,384]{2,1,0:T(8,128)(2,1)S(1)}, u32[]{:S(2)}, u32[]{:S(2)}) collective-permute-start(bf16[4,80,384]{2,1,0:T(8,128)(2,1)S(1)} %bitcast.197), channel_id=1, source_target_pairs={{0,1},{1,0},{2,3},{3,2},{4,5},{5,4},{6,7},{7,6},{8,9},{9,8},{10,11... | collective-permute-start | bytes 737288 | tf_op jit(solution)/shard_map/ppermute | solution.py:968
  194.3 10.8 %collective-permute-start.24 = (bf16[4,80,384]{2,1,0:T(8,128)(2,1)S(1)}, bf16[4,80,384]{2,1,0:T(8,128)(2,1)S(1)}, u32[]{:S(2)}, u32[]{:S(2)}) collective-permute-start(bf16[4,80,384]{2,1,0:T(8,128)(2,1)S(1)} %collective-permute-done.20.refs_3_), channel_id=1, source_target_pairs={{0,1},{1,0},{2,3},{3,2},{4,5},{5,4},{6,7},{7,6},{8,9},{9,8},{10,11... | collective-permute-start | bytes 737288 | tf_op jit(solution)/shard_map/ppermute | solution.py:968
  194.8 10.3 %collective-permute-start.23 = (bf16[4,80,384]{2,1,0:T(8,128)(2,1)S(1)}, bf16[4,80,384]{2,1,0:T(8,128)(2,1)S(1)}, u32[]{:S(2)}, u32[]{:S(2)}) collective-permute-start(bf16[4,80,384]{2,1,0:T(8,128)(2,1)S(1)} %collective-permute-done.19.refs_2_), channel_id=1, source_target_pairs={{0,1},{1,0},{2,3},{3,2},{4,5},{5,4},{6,7},{7,6},{8,9},{9,8},{10,11... | collective-permute-start | bytes 737288 | tf_op jit(solution)/shard_map/ppermute | solution.py:968
  194.8 10.3 %collective-permute-start.22 = (bf16[4,80,384]{2,1,0:T(8,128)(2,1)S(1)}, bf16[4,80,384]{2,1,0:T(8,128)(2,1)S(1)}, u32[]{:S(2)}, u32[]{:S(2)}) collective-permute-start(bf16[4,80,384]{2,1,0:T(8,128)(2,1)S(1)} %collective-permute-done.18.refs_1_), channel_id=1, source_target_pairs={{0,1},{1,0},{2,3},{3,2},{4,5},{5,4},{6,7},{7,6},{8,9},{9,8},{10,11... | collective-permute-start | bytes 737288 | tf_op jit(solution)/shard_map/ppermute | solution.py:968
  (42 other events, 383.8 us)

commit v3 on v2

--- a/solution.py
+++ b/solution.py
@@ -12,7 +12,6 @@
 EPS = 1e-05
 SCALE = 0.125
 MASKED = -1e30
-BIG = 56 * 1024 * 1024
 
 f32 = jnp.float32
 bf16 = jnp.bfloat16
@@ -129,8 +128,8 @@
     return jax.ShapeDtypeStruct(shape, dtype)
 
 
-def params(limit=BIG):
-    return pltpu.CompilerParams(vmem_limit_bytes=limit)
+def params(mib):
+    return pltpu.CompilerParams(vmem_limit_bytes=mib * 1024 * 1024)
 
 
 def cost(flops, nbytes):
@@ -194,7 +193,7 @@
             shape_of((count, rows, 2 * width), bf16),
         ],
         scratch_shapes=[pltpu.VMEM((width, 2 * width), bf16)],
-        compiler_params=params(),
+        compiler_params=params(20),
         cost_estimate=cost(4 * count * rows * width * width, 8 * count * rows * width),
         name="norm_tokens",
     )(video, gains, qkv, qkv)
@@ -287,7 +286,17 @@
     return pl.pallas_call(
         functools.partial(first_kernel, len(gathered), count, tokens),
         grid=(1,),
-        in_specs=[full(x.shape) for x in operands],
+        in_specs=[full(x.shape) for x in gathered]
+        + [
+            full(mw.shape),
+            full(mg.shape),
+            pl.BlockSpec((2, 3, width, width), lambda i: (0, 0, 0, 0)),
+            pl.BlockSpec((2, width, width), lambda i: (0, 0, 0)),
+            full(up.shape),
+            full(down.shape),
+            full(gains.shape),
+            full(kv.shape),
+        ],
         out_specs=[full((slots, width))] * 2 + [full((slots, 2 * width))] + [full((slots, width))] * 2,
         out_shape=[
             shape_of((slots, width), f32),
@@ -297,7 +306,7 @@
             shape_of((slots, width), f32),
         ],
         scratch_shapes=[pltpu.VMEM((slots, width), f32)],
-        compiler_params=params(),
+        compiler_params=params(16),
         cost_estimate=cost(4e9, 12e6),
         name="first_rows",
     )(*operands)
@@ -336,8 +345,9 @@
 
 def attend_kernel(
     tokens, normed_ref, kv_ref, video_ref, message_ref, nmsg_ref, kvmsg_ref, wq_ref, wv_ref, wo_ref,
-    resid_ref, ctx_ref, lse_ref, wqt, wvt,
+    *refs,
 ):
+    resid_ref, ctx_ref, lse_ref, wqt, wvt = refs[-5:]
     step = pl.program_id(0)
 
     @pl.when(step == 0)
@@ -384,7 +394,7 @@
         resid_ref[i] = base + tn(context_t, wo_ref[...])
 
 
-def attend(normed, kv, video, message, nmsg, kvmsg, qkv, outw, tokens):
+def attend(normed, kv, video, message, nmsg, kvmsg, qkv, outw, tokens, after=()):
     count, rows, width = normed.shape
     slots = message.shape[0]
     batch = share_of(count, 2)
@@ -401,7 +411,8 @@
             square(width, 1, 0),
             square(width, 1, 2),
             square(width, 1),
-        ],
+        ]
+        + [pl.BlockSpec(memory_space=pl.ANY)] * len(after),
         out_specs=[
             frames_block(batch, (rows, width)),
             frames_block(batch, (width, rows)),
@@ -413,10 +424,10 @@
             shape_of((count, 8, rows), f32),
         ],
         scratch_shapes=[pltpu.VMEM((width, width), bf16)] * 2,
-        compiler_params=params(),
+        compiler_params=params(20),
         cost_estimate=cost(14e9, 10e6),
         name="attend",
-    )(normed, kv, video, message, nmsg, kvmsg, qkv, qkv, outw)
+    )(normed, kv, video, message, nmsg, kvmsg, qkv, qkv, outw, *after)
 
 
 def caption_kernel(
@@ -452,9 +463,9 @@
     gain = gains_ref[3:4, :]
     normed = (unit * gain).astype(bf16)
     visual = jnp.concatenate([g[...] for g in gathered], axis=0)
-    queries = nn(normed, qkv_ref[2, 0]).astype(bf16)
-    keys = nn(visual, qkv_ref[2, 1]).astype(bf16)
-    values = nn(visual, qkv_ref[2, 2]).astype(bf16)
+    queries = nn(normed, qkv_ref[0, 0]).astype(bf16)
+    keys = nn(visual, qkv_ref[0, 1]).astype(bf16)
+    values = nn(visual, qkv_ref[0, 2]).astype(bf16)
 
     masks = [head_mask((count, width), 1, h) for h in range(HEADS)]
     zero = jnp.zeros((count, width), bf16)
@@ -473,22 +484,22 @@
     probs = expo / jnp.sum(expo, axis=1, keepdims=True)
     low = probs.astype(bf16)
     context = merge(nn(low, values)).astype(bf16)
-    out_ref[...] = (pack + valid * nn(context, outw_ref[2])).astype(bf16)
+    out_ref[...] = (pack + valid * nn(context, outw_ref[0])).astype(bf16)
 
     cot = cot_ref[...].astype(f32)
     branch = (cot * valid).astype(bf16)
-    split_d = by_head(nt(branch, outw_ref[2]).astype(bf16))
+    split_d = by_head(nt(branch, outw_ref[0]).astype(bf16))
     dvalues = tn(low, split_d)
     dprobs = nt(split_d, values)
     dscores = probs * (dprobs - jnp.sum(dprobs * probs, axis=1, keepdims=True))
     dscores = jnp.where(allowed_all, dscores, 0.0).astype(bf16)
     dqueries = (merge(nn(dscores, keys)) * SCALE).astype(bf16)
     dkeys = tn(dscores, split_q) * SCALE
-    dnormed = nt(dqueries, qkv_ref[2, 0])
+    dnormed = nt(dqueries, qkv_ref[0, 0])
     grad_ref[...] = (cot + norm_back(unit, inv, gain, dnormed)).astype(bf16)
     gain_ref[...] = jnp.concatenate([row_sum(dnormed * unit), jnp.zeros((7, width), f32)], axis=0)
     low_k, low_v = dkeys.astype(bf16), dvalues.astype(bf16)
-    part = nt(low_k, qkv_ref[2, 1]) + nt(low_v, qkv_ref[2, 2])
+    part = nt(low_k, qkv_ref[0, 1]) + nt(low_v, qkv_ref[0, 2])
     for g in range(pieces):
         part_refs[g][...] = part[g * slots : (g + 1) * slots]
     if acc.shape[0] > 4 * width:
@@ -497,7 +508,7 @@
     acc[width : 2 * width, :] = tn(visual, low_k)
     acc[2 * width : 3 * width, :] = tn(visual, low_v)
     acc[3 * width : 4 * width, :] = tn(context, branch)
-    emit(where_ref, acc, keep_ref, send_ref)
+    emit(where_ref, acc, keep_ref, send_ref, True)
 
 
 def captions_step(where, lengths, gathered, caps, cot, qkv, outw, gains, plan):
@@ -506,11 +517,17 @@
     pieces = len(gathered)
     slots = gathered[0].shape[0]
     operands = list(gathered) + [caps, cot, qkv, outw, gains]
-    acc_rows, packet_specs, packet_shapes = plan.packet(4 * width, width)
+    acc_rows, packet_specs, packet_shapes = plan.packet(4 * width, width, True)
     return pl.pallas_call(
         functools.partial(caption_kernel, pieces, groups, plan.clips, count // groups),
         grid=(1,),
-        in_specs=[scalars(), scalars()] + [full(x.shape) for x in operands],
+        in_specs=[scalars(), scalars()]
+        + [full(x.shape) for x in operands[:-3]]
+        + [
+            pl.BlockSpec((1, 3, width, width), lambda i: (2, 0, 0, 0)),
+            pl.BlockSpec((1, width, width), lambda i: (2, 0, 0)),
+            full(gains.shape),
+        ],
         out_specs=[full((count, width))] * 2
         + [full((8, width))]
         + [full((slots, width))] * pieces
@@ -520,7 +537,7 @@
         + [shape_of((slots, width), f32)] * pieces
         + packet_shapes,
         scratch_shapes=[pltpu.VMEM((acc_rows, width), f32)],
-        compiler_params=params(),
+        compiler_params=params(12),
         cost_estimate=cost(4e9, 8e6),
         name="captions_step",
     )(where, lengths, *operands)
@@ -530,7 +547,7 @@
     pieces, patch, ff, where_ref, resid_ref, cot_ref, final_ref, gains_ref, up_ref, down_ref, *refs
 ):
     parts = refs[:pieces]
-    more_keep, more_send, out_ref, dresid_ref, gain_ref, keep_ref, send_ref, acc, dcls = refs[pieces:]
+    out_ref, dresid_ref, gain_ref, keep_ref, send_ref, acc, dcls = refs[-7:]
     step = pl.program_id(0)
     batch, rows, width = resid_ref.shape
     wide = acc.shape[1]
@@ -581,19 +598,17 @@
 
     @pl.when(step == pl.num_programs(0) - 1)
     def _():
-        emit(where_ref, acc, keep_ref, send_ref, more_keep, more_send)
-
-
-def mlp_step(where, resid, cot, final, gains, up, down, parts, more, plan):
+        emit(where_ref, acc, keep_ref, send_ref)
+
+
+def mlp_step(where, resid, cot, final, gains, up, down, parts, plan, after=()):
     count, rows, width = resid.shape
     patch = cot.shape[1]
     ff = up.shape[1]
     slots = final.shape[0]
     batch = share_of(count, 2)
     wide = 2 * width
-    acc_rows, packet_specs, packet_shapes = plan.packet(
-        2 * ff * width // wide, wide, more[0].shape[-1]
-    )
+    acc_rows, packet_specs, packet_shapes = plan.packet(2 * ff * width // wide, wide)
     return pl.pallas_call(
         functools.partial(mlp_kernel, len(parts), patch, ff),
         grid=(count // batch,),
@@ -607,7 +622,7 @@
             full(down.shape),
         ]
         + [full((slots, width))] * len(parts)
-        + [full(x.shape) for x in more],
+        + [pl.BlockSpec(memory_space=pl.ANY)] * len(after),
         out_specs=[
             frames_block(batch, (patch, width)),
             frames_block(batch, (rows, width)),
@@ -621,10 +636,10 @@
         ]
         + packet_shapes,
         scratch_shapes=[pltpu.VMEM((acc_rows, wide), f32), pltpu.VMEM((slots, width), f32)],
-        compiler_params=params(),
+        compiler_params=params(36),
         cost_estimate=cost(20e9, 20e6),
         name="mlp_step",
-    )(where, resid, cot, final, gains, up, down, *parts, *more)
+    )(where, resid, cot, final, gains, up, down, *parts, *after)
 
 
 def attend_back_kernel(tokens, first, last, waits, where_ref, normed_ref, kv_ref, *refs):
@@ -771,7 +786,7 @@
             pltpu.VMEM((width, width), bf16),
             pltpu.VMEM((width, 3 * width), bf16),
         ],
-        compiler_params=params(),
+        compiler_params=params(26),
         cost_estimate=cost(4.5e9 * steps, 4e6 * steps),
         name="attend_back",
     )(
@@ -780,52 +795,58 @@
     )
 
 
-def message_back_kernel(
-    layout, together, where_ref, *refs
-):
+def message_back_kernel(layout, together, where_ref, *refs):
     segs, frames, clips = layout
-    pieces = refs[: segs * frames]
+    pieces, more = refs[: segs * frames], refs[segs * frames : segs * frames + segs]
+    refs = refs[segs * frames + segs :]
+    mw_ref, mg_ref, qkv_ref, outw_ref = refs[:4]
     (
-        mw_ref, mg_ref, qkv_ref, outw_ref, big_in, out_in,
         big_ref, out_ref, mwg_ref, gain_ref, gains_ref, dclass_ref,
-        whole, classes, dmsgs, keys, values, queries, context, dcontext, dq, dk, dv, dstart,
-    ) = refs[segs * frames :]
-    del big_in, out_in
+        whole, classes, dmsgs, dstart, wqt, wkt, wvt, wall,
+    ) = refs[6:]
     width = mw_ref.shape[0]
     slots = dclass_ref.shape[0]
-    chunk = pieces[0].shape[1] - 2 * slots
-    place(layout, where_ref, pieces, whole, slice(0, chunk), slice(0, width))
+    chunk = pieces[0].shape[1] - slots
+    place(
+        layout, where_ref, lambda a, b, d: pieces[a * frames + b][d, :chunk, :], whole, chunk
+    )
     for j in range(3):
         big_ref[1, j] = whole[j * width : (j + 1) * width, :].astype(f32).T
     out_ref[1] = whole[3 * width : 4 * width, :].astype(f32)
     me_f, me_s, me_c = where_ref[0], where_ref[1], where_ref[2]
-    total = together * slots
-    rows = frames * total
+    rows = frames * together * slots
     steps = segs * clips // together
+    side = frames * slots * max(1, min(together, 128 // (frames * slots)))
+    blocks = [slice(at, at + side) for at in range(0, rows, side)]
 
     def row_of(s, f, c):
         group = s * clips + c
         step, inside = group // together, group % together
-        return step, pl.multiple_of(f * total + inside * slots, 16)
+        return step, pl.multiple_of((inside * frames + f) * slots, 16)
 
     for a in range(segs):
         for b in range(frames):
             for d in range(clips):
-                piece = pieces[a * frames + b][d]
                 step, at = row_of(me_s ^ a, me_f ^ b, me_c ^ d)
-                classes[step, pl.ds(at, slots), :] = piece[chunk : chunk + slots]
-                dmsgs[step, pl.ds(at, slots), :] = piece[chunk + slots :]
+                classes[step, pl.ds(at, slots), :] = more[a][d, b, more[a].shape[2] - slots :, :]
+                dmsgs[step, pl.ds(at, slots), :] = pieces[a * frames + b][d, chunk:, :]
     gain_total = jnp.zeros((slots, width), f32)
     for i in range(frames * together):
         for step in range(steps):
             gain_total += dmsgs[step, i * slots : (i + 1) * slots, :].astype(f32)
     gains_ref[...] = gain_total[slots - 4 : slots]
 
+    wqt[...] = qkv_ref[0, 0].T
+    wkt[...] = qkv_ref[0, 1].T
+    wvt[...] = qkv_ref[0, 2].T
+    for j in range(3):
+        wall[:, j * width : (j + 1) * width] = qkv_ref[0, j]
     index = lax.broadcasted_iota(jnp.int32, (rows, 1), 0) % slots
-    columns, spread = head_columns(width), head_rows(width)
-    spread_low = spread.astype(bf16)
-    cut = [slice(g * total, (g + 1) * total) for g in range(frames)]
+    key = lax.broadcasted_iota(jnp.int32, (side, side), 0)
+    query = lax.broadcasted_iota(jnp.int32, (side, side), 1)
+    same = (key % slots == query % slots) & (key // (frames * slots) == query // (frames * slots))
     my_step, my_at = row_of(me_s, me_f, me_c)
+    own = [slice(h * HEAD_DIM, (h + 1) * HEAD_DIM) for h in range(HEADS)]
 
     def batch(step, put):
         dm = jnp.where(index < slots - 6, dmsgs[step].astype(f32), 0.0).astype(bf16)
@@ -833,42 +854,56 @@
         start = nn(cls, mw_ref[...]).astype(bf16)
         unit, inv = unit_norm(start.astype(f32))
         normed = (unit * mg_ref[...]).astype(bf16)
-        queries[...] = nn(normed, qkv_ref[0, 0]).astype(bf16)
-        keys[...] = nn(normed, qkv_ref[0, 1]).astype(bf16)
-        values[...] = nn(normed, qkv_ref[0, 2]).astype(bf16)
-        dcontext[...] = nt(dm, outw_ref[0])
-        dk[...] = jnp.zeros(dk.shape, f32)
-        dv[...] = jnp.zeros(dv.shape, f32)
-
-        @pl.loop(0, frames)
-        def _(f):
-            here = pl.ds(pl.multiple_of(f * total, 16), total)
-            query = queries[here, :].astype(f32)
-            dctx = dcontext[here, :]
-            probs = message_probs(message_scores(query, [keys[c, :] for c in cut], columns))
-            wide = [nn(p.astype(bf16), spread_low) for p in probs]
-            context[here, :] = functools.reduce(
-                jnp.add, [w * values[c, :].astype(f32) for w, c in zip(wide, cut)]
-            ).astype(bf16)
-            dprobs = [exact(dctx * values[c, :].astype(f32), columns) for c in cut]
-            inner = functools.reduce(jnp.add, [p * d for p, d in zip(probs, dprobs)])
-            total_dq = jnp.zeros((total, width), f32)
-            for g in range(frames):
-                dscore = exact(probs[g] * (dprobs[g] - inner) * SCALE, spread)
-                total_dq = total_dq + dscore * keys[cut[g], :].astype(f32)
-                dk[cut[g], :] += dscore * query
-                dv[cut[g], :] += wide[g] * dctx
-            dq[here, :] = total_dq
-
-        low_q, low_k, low_v = dq[...].astype(bf16), dk[...].astype(bf16), dv[...].astype(bf16)
-        put(big_ref, (0, 0), tn(normed, low_q))
-        put(big_ref, (0, 1), tn(normed, low_k))
-        put(big_ref, (0, 2), tn(normed, low_v))
-        put(out_ref, 0, tn(context[...], dm))
-        dnormed = nt(low_q, qkv_ref[0, 0]) + nt(low_k, qkv_ref[0, 1]) + nt(low_v, qkv_ref[0, 2])
-        put(gain_ref, ..., row_sum(dnormed * unit))
-        dstart[...] = norm_back(unit, inv, mg_ref[...], dnormed) + dm.astype(f32)
-        put(mwg_ref, ..., tn(cls, dstart[...].astype(bf16)))
+        keys = nn(normed, qkv_ref[0, 1]).astype(bf16)
+        values = nn(normed, qkv_ref[0, 2]).astype(bf16)
+        queries_t = nt(wqt[...], normed).astype(bf16) * jnp.bfloat16(SCALE)
+        keys_t = nt(wkt[...], normed).astype(bf16)
+        values_t = nt(wvt[...], normed).astype(bf16)
+        dcontext_t = nt(outw_ref[0], dm).astype(bf16)
+        scores, dprobs, low, dscores, ctx, dq, dk, dv = {}, {}, {}, {}, {}, {}, {}, {}
+
+        def score(job):
+            i, h = job
+            at = blocks[i]
+            scores[job] = nn(pair_lanes(keys[at], h), half_pair(queries_t[:, at], h))
+            dprobs[job] = nn(pair_lanes(values[at], h), half_pair(dcontext_t[:, at], h))
+
+        def soften(job):
+            one = jnp.where(same, scores.pop(job), MASKED)
+            expo = jnp.exp(one - jnp.max(one, axis=0, keepdims=True))
+            probs = expo * (1.0 / row_sum(expo))
+            low[job] = probs.astype(bf16)
+            weighted = dprobs.pop(job) * probs
+            dscores[job] = (weighted - probs * row_sum(weighted)).astype(bf16)
+
+        def mix(job):
+            i, h = job
+            at = blocks[i]
+            ctx[job] = nn(values_t[own[h], at], low[job])
+            dq[job] = nn(keys_t[own[h], at], dscores[job]) * SCALE
+            dk[job] = nt(queries_t[own[h], at], dscores.pop(job))
+            dv[job] = nt(dcontext_t[own[h], at], low.pop(job))
+
+        jobs = [(i, h) for i in range(len(blocks)) for h in range(HEADS)]
+        stagger(jobs, [score, soften, mix], 2)
+
+        def gather(parts):
+            lanes = [
+                jnp.concatenate([p[i, h] for p in parts for h in range(HEADS)], axis=0)
+                for i in range(len(blocks))
+            ]
+            return (jnp.concatenate(lanes, axis=1) if len(lanes) > 1 else lanes[0]).astype(bf16)
+
+        put(out_ref, 0, nn(gather([ctx]), dm))
+        dall = gather([dq, dk, dv])
+        grads = nn(dall, normed)
+        for j in range(3):
+            put(big_ref, (0, j), grads[j * width : (j + 1) * width].T)
+        dnormed = nn(wall[...], dall).T
+        put(gain_ref, ..., jnp.sum(dnormed * unit, axis=0))
+        ds = norm_back(unit, inv, mg_ref[...], dnormed) + dm.astype(f32)
+        dstart[...] = ds
+        put(mwg_ref, ..., tn(cls, ds.astype(bf16)))
 
         @pl.when(my_step == step)
         def _():
@@ -877,71 +912,74 @@
     def first(ref, at, value):
         ref[at] = value
 
-    def more(ref, at, value):
+    def again(ref, at, value):
         ref[at] += value
 
     batch(0, first)
     if steps > 1:
-        pl.loop(1, steps)(lambda step: batch(step, more))
-
-
-def message_back(where, pieces, mw, mg, qkv, outw, big, out, layout, slots):
+        pl.loop(1, steps)(lambda step: batch(step, again))
+
+
+def message_back(where, pieces, side, mw, mg, qkv, outw, big, out, layout, slots):
     segs, frames, clips = layout
     width = mw.shape[0]
     groups = segs * clips
     together = max(1, min(groups, 512 // (frames * slots)))
     rows = frames * together * slots
     everyone = (groups // together, rows, width)
-    operands = list(pieces) + [mw, mg, qkv, outw]
-    where_big = 1 + len(operands)
+    operands = list(pieces) + list(side) + [mw, mg]
+    chunk = pieces[0].shape[1] - slots
     return pl.pallas_call(
         functools.partial(message_back_kernel, layout, together),
         grid=(1,),
         in_specs=[scalars()]
         + [full(x.shape) for x in operands]
-        + [pl.BlockSpec(memory_space=pl.ANY)] * 2,
+        + [
+            pl.BlockSpec((1, 3, width, width), lambda i: (0, 0, 0, 0)),
+            pl.BlockSpec((1, width, width), lambda i: (0, 0, 0)),
+            pl.BlockSpec(memory_space=pl.ANY),
+            pl.BlockSpec(memory_space=pl.ANY),
+        ],
         out_specs=[
             pl.BlockSpec((2, 3, width, width), lambda i: (0, 0, 0, 0)),
             pl.BlockSpec((2, width, width), lambda i: (0, 0, 0)),
             full((width, width)),
-            full((1, width)),
+            full((width,)),
             full((4, width)),
             full((slots, width)),
         ],
         out_shape=[
-            shape_of(big.shape, f32),
-            shape_of(out.shape, f32),
+            shape_of((3, 3, width, width), f32),
+            shape_of((3, width, width), f32),
             shape_of((width, width), f32),
-            shape_of((1, width), f32),
+            shape_of((width,), f32),
             shape_of((4, width), f32),
             shape_of((slots, width), f32),
         ],
-        input_output_aliases={where_big: 0, where_big + 1: 1},
-        scratch_shapes=[
-            pltpu.VMEM((groups * frames * (pieces[0].shape[1] - 2 * slots), width), bf16)
-        ]
+        input_output_aliases={len(operands) + 3: 0, len(operands) + 4: 1},
+        scratch_shapes=[pltpu.VMEM((groups * frames * chunk, width), bf16)]
         + [pltpu.VMEM(everyone, bf16)] * 2
-        + [pltpu.VMEM((rows, width), bf16)] * 4
-        + [pltpu.VMEM((rows, width), f32)] * 5,
-        compiler_params=params(),
+        + [pltpu.VMEM((rows, width), f32)]
+        + [pltpu.VMEM((width, width), bf16)] * 3
+        + [pltpu.VMEM((width, 3 * width), bf16)],
+        compiler_params=params(56),
         cost_estimate=cost(6e9, 12e6),
         name="message_back",
-    )(where, *operands, big, out)
-
-
-def emit(where_ref, acc, keep_ref, send_ref, more_keep=None, more_send=None):
+    )(where, *operands, qkv, outw, big, out)
+
+
+def emit(where_ref, acc, keep_ref, send_ref, clip_first=False):
     frames, clips, chunk = keep_ref.shape[:3]
-    width = acc.shape[1]
+    if clip_first:
+        frames, clips = clips, frames
     me_f, me_s, me_c = where_ref[0], where_ref[1], where_ref[2]
     for a, out in enumerate((keep_ref, send_ref)):
-        more = (more_keep, more_send)[a]
         for b in range(frames):
             for d in range(clips):
-                to = ((me_s ^ a) * frames + (me_f ^ b)) * clips + (me_c ^ d)
+                f = b if clip_first else me_f ^ b
+                to = ((me_s ^ a) * frames + f) * clips + (me_c ^ d)
                 at = pl.multiple_of(to * chunk, 16)
-                out[b, d, :, :width] = acc[pl.ds(at, chunk), :].astype(bf16)
-                if more is not None:
-                    out[b, d, :, width:] = more[b, d]
+                out[(d, b) if clip_first else (b, d)] = acc[pl.ds(at, chunk), :].astype(bf16)
 
 
 class Plan:
@@ -957,9 +995,11 @@
         share = -(-rows // self.devices)
         return -(-share // 16) * 16
 
-    def packet(self, rows, width, more=0):
+    def packet(self, rows, width, clip_first=False):
         chunk = self.chunk(rows)
-        shape = (self.frames, self.rings, chunk, width + more)
+        shape = (self.frames, self.rings, chunk, width)
+        if clip_first:
+            shape = (self.rings, self.frames, chunk, width)
         return chunk * self.devices, [full(shape)] * 2, [shape_of(shape, bf16)] * 2
 
 
@@ -972,6 +1012,10 @@
     return functools.reduce(jnp.add, [t.astype(f32) for t in terms]).astype(bf16)
 
 
+def behind(x, *others):
+    return lax.optimization_barrier((x, others))[0]
+
+
 def reduce_seg(keep, send):
     return [keep, swap(send, "seg", 1)]
 
@@ -984,24 +1028,27 @@
     return [t[0] for t in terms] + [swap(x, "frame", b + 1) for b, x in enumerate(sends)]
 
 
-def reduce_clip(terms):
+def clip_bits():
     count = lax.axis_size("clip")
-    bit = 1
-    while bit < count:
-        paired = [t.reshape((-1, 2) + t.shape[1:]) for t in terms]
-        send = total([p[:, 1] for p in paired])
-        terms = [p[:, 0] for p in paired] + [swap(send, "clip", bit)]
-        bit *= 2
-    return total([t[0] for t in terms])
-
-
-def gather_clip(own):
-    held = own[None]
-    bit = lax.axis_size("clip") // 2
-    while bit:
-        held = jnp.stack([held, swap(held, "clip", bit)], axis=1)
-        held = held.reshape((-1,) + own.shape)
-        bit //= 2
+    return [1 << j for j in range(count.bit_length() - 1)]
+
+
+def clip_send(terms):
+    paired = [t.reshape((-1, 2) + t.shape[1:]) for t in terms]
+    return [p[:, 0] for p in paired], total([p[:, 1] for p in paired])
+
+
+def clip_reduce(terms, bits):
+    for bit in bits:
+        terms, send = clip_send(terms)
+        terms = terms + [swap(send, "clip", bit)]
+    return terms
+
+
+def clip_gather(held, bits):
+    for bit in reversed(bits):
+        both = jnp.stack([held, swap(held, "clip", bit)], axis=1)
+        held = both.reshape((-1,) + held.shape[1:])
     return held
 
 
@@ -1009,31 +1056,41 @@
     return [held] + [swap(held, "frame", b) for b in range(1, lax.axis_size("frame"))]
 
 
+def clip_all(own):
+    return jnp.stack([own] + [swap(own, "clip", d) for d in range(1, lax.axis_size("clip"))])
+
+
+def tree(terms):
+    terms = [t.astype(f32) for t in terms]
+    while len(terms) > 1:
+        terms = [a + b for a, b in zip(terms[::2], terms[1::2])]
+    return terms[0].astype(bf16)
+
+
 def gather_seg(held):
     return held + [swap(h, "seg", 1) for h in held]
 
 
-def place(layout, where_ref, pieces, whole, rows, lanes):
+def place(layout, where_ref, piece, whole, chunk, absolute=False):
     segs, frames, clips = layout
-    chunk = rows.stop - rows.start
     me_f, me_s, me_c = where_ref[0], where_ref[1], where_ref[2]
     for a in range(segs):
         for b in range(frames):
             for d in range(clips):
-                of = ((me_s ^ a) * frames + (me_f ^ b)) * clips + (me_c ^ d)
-                at = pl.multiple_of(of * chunk, 16)
-                whole[pl.ds(at, chunk), :] = pieces[a * frames + b][d, rows, lanes]
+                f = b if absolute else me_f ^ b
+                of = ((me_s ^ a) * frames + f) * clips + (me_c ^ d)
+                whole[pl.ds(pl.multiple_of(of * chunk, 16), chunk), :] = piece(a, b, d)
 
 
 def unpack_kernel(layout, where_ref, *refs):
-    count = layout[0] * layout[1]
-    pieces = refs[:count]
-    up_ref, down_ref, big_ref, out_ref, whole, more = refs[count:]
+    segs, frames, clips = layout
+    main, side = refs[:segs], refs[segs : 2 * segs]
+    up_ref, down_ref, big_ref, out_ref, whole, more = refs[2 * segs :]
     width, ff = up_ref.shape
     wide = whole.shape[1]
-    rows = slice(0, pieces[0].shape[1])
-    place(layout, where_ref, pieces, whole, rows, slice(0, wide))
-    place(layout, where_ref, pieces, more, rows, slice(wide, wide + width))
+    place(layout, where_ref, lambda a, b, d: main[a][b * clips + d], whole, main[0].shape[1])
+    chunk = more.shape[0] // (segs * frames * clips)
+    place(layout, where_ref, lambda a, b, d: side[a][d, b, :chunk, :], more, chunk, True)
     blocks = ff // wide
     for c in range(blocks):
         span = slice(c * wide, (c + 1) * wide)
@@ -1045,13 +1102,12 @@
     out_ref[0] = more[3 * width : 4 * width, :].astype(f32)
 
 
-def unpack(where, pieces, width, ff, plan):
-    chunk, wide = pieces[0].shape[1:]
-    everything = plan.devices * chunk
+def unpack(where, main, side, width, ff, plan, slots):
+    chunk, wide = main[0].shape[1:]
     return pl.pallas_call(
         functools.partial(unpack_kernel, plan.layout),
         grid=(1,),
-        in_specs=[scalars()] + [full(x.shape) for x in pieces],
+        in_specs=[scalars()] + [full(x.shape) for x in main + side],
         out_specs=[
             full((width, ff)),
             full((ff, width)),
@@ -1065,37 +1121,34 @@
             shape_of((3, width, width), f32),
         ],
         scratch_shapes=[
-            pltpu.VMEM((everything, wide - width), bf16),
-            pltpu.VMEM((everything, width), bf16),
-        ],
-        compiler_params=params(),
+            pltpu.VMEM((plan.devices * chunk, wide), bf16),
+            pltpu.VMEM((plan.devices * (side[0].shape[2] - slots), width), bf16),
+        ],
+        compiler_params=params(56),
         cost_estimate=cost(2e9, 12e6),
         name="unpack",
-    )(where, *pieces)
-
-
-def last_rows_kernel(gain_a, gain_b, gain_c, dmsg_ref, classes_ref, out_ref):
+    )(where, *main, *side)
+
+
+def last_rows_kernel(gain_a, gain_b, gain_c, dmsg_ref, out_ref):
     slots, width = dmsg_ref.shape
-    filled = dmsg_ref[0 : slots - 6, :]
     rows = [
-        filled,
+        dmsg_ref[0 : slots - 6, :],
         jnp.zeros((2, width), f32),
         gain_a[0:1, :],
         gain_b[0:1, :],
         gain_b[1:2, :],
         gain_c[0:1, :],
     ]
-    out_ref[slots:, :] = jnp.concatenate(rows, axis=0).astype(bf16)
-    out_ref[:slots, :] = classes_ref[...]
-
-
-def last_rows(gain_a, gain_b, gain_c, dmsg, classes):
-    slots, width = dmsg.shape
+    out_ref[...] = jnp.concatenate(rows, axis=0).astype(bf16)
+
+
+def last_rows(gain_a, gain_b, gain_c, dmsg):
     return pl.pallas_call(
         last_rows_kernel,
-        out_shape=shape_of((2 * slots, width), bf16),
+        out_shape=shape_of(dmsg.shape, bf16),
         name="last_rows",
-    )(gain_a, gain_b, gain_c, dmsg, classes)
+    )(gain_a, gain_b, gain_c, dmsg)
 
 
 def local(
@@ -1127,42 +1180,79 @@
         kv, tokens,
     )
     visuals = gather_frame(visual)
-    resid, ctx, lse = attend(
-        normed, kv, frames, message, nmsg, kvmsg, qkv_weights, out_weights, tokens
-    )
     results = captions_step(
         where, lengths, visuals, caps, cap_cots, qkv_weights, out_weights, gains, plan
     )
     caption_out, caption_grad, gain_c = results[:3]
     parts = list(results[3:-2])
     parts = [parts[0]] + [swap(parts[b], "frame", b) for b in range(1, plan.frames)]
+    bits = clip_bits()
+    side = reduce_seg(*results[-2:])
+    side, side_send = clip_send(side)
+    resid, ctx, lse = attend(
+        normed, kv, frames, message, nmsg, kvmsg, qkv_weights, out_weights, tokens, [side_send]
+    )
+    side = side + [swap(side_send, "clip", bits[0])]
+    side, parts, resid = behind((side, parts, resid))
+    side, side_send = clip_send(side)
     video_out, dresid, gain_b, keep, send = mlp_step(
-        where, resid, cots, final, gains, mlp_up, mlp_down, parts, results[-2:], plan
+        where, resid, cots, final, gains, mlp_up, mlp_down, parts, plan, [side_send]
     )
-    terms = reduce_seg(keep, send)
+    side = side + [swap(side_send, "clip", bits[1])]
+    side, video_out, dresid, keep, send = behind((side, video_out, dresid, keep, send))
+    side = total([t[0] for t in clip_reduce(side, bits[2:])])
+    main = reduce_seg(keep, send)
+    side = gather_frame(side)
+    turned = video_out.reshape(video.shape).transpose(1, 2, 3, 0, 4)
+    main, dresid, turned, side = behind((main, dresid, turned, side))
+    video_out = turned.transpose(3, 0, 1, 2, 4)
+    sends = frame_sends(main)
+    side = jnp.concatenate([tree(side), jnp.stack(gathered)], axis=1)[None]
+    sends, dresid, side = behind((sends, dresid, side))
     batch = share_of(count, 2)
     steps = count // batch
-    early = min(1, steps - 1)
+    late_steps = 2
     back = functools.partial(
         attend_back, where, normed, kv, frames, message, nmsg, kvmsg, ctx, lse, dresid, gains,
         qkv_weights, out_weights, plan, batch,
     )
-    carried = back(0, early) if early else ()
-    sends = frame_sends(terms)
-    grad, dmsg, dcls, gain_a, keep, send = back(early, steps - early, carried, sends)
-    terms = reduce_frame(terms, sends)
-    rest = last_rows(gain_a, gain_b, gain_c, dmsg, classes)
+    carried = back(0, steps - late_steps)
+    main = reduce_frame(main, sends)
+    side = clip_gather(side, bits[1:])
+    carried, main, side = behind((carried, main, side))
+    main, send = clip_send(main)
+    send, carried, side = behind((send, carried, side))
+    got = swap(send, "clip", bits[0])
+    side = clip_gather(side, bits[:1])
+    grad, dmsg, dcls, gain_a, keep, send = back(steps - late_steps, late_steps, carried)
+    main, side, keep, send, gain_a = behind((main + [got], side, keep, send, gain_a))
+
     late = reduce_seg(keep, send)
-    mlp_own = reduce_clip(terms)
+    main = clip_reduce(main, bits[1:])
+    side = gather_seg([side])
+    rest = last_rows(gain_a, gain_b, gain_c, dmsg)
+    late, main, rest, side = behind((late, main, rest, side))
     late = reduce_frame(late, frame_sends(late))
-    mlp_held = gather_clip(mlp_own)
-    late_own = reduce_clip(late)
-    mlp_all = gather_seg(gather_frame(mlp_held))
-    late_all = gather_seg(gather_frame(gather_clip(jnp.concatenate([late_own, rest], axis=0))))
-
-    up_grad, down_grad, big, out = unpack(where, mlp_all, width, ff, plan)
+    held = clip_gather(total(main), bits)
+    held, late, side = behind((held, late, side))
+    frames_n, half = plan.frames, max(1, plan.frames // 2)
+    first = [swap(held, "frame", b) for b in range(frames_n - 1, frames_n - 1 - half // 2, -1)]
+    late_sum = total(late)
+    late = [late_sum[0]] + [swap(late_sum[d], "clip", d) for d in range(1, plan.rings)]
+    held, late, first = behind((held, late, first))
+    rest_b = range(frames_n - 1 - half // 2, 0, -1)
+    second = [swap(held, "frame", b) for b in rest_b]
+    late = clip_all(jnp.concatenate([total(late), rest], axis=0))
+    held, late, first, second = behind((held, late, first, second))
+    held = [held] + (first + second)[::-1]
+    held = gather_seg([jnp.concatenate(held, axis=0)])
+    late = gather_frame(late)
+    up_grad, down_grad, big, out = unpack(where, held, side, width, ff, plan, slots)
+    late, up_grad = behind((late, up_grad))
+    late = gather_seg(late)
     big, out, mw_grad, mg_grad, gains_grad, dclass = message_back(
-        where, late_all, message_weight, gain, qkv_weights, out_weights, big, out, plan.layout, slots
+        where, late, side, message_weight, gain, qkv_weights, out_weights, big, out, plan.layout,
+        slots,
     )
     fixed = (dclass + dcls)[:count].astype(bf16).reshape(micro, clips, per_frame, 1, width)
     grad = lax.dynamic_update_slice(grad.reshape(video.shape), fixed, (0, 0, 0, 0, 0))
@@ -1172,7 +1262,7 @@
         grad,
         caption_grad.reshape(captions.shape),
         mw_grad,
-        mg_grad.reshape(width),
+        mg_grad,
         big,
         out,
         up_grad,

time: 229 us -> 187 us (0.82)
  Pallas kernels: 116 us -> 86.2 us
  waiting for transfers between devices: 46.5 us -> 28.3 us
  starting transfers between devices: 44.1 us -> 50.3 us
  other arithmetic: 5.8 us -> 2.08 us
  local copies, waits for them, and re-layouts: 14.3 us -> 17.9 us
    ppermute x39 -> x47, waiting for transfers between devices: 46.5 us -> 28.3 us  [swap(): return lax.ppermute(x, axis, [(i, i ^ k) for i in range(count)])]
    pallas_call x1, Pallas kernels: 20.1 us -> 11.1 us  [message_back(): pl.pallas_call(functools.partial(message_back_kernel, layout, together),...]
    ppermute x39 -> x47, starting transfers between devices: 44.1 us -> 50.3 us  [swap(): return lax.ppermute(x, axis, [(i, i ^ k) for i in range(count)])]
    unnamed x73 -> x91, local copies, waits for them, and re-layouts: 8.5 us -> 14 us
    pallas_call x2, Pallas kernels: 28.3 us -> 22.9 us  [attend_back(): pl.pallas_call(functools.partial(attend_back_kernel, patch + 1, first, la...]
    pallas_call x1, Pallas kernels: 8.31 us -> 3.74 us  [first_rows(): pl.pallas_call(functools.partial(first_kernel, len(gathered), count, toke...]
    pallas_call x1, Pallas kernels: 28.4 us -> 24.4 us  [mlp_step(): pl.pallas_call(functools.partial(mlp_kernel, len(parts), patch, ff), grid...]
    pallas_call x1, Pallas kernels: 5.52 us -> 2.9 us  [norm_tokens(): pl.pallas_call(norm_kernel, grid=(count // batch,), in_specs=[frames_bloc...]
  transfers between devices with their start and end apart: 39 -> 47, of which waited for: 12 -> 17; matrix products, arithmetic and copies ran while one was open for 6% -> 3% of each run, Pallas kernels for 23% -> 36%
where the time goes in v3:
time: 187 us; the launch traced here: 186 us
  Pallas kernels  86.2 us (46%)
  starting transfers between devices  50.3 us (27%)
  waiting for transfers between devices  28.3 us (15%)
  local copies, waits for them, and re-layouts  17.9 us (10%)
  other arithmetic  2.08 us (1%)
    ppermute x47, starting transfers between devices, swap(): return lax.ppermute(x, axis, [(i, i ^ k) for i in range(count)])  50.3 us
    ppermute x47, waiting for transfers between devices, swap(): return lax.ppermute(x, axis, [(i, i ^ k) for i in range(count)])  28.3 us
    pallas_call x1, Pallas kernels, mlp_step(): pl.pallas_call(functools.partial(mlp_kernel, len(parts), patch, ff), grid...  24.4 us
    pallas_call x2, Pallas kernels, attend_back(): pl.pallas_call(functools.partial(attend_back_kernel, patch + 1, first, la...  22.9 us
    unnamed x91, local copies, waits for them, and re-layouts  14 us
    pallas_call x1, Pallas kernels, message_back(): pl.pallas_call(functools.partial(message_back_kernel, layout, together),...  11.1 us
    pallas_call x1, Pallas kernels, attend(): pl.pallas_call(functools.partial(attend_kernel, tokens), grid=(count // b...  9.12 us
    pallas_call x1, Pallas kernels, unpack(): pl.pallas_call(functools.partial(unpack_kernel, plan.layout), grid=(1,),...  5.58 us
  transfers between devices with their start and end apart: 47, of which 17 were waited for; matrix products, arithmetic and copies ran while one was open for 3% of the time, Pallas kernels for 36%

profile of v3, /device:TPU:0, one launch (start us, length us, event | category | flops | bytes accessed | tf_op | source)
XLA Modules:
  0.0 186.3 jit_solution(14397556489283586220)
XLA Ops:
  2.0 3.9 %collective-permute-start.2 = (bf16[16,384]{1,0:T(8,128)(2,1)}, bf16[16,384]{1,0:T(8,128)(2,1)S(1)}, u32[]{:S(2)}, u32[]{:S(2)}) collective-permute-start(bf16[16,384]{1,0:T(8,128)(2,1)} %class_rows.1.refs_0_), channel_id=1, source_target_pairs={{0,6},{2,4},{4,2},{6,0},{1,7},{3,5},{5,3},{7,1},{8,14},{10,12},{12... | collective-permute-start | bytes 36872 | tf_op jit(solution)/shard_map/ppermute | solution.py:1008
  6.5 1.6 copy.47
  8.1 2.9 %norm_tokens.1 = (bf16[10,208,384]{2,1,0:T(8,128)(2,1)S(1)}, bf16[10,208,768]{2,1,0:T(8,128)(2,1)S(1)}) custom-call(bf16[10,197,384]{2,1,0:T(8,128)(2,1)S(1)} %bitcast.181, f32[4,384]{1,0:T(4,128)S(1)} %copy-done.10, bf16[3,3,384,384]{3,2,1,0:T(8,128)(2,1)S(1)} %copy-done, bf16[3,3,384,384]{3,2,1,0:T(8,128)(2,1)S(1)} %copy-done), custom_call_target="tpu_custom_call" | custom-call | flops 1226833920 | bytes 6389760 | tf_op jit(solution)/shard_map/norm_tokens/pallas_call | solution.py:178
  11.1 1.7 copy-done.13
  13.9 1.9 %copy-done.14 = bf16[10,208,768]{2,1,0:T(8,128)(2,1)S(1)} copy-done((bf16[10,208,768]{2,1,0:T(8,128)(2,1)S(1)}, bf16[10,208,768]{2,1,0:T(8,128)(2,1)}, u32[]{:S(2)}) %copy-start.14) | copy-done | bytes 3194904
  19.6 3.7 %first_rows.1 = (f32[16,384]{1,0:T(8,128)S(1)}, f32[16,384]{1,0:T(8,128)S(1)}, f32[16,768]{1,0:T(8,128)S(1)}, bf16[16,384]{1,0:T(8,128)(2,1)S(1)}, f32[16,384]{1,0:T(8,128)S(1)}) custom-call(bf16[16,384]{1,0:T(8,128)(2,1)S(1)} %copy-done.5, bf16[16,384]{1,0:T(8,128)(2,1)S(1)} %collective-permute-done.refs_1_, ...), custom_call_target="tpu_custom_call" | custom-call | flops 4000000000 | bytes 12000000 | tf_op jit(solution)/shard_map/first_rows/pallas_call | solution.py:286
  23.3 2.9 %collective-permute-start.5 = (bf16[16,384]{1,0:T(8,128)(2,1)S(1)}, bf16[16,384]{1,0:T(8,128)(2,1)S(1)}, u32[]{:S(2)}, u32[]{:S(2)}) collective-permute-start(bf16[16,384]{1,0:T(8,128)(2,1)S(1)} %get-tuple-element.150.refs_0_), channel_id=1, source_target_pairs={{0,6},{2,4},{4,2},{6,0},{1,7},{3,5},{5,3},{7,1},{8,14},{10,12},{12... | collective-permute-start | bytes 36872 | tf_op jit(solution)/shard_map/ppermute | solution.py:1008
  28.0 2.0 %collective-permute-done.4.refs_2_ = bf16[16,384]{1,0:T(8,128)(2,1)S(1)} collective-permute-done((bf16[16,384]{1,0:T(8,128)(2,1)S(1)}, bf16[16,384]{1,0:T(8,128)(2,1)S(1)}, u32[]{:S(2)}, u32[]{:S(2)}) %collective-permute-start.4) | collective-permute-done | bytes 12320 | tf_op jit(solution)/shard_map/ppermute | solution.py:1008
  30.5 3.8 %captions_step.1 = (bf16[64,384]{1,0:T(8,128)(2,1)}, bf16[64,384]{1,0:T(8,128)(2,1)}, f32[8,384]{1,0:T(8,128)S(1)}, f32[16,384]{1,0:T(8,128)S(1)}, f32[16,384]{1...) custom-call(s32[3]{0:T(128)S(1)} %pad_add_fusion.where_ref, ...), custom_call_target="tpu_custom_call" | custom-call | flops 4000000000 | bytes 8000000 | tf_op jit(solution)/shard_map/captions_step/pallas_call | solution.py:521
  35.3 1.9 %collective-permute-start.9 = (f32[16,384]{1,0:T(8,128)S(1)}, f32[16,384]{1,0:T(8,128)S(1)}, u32[]{:S(2)}, u32[]{:S(2)}) collective-permute-start(f32[16,384]{1,0:T(8,128)S(1)} %get-tuple-element.155), channel_id=1, source_target_pairs={{0,4},{2,6},{4,0},{6,2},{1,5},{3,7},{5,1},{7,3},{8,12},{10,14},{12... | collective-permute-start | bytes 73736 | tf_op jit(solution)/shard_map/ppermute | solution.py:1008
  38.7 1.6 collective-permute-start.7
  40.4 9.1 %attend.1 = (f32[10,208,384]{2,1,0:T(8,128)S(1)}, bf16[10,384,208]{2,1,0:T(8,128)(2,1)S(1)}, f32[10,8,208]{2,1,0:T(8,128)S(1)}) custom-call(bf16[10,208,384]{2,1,0:T(8,128)(2,1)S(1)} %copy-done.17, bf16[10,208,768]{2,1,0:T(8,128)(2,1)S(1)} %copy-done.15, bf16[10,197,384]{2,1,0:T(8,128)(2,1)S(1)} %bitcast.182, ...), custom_call_target="tpu_custom_call" | custom-call | flops 14000000000 | bytes 10000000 | tf_op jit(solution)/shard_map/attend/pallas_call | solution.py:401
  49.7 2.7 %collective-permute-start.11 = (bf16[1,4,48,384]{3,2,1,0:T(8,128)(2,1)S(1)}, bf16[1,4,48,384]{3,2,1,0:T(8,128)(2,1)S(1)}, u32[]{:S(2)}, u32[]{:S(2)}) collective-permute-start(bf16[1,4,48,384]{3,2,1,0:T(8,128)(2,1)S(1)} %fusion.4.refs_4_), channel_id=1, source_target_pairs={{0,16},{8,24},{16,0},{24,8},{1,17},{9,25},{17,1},{25,9},{2,18},{10... | collective-permute-start | bytes 442376 | tf_op jit(solution)/shard_map/ppermute | solution.py:1008
  52.4 24.4 %mlp_step.1 = (bf16[10,197,384]{2,1,0:T(8,128)(2,1)S(1)}, f32[10,208,384]{2,1,0:T(8,128)S(1)}, f32[8,384]{1,0:T(8,128)S(1)}, bf16[4,4,48,768]{3,2,1,0:T(8,128)(2,1)S(1)}, bf16[4,4,48,768]{3,2,1,0:T(8,128)(2,1)S(1)}) custom-call(s32[3]{0:T(128)S(1)} %pad_add_fusion.where_ref, f32[10,208,384]{2,1,0:T(8,128)S(1)} %get-tuple-element.165.resid_ref, ...), custom_call_target="tpu_custom_call" | custom-call | flops 20000000000 | bytes 20000000 | tf_op jit(solution)/shard_map/mlp_step/pallas_call | solution.py:612
  80.5 2.3 %copy.86 = bf16[2,5,1,197,384]{4,0,3,2,1:T(2,128)(2,1)} copy(bf16[2,5,1,197,384]{4,3,1,0,2:T(8,128)(2,1)S(1)} %bitcast.187) | data formatting | bytes 3025920 | tf_op jit(solution)/shard_map/reshape | solution.py:1206
  82.8 1.8 collective-permute-done.15
  84.6 2.7 %collective-permute-done.14 = bf16[4,48,384]{2,1,0:T(8,128)(2,1)S(1)} collective-permute-done((bf16[4,48,384]{2,1,0:T(8,128)(2,1)S(1)}, bf16[4,48,384]{2,1,0:T(8,128)(2,1)S(1)}, u32[]{:S(2)}, u32[]{:S(2)}) %collective-permute-start.14) | collective-permute-done | bytes 147488 | tf_op jit(solution)/shard_map/ppermute | solution.py:1008
  92.4 13.1 %attend_back.2 = (bf16[10,197,384]{2,1,0:T(8,128)(2,1)S(1)}, f32[16,384]{1,0:T(8,128)S(1)}, f32[16,384]{1,0:T(8,128)S(1)}, f32[8,384]{1,0:T(8,128)S(1)}, f32[1536,384]{1,0:T(8,128)S(1)}) custom-call(s32[3]{0:T(128)S(1)} %pad_add_fusion.where_ref, bf16[10,208,384]{2,1,0:T(8,128)(2,1)S(1)} %copy-done.17, bf16[10,208,768]{2,1,0:T(8,128)(2,1)S(1)} %copy-done.15, ...), custom_call_target="tpu_custom_call" | custom-call | flops 13500000256 | bytes 12000000 | tf_op jit(solution)/shard_map/attend_back/pallas_call | solution.py:752
  106.3 1.6 collective-permute-start.21
  107.9 9.9 %attend_back.3 = (bf16[10,197,384]{2,1,0:T(8,128)(2,1)S(1)}, f32[16,384]{1,0:T(8,128)S(1)}, f32[16,384]{1,0:T(8,128)S(1)}, f32[8,384]{1,0:T(8,128)S(1)}, bf16[4,...) custom-call(s32[3]{0:T(128)S(1)} %pad_add_fusion.where_ref, ...), custom_call_target="tpu_custom_call", output_to_operand_aliasing={{0}: (15, {})} | custom-call | flops 8999999488 | bytes 8000000 | tf_op jit(solution)/shard_map/attend_back/pallas_call | solution.py:752
  119.3 2.0 %collective-permute-start.23 = (bf16[1,48,768]{2,1,0:T(8,128)(2,1)S(1)}, bf16[1,48,768]{2,1,0:T(8,128)(2,1)S(1)}, u32[]{:S(2)}, u32[]{:S(2)}) collective-permute-start(bf16[1,48,768]{2,1,0:T(8,128)(2,1)S(1)} %fusion.12), channel_id=1, source_target_pairs={{0,16},{8,24},{16,0},{24,8},{1,17},{9,25},{17,1},{25,9},{2,18},{10... | collective-permute-start | bytes 221192 | tf_op jit(solution)/shard_map/ppermute | solution.py:1008
  122.9 3.4 %collective-permute-done.23 = bf16[1,48,768]{2,1,0:T(8,128)(2,1)S(1)} collective-permute-done((bf16[1,48,768]{2,1,0:T(8,128)(2,1)S(1)}, bf16[1,48,768]{2,1,0:T(8,128)(2,1)S(1)}, u32[]{:S(2)}, u32[]{:S(2)}) %collective-permute-start.23) | collective-permute-done | bytes 73760 | tf_op jit(solution)/shard_map/ppermute | solution.py:1008
  132.8 5.3 %collective-permute-done.26 = bf16[2,48,768]{2,1,0:T(8,128)(2,1)S(1)} collective-permute-done((bf16[2,48,768]{2,1,0:T(8,128)(2,1)S(1)}, bf16[2,48,768]{2,1,0:T(8,128)(2,1)S(1)}, u32[]{:S(2)}, u32[]{:S(2)}) %collective-permute-start.26) | collective-permute-done | bytes 147488 | tf_op jit(solution)/shard_map/ppermute | solution.py:1008
  139.9 1.9 %collective-permute-start.32 = (bf16[48,384]{1,0:T(8,128)(2,1)S(1)}, bf16[48,384]{1,0:T(8,128)(2,1)S(1)}, u32[]{:S(2)}, u32[]{:S(2)}) collective-permute-start(bf16[48,384]{1,0:T(8,128)(2,1)S(1)} %get-tuple-element.315), channel_id=1, source_target_pairs={{0,24},{8,16},{16,8},{24,0},{1,25},{9,17},{17,9},{25,1},{2,26},{10... | collective-permute-start | bytes 110600 | tf_op jit(solution)/shard_map/ppermute | solution.py:1008
  141.8 2.6 %collective-permute-start.30 = (bf16[48,384]{1,0:T(8,128)(2,1)S(1)}, bf16[48,384]{1,0:T(8,128)(2,1)S(1)}, u32[]{:S(2)}, u32[]{:S(2)}) collective-permute-start(bf16[48,384]{1,0:T(8,128)(2,1)S(1)} %get-tuple-element.317), channel_id=1, source_target_pairs={{0,8},{8,0},{16,24},{24,16},{1,9},{9,1},{17,25},{25,17},{2,10},{10... | collective-permute-start | bytes 110600 | tf_op jit(solution)/shard_map/ppermute | solution.py:1008
  149.2 2.0 %collective-permute-start.35 = (bf16[64,384]{1,0:T(8,128)(2,1)S(1)}, bf16[64,384]{1,0:T(8,128)(2,1)S(1)}, u32[]{:S(2)}, u32[]{:S(2)}) collective-permute-start(bf16[64,384]{1,0:T(8,128)(2,1)S(1)} %get-tuple-element.322), channel_id=1, source_target_pairs={{0,16},{8,24},{16,0},{24,8},{1,17},{9,25},{17,1},{25,9},{2,18},{10... | collective-permute-start | bytes 147464 | tf_op jit(solution)/shard_map/ppermute | solution.py:1008
  151.4 2.3 %collective-permute-start.36 = (bf16[64,384]{1,0:T(8,128)(2,1)S(1)}, bf16[64,384]{1,0:T(8,128)(2,1)S(1)}, u32[]{:S(2)}, u32[]{:S(2)}) collective-permute-start(bf16[64,384]{1,0:T(8,128)(2,1)S(1)} %get-tuple-element.322), channel_id=1, source_target_pairs={{0,24},{8,16},{16,8},{24,0},{1,25},{9,17},{17,9},{25,1},{2,26},{10... | collective-permute-start | bytes 147464 | tf_op jit(solution)/shard_map/ppermute | solution.py:1008
  153.7 1.9 %collective-permute-done.35 = bf16[64,384]{1,0:T(8,128)(2,1)S(1)} collective-permute-done((bf16[64,384]{1,0:T(8,128)(2,1)S(1)}, bf16[64,384]{1,0:T(8,128)(2,1)S(1)}, u32[]{:S(2)}, u32[]{:S(2)}) %collective-permute-start.35) | collective-permute-done | bytes 49184 | tf_op jit(solution)/shard_map/ppermute | solution.py:1008
  155.7 1.7 collective-permute-done.36
  162.2 5.6 %unpack.1 = (f32[384,1536]{1,0:T(8,128)}, f32[1536,384]{1,0:T(8,128)}, f32[3,3,384,384]{3,2,1,0:T(8,128)}, f32[3,384,384]{2,1,0:T(8,128)}) custom-call(s32[3]{0:T(128)} %copy-done.12, bf16[16,48,768]{2,1,0:T(8,128)(2,1)} %copy-done.32, bf16[16,48,768]{2,1,0:T(8,128)(2,1)} %copy-done.35, bf16[4,4,64,384]{3,2,1,0:T(8,128)(2,1)} %bitcast.212, ...), custom_call_target="tpu_custom_call" | custom-call | flops 2000000000 | bytes 12000000 | tf_op jit(solution)/shard_map/unpack/pallas_call | solution.py:1107
  167.8 2.2 %collective-permute-done.40.refs_2_ = bf16[4,64,384]{2,1,0:T(8,128)(2,1)S(1)} collective-permute-done((bf16[4,64,384]{2,1,0:T(8,128)(2,1)S(1)}, bf16[4,64,384]{2,1,0:T(8,128)(2,1)S(1)}, u32[]{:S(2)}, u32[]{:S(2)}) %collective-permute-start.40) | collective-permute-done | bytes 196640 | tf_op jit(solution)/shard_map/ppermute | solution.py:1008
  173.3 11.1 %message_back.1 = (f32[3,3,384,384]{3,2,1,0:T(8,128)}, f32[3,384,384]{2,1,0:T(8,128)}, f32[384,384]{1,0:T(8,128)}, f32[384]{0:T(512)}, f32[4,384]{1,0:T(4,128)}, /*index=5*/f32[16,384]{1,0:T(8,128)}) custom-call(s32[3]{0:T(128)} %copy-done.12, bf16[4,64,384]{2,1,0:T(8,128)(2,1)} %copy-done.31, ...), custom_call_target="tpu_custom_call", output_to_operand_aliasing={{0}: (15, {}), {1}: (16, {})} | custom-call | flops 6000000000 | bytes 12000000 | tf_op jit(solution)/shard_map/message_back/pallas_call | solution.py:932
  (211 shorter events, 47.4 us)
Async XLA Ops:
  2.0 11.9 %collective-permute-start.2 = (bf16[16,384]{1,0:T(8,128)(2,1)}, bf16[16,384]{1,0:T(8,128)(2,1)S(1)}, u32[]{:S(2)}, u32[]{:S(2)}) collective-permute-start(bf16[16,384]{1,0:T(8,128)(2,1)} %class_rows.1.refs_0_), channel_id=1, source_target_pairs={{0,6},{2,4},{4,2},{6,0},{1,7},{3,5},{5,3},{7,1},{8,14},{10,12},{12... | collective-permute-start | bytes 36872 | tf_op jit(solution)/shard_map/ppermute | solution.py:1008
  5.8 8.0 %collective-permute-start.1 = (bf16[16,384]{1,0:T(8,128)(2,1)}, bf16[16,384]{1,0:T(8,128)(2,1)S(1)}, u32[]{:S(2)}, u32[]{:S(2)}) collective-permute-start(bf16[16,384]{1,0:T(8,128)(2,1)} %class_rows.1.refs_0_), channel_id=1, source_target_pairs={{0,4},{2,6},{4,0},{6,2},{1,5},{3,7},{5,1},{7,3},{8,12},{10,14},{12... | collective-permute-start | bytes 36872 | tf_op jit(solution)/shard_map/ppermute | solution.py:1008
  6.4 7.6 %collective-permute-start = (bf16[16,384]{1,0:T(8,128)(2,1)}, bf16[16,384]{1,0:T(8,128)(2,1)S(1)}, u32[]{:S(2)}, u32[]{:S(2)}) collective-permute-start(bf16[16,384]{1,0:T(8,128)(2,1)} %class_rows.1.refs_0_), channel_id=1, source_target_pairs={{0,2},{2,0},{4,6},{6,4},{1,3},{3,1},{5,7},{7,5},{8,10},{10,8},{12,... | collective-permute-start | bytes 36872 | tf_op jit(solution)/shard_map/ppermute | solution.py:1008
  35.1 14.5 %collective-permute-start.8 = (f32[16,384]{1,0:T(8,128)S(1)}, f32[16,384]{1,0:T(8,128)S(1)}, u32[]{:S(2)}, u32[]{:S(2)}) collective-permute-start(f32[16,384]{1,0:T(8,128)S(1)} %get-tuple-element.154), channel_id=1, source_target_pairs={{0,2},{2,0},{4,6},{6,4},{1,3},{3,1},{5,7},{7,5},{8,10},{10,8},{12,... | collective-permute-start | bytes 73736 | tf_op jit(solution)/shard_map/ppermute | solution.py:1008
  35.3 14.3 %collective-permute-start.9 = (f32[16,384]{1,0:T(8,128)S(1)}, f32[16,384]{1,0:T(8,128)S(1)}, u32[]{:S(2)}, u32[]{:S(2)}) collective-permute-start(f32[16,384]{1,0:T(8,128)S(1)} %get-tuple-element.155), channel_id=1, source_target_pairs={{0,4},{2,6},{4,0},{6,2},{1,5},{3,7},{5,1},{7,3},{8,12},{10,14},{12... | collective-permute-start | bytes 73736 | tf_op jit(solution)/shard_map/ppermute | solution.py:1008
  37.2 12.4 %collective-permute-start.10 = (f32[16,384]{1,0:T(8,128)S(1)}, f32[16,384]{1,0:T(8,128)S(1)}, u32[]{:S(2)}, u32[]{:S(2)}) collective-permute-start(f32[16,384]{1,0:T(8,128)S(1)} %get-tuple-element.156), channel_id=1, source_target_pairs={{0,6},{2,4},{4,2},{6,0},{1,7},{3,5},{5,3},{7,1},{8,14},{10,12},{12... | collective-permute-start | bytes 73736 | tf_op jit(solution)/shard_map/ppermute | solution.py:1008
  38.7 10.9 %collective-permute-start.7 = (bf16[2,4,48,384]{3,2,1,0:T(8,128)(2,1)S(1)}, bf16[2,4,48,384]{3,2,1,0:T(8,128)(2,1)S(1)}, u32[]{:S(2)}, u32[]{:S(2)}) collective-permute-start(bf16[2,4,48,384]{3,2,1,0:T(8,128)(2,1)S(1)} %fusion.refs_0_), channel_id=1, source_target_pairs={{0,8},{8,0},{16,24},{24,16},{1,9},{9,1},{17,25},{25,17},{2,10},{10... | collective-permute-start | bytes 884744 | tf_op jit(solution)/shard_map/ppermute | solution.py:1008
  49.7 27.1 %collective-permute-start.11 = (bf16[1,4,48,384]{3,2,1,0:T(8,128)(2,1)S(1)}, bf16[1,4,48,384]{3,2,1,0:T(8,128)(2,1)S(1)}, u32[]{:S(2)}, u32[]{:S(2)}) collective-permute-start(bf16[1,4,48,384]{3,2,1,0:T(8,128)(2,1)S(1)} %fusion.4.refs_4_), channel_id=1, source_target_pairs={{0,16},{8,24},{16,0},{24,8},{1,17},{9,25},{17,1},{25,9},{2,18},{10... | collective-permute-start | bytes 442376 | tf_op jit(solution)/shard_map/ppermute | solution.py:1008
  76.8 10.7 %collective-permute-start.12 = (bf16[4,4,48,768]{3,2,1,0:T(8,128)(2,1)S(1)}, bf16[4,4,48,768]{3,2,1,0:T(8,128)(2,1)S(1)}, u32[]{:S(2)}, u32[]{:S(2)}) collective-permute-start(bf16[4,4,48,768]{3,2,1,0:T(8,128)(2,1)S(1)} %get-tuple-element.176), channel_id=1, source_target_pairs={{0,1},{1,0},{2,3},{3,2},{4,5},{5,4},{6,7},{7,6},{8,9},{9,8},{10,11... | collective-permute-start | bytes 3538952 | tf_op jit(solution)/shard_map/ppermute | solution.py:1008
  77.0 7.7 %collective-permute-start.15 = (bf16[4,48,384]{2,1,0:T(8,128)(2,1)S(1)}, bf16[4,48,384]{2,1,0:T(8,128)(2,1)S(1)}, u32[]{:S(2)}, u32[]{:S(2)}) collective-permute-start(bf16[4,48,384]{2,1,0:T(8,128)(2,1)S(1)} %fusion.5), channel_id=1, source_target_pairs={{0,6},{2,4},{4,2},{6,0},{1,7},{3,5},{5,3},{7,1},{8,14},{10,12},{12... | collective-permute-start | bytes 442376 | tf_op jit(solution)/shard_map/ppermute | solution.py:1008
  78.5 8.8 %collective-permute-start.14 = (bf16[4,48,384]{2,1,0:T(8,128)(2,1)S(1)}, bf16[4,48,384]{2,1,0:T(8,128)(2,1)S(1)}, u32[]{:S(2)}, u32[]{:S(2)}) collective-permute-start(bf16[4,48,384]{2,1,0:T(8,128)(2,1)S(1)} %fusion.5), channel_id=1, source_target_pairs={{0,4},{2,6},{4,0},{6,2},{1,5},{3,7},{5,1},{7,3},{8,12},{10,14},{12... | collective-permute-start | bytes 442376 | tf_op jit(solution)/shard_map/ppermute | solution.py:1008
  79.1 8.4 %collective-permute-start.13 = (bf16[4,48,384]{2,1,0:T(8,128)(2,1)S(1)}, bf16[4,48,384]{2,1,0:T(8,128)(2,1)S(1)}, u32[]{:S(2)}, u32[]{:S(2)}) collective-permute-start(bf16[4,48,384]{2,1,0:T(8,128)(2,1)S(1)} %fusion.5), channel_id=1, source_target_pairs={{0,2},{2,0},{4,6},{6,4},{1,3},{3,1},{5,7},{7,5},{8,10},{10,8},{12,... | collective-permute-start | bytes 442376 | tf_op jit(solution)/shard_map/ppermute | solution.py:1008
  87.9 17.7 %collective-permute-start.19 = (bf16[1,4,64,384]{3,2,1,0:T(8,128)(2,1)S(1)}, bf16[1,4,64,384]{3,2,1,0:T(8,128)(2,1)S(1)}, u32[]{:S(2)}, u32[]{:S(2)}) collective-permute-start(bf16[1,4,64,384]{3,2,1,0:T(8,128)(2,1)S(1)} %maximum_bitcast_fusion.1), channel_id=1, source_target_pairs={{0,16},{8,24},{16,0},{24,8},{1,17},{9,25},{17,1},{25,9},{2,18},{10... | collective-permute-start | bytes 589832 | tf_op jit(solution)/shard_map/ppermute | solution.py:1008
  88.9 16.7 %collective-permute-start.16 = (bf16[4,48,768]{2,1,0:T(8,128)(2,1)S(1)}, bf16[4,48,768]{2,1,0:T(8,128)(2,1)S(1)}, u32[]{:S(2)}, u32[]{:S(2)}) collective-permute-start(bf16[4,48,768]{2,1,0:T(8,128)(2,1)S(1)} %get-tuple-element.200), channel_id=1, source_target_pairs={{0,2},{2,0},{4,6},{6,4},{1,3},{3,1},{5,7},{7,5},{8,10},{10,8},{12,... | collective-permute-start | bytes 884744 | tf_op jit(solution)/shard_map/ppermute | solution.py:1008
  89.4 16.1 %collective-permute-start.17 = (bf16[4,48,768]{2,1,0:T(8,128)(2,1)S(1)}, bf16[4,48,768]{2,1,0:T(8,128)(2,1)S(1)}, u32[]{:S(2)}, u32[]{:S(2)}) collective-permute-start(bf16[4,48,768]{2,1,0:T(8,128)(2,1)S(1)} %get-tuple-element.201), channel_id=1, source_target_pairs={{0,4},{2,6},{4,0},{6,2},{1,5},{3,7},{5,1},{7,3},{8,12},{10,14},{12... | collective-permute-start | bytes 884744 | tf_op jit(solution)/shard_map/ppermute | solution.py:1008
  90.9 14.7 %collective-permute-start.18 = (bf16[4,48,768]{2,1,0:T(8,128)(2,1)S(1)}, bf16[4,48,768]{2,1,0:T(8,128)(2,1)S(1)}, u32[]{:S(2)}, u32[]{:S(2)}) collective-permute-start(bf16[4,48,768]{2,1,0:T(8,128)(2,1)S(1)} %get-tuple-element.202), channel_id=1, source_target_pairs={{0,6},{2,4},{4,2},{6,0},{1,7},{3,5},{5,3},{7,1},{8,14},{10,12},{12... | collective-permute-start | bytes 884744 | tf_op jit(solution)/shard_map/ppermute | solution.py:1008
  105.8 13.3 %collective-permute-start.20 = (bf16[2,48,768]{2,1,0:T(8,128)(2,1)S(1)}, bf16[2,48,768]{2,1,0:T(8,128)(2,1)S(1)}, u32[]{:S(2)}, u32[]{:S(2)}) collective-permute-start(bf16[2,48,768]{2,1,0:T(8,128)(2,1)S(1)} %fusion.9), channel_id=1, source_target_pairs={{0,8},{8,0},{16,24},{24,16},{1,9},{9,1},{17,25},{25,17},{2,10},{10... | collective-permute-start | bytes 442376 | tf_op jit(solution)/shard_map/ppermute | solution.py:1008
  106.3 12.5 %collective-permute-start.21 = (bf16[2,4,64,384]{3,2,1,0:T(8,128)(2,1)S(1)}, bf16[2,4,64,384]{3,2,1,0:T(8,128)(2,1)S(1)}, u32[]{:S(2)}, u32[]{:S(2)}) collective-permute-start(bf16[2,4,64,384]{3,2,1,0:T(8,128)(2,1)S(1)} %maximum_bitcast_fusion), channel_id=1, source_target_pairs={{0,8},{8,0},{16,24},{24,16},{1,9},{9,1},{17,25},{25,17},{2,10},{10... | collective-permute-start | bytes 1179656 | tf_op jit(solution)/shard_map/ppermute | solution.py:1008
  119.1 7.3 %collective-permute-start.24 = (bf16[4,4,64,384]{3,2,1,0:T(8,128)(2,1)S(1)}, bf16[4,4,64,384]{3,2,1,0:T(8,128)(2,1)}, u32[]{:S(2)}, u32[]{:S(2)}) collective-permute-start(bf16[4,4,64,384]{3,2,1,0:T(8,128)(2,1)S(1)} %bitcast.211), channel_id=1, source_target_pairs={{0,1},{1,0},{2,3},{3,2},{4,5},{5,4},{6,7},{7,6},{8,9},{9,8},{10,11... | collective-permute-start | bytes 2359304 | tf_op jit(solution)/shard_map/ppermute | solution.py:1008
  119.3 7.1 %collective-permute-start.23 = (bf16[1,48,768]{2,1,0:T(8,128)(2,1)S(1)}, bf16[1,48,768]{2,1,0:T(8,128)(2,1)S(1)}, u32[]{:S(2)}, u32[]{:S(2)}) collective-permute-start(bf16[1,48,768]{2,1,0:T(8,128)(2,1)S(1)} %fusion.12), channel_id=1, source_target_pairs={{0,16},{8,24},{16,0},{24,8},{1,17},{9,25},{17,1},{25,9},{2,18},{10... | collective-permute-start | bytes 221192 | tf_op jit(solution)/shard_map/ppermute | solution.py:1008
  126.4 5.9 %collective-permute-start.25 = (bf16[1,48,768]{2,1,0:T(8,128)(2,1)S(1)}, bf16[1,48,768]{2,1,0:T(8,128)(2,1)S(1)}, u32[]{:S(2)}, u32[]{:S(2)}) collective-permute-start(bf16[1,48,768]{2,1,0:T(8,128)(2,1)S(1)} %add_convert_fusion.13), channel_id=1, source_target_pairs={{0,16},{8,24},{16,0},{24,8},{1,17},{9,25},{17,1},{25,9},{2,18},{10... | collective-permute-start | bytes 221192 | tf_op jit(solution)/shard_map/ppermute | solution.py:1008
  127.2 10.9 %collective-permute-start.29 = (bf16[4,48,384]{2,1,0:T(8,128)(2,1)S(1)}, bf16[4,48,384]{2,1,0:T(8,128)(2,1)S(1)}, u32[]{:S(2)}, u32[]{:S(2)}) collective-permute-start(bf16[4,48,384]{2,1,0:T(8,128)(2,1)S(1)} %get-tuple-element.312), channel_id=1, source_target_pairs={{0,6},{2,4},{4,2},{6,0},{1,7},{3,5},{5,3},{7,1},{8,14},{10,12},{12... | collective-permute-start | bytes 442376 | tf_op jit(solution)/shard_map/ppermute | solution.py:1008
  128.8 9.4 %collective-permute-start.28 = (bf16[4,48,384]{2,1,0:T(8,128)(2,1)S(1)}, bf16[4,48,384]{2,1,0:T(8,128)(2,1)S(1)}, u32[]{:S(2)}, u32[]{:S(2)}) collective-permute-start(bf16[4,48,384]{2,1,0:T(8,128)(2,1)S(1)} %get-tuple-element.313), channel_id=1, source_target_pairs={{0,4},{2,6},{4,0},{6,2},{1,5},{3,7},{5,1},{7,3},{8,12},{10,14},{12... | collective-permute-start | bytes 442376 | tf_op jit(solution)/shard_map/ppermute | solution.py:1008
  129.3 8.9 %collective-permute-start.27 = (bf16[4,48,384]{2,1,0:T(8,128)(2,1)S(1)}, bf16[4,48,384]{2,1,0:T(8,128)(2,1)S(1)}, u32[]{:S(2)}, u32[]{:S(2)}) collective-permute-start(bf16[4,48,384]{2,1,0:T(8,128)(2,1)S(1)} %get-tuple-element.314), channel_id=1, source_target_pairs={{0,2},{2,0},{4,6},{6,4},{1,3},{3,1},{5,7},{7,5},{8,10},{10,8},{12,... | collective-permute-start | bytes 442376 | tf_op jit(solution)/shard_map/ppermute | solution.py:1008
  138.2 8.9 %collective-permute-start.33 = (bf16[4,48,768]{2,1,0:T(8,128)(2,1)S(1)}, bf16[4,48,768]{2,1,0:T(8,128)(2,1)S(1)}, u32[]{:S(2)}, u32[]{:S(2)}) collective-permute-start(bf16[4,48,768]{2,1,0:T(8,128)(2,1)S(1)} %bitcast.203), channel_id=1, source_target_pairs={{0,6},{2,4},{4,2},{6,0},{1,7},{3,5},{5,3},{7,1},{8,14},{10,12},{12... | collective-permute-start | bytes 884744 | tf_op jit(solution)/shard_map/ppermute | solution.py:1008
  147.1 10.3 %collective-permute-start.38 = (bf16[4,48,768]{2,1,0:T(8,128)(2,1)S(1)}, bf16[4,48,768]{2,1,0:T(8,128)(2,1)S(1)}, u32[]{:S(2)}, u32[]{:S(2)}) collective-permute-start(bf16[4,48,768]{2,1,0:T(8,128)(2,1)S(1)} %bitcast.204), channel_id=1, source_target_pairs={{0,2},{2,0},{4,6},{6,4},{1,3},{3,1},{5,7},{7,5},{8,10},{10,8},{12,... | collective-permute-start | bytes 884744 | tf_op jit(solution)/shard_map/ppermute | solution.py:1008
  147.7 9.8 %collective-permute-start.37 = (bf16[4,48,768]{2,1,0:T(8,128)(2,1)S(1)}, bf16[4,48,768]{2,1,0:T(8,128)(2,1)S(1)}, u32[]{:S(2)}, u32[]{:S(2)}) collective-permute-start(bf16[4,48,768]{2,1,0:T(8,128)(2,1)S(1)} %bitcast.205), channel_id=1, source_target_pairs={{0,4},{2,6},{4,0},{6,2},{1,5},{3,7},{5,1},{7,3},{8,12},{10,14},{12... | collective-permute-start | bytes 884744 | tf_op jit(solution)/shard_map/ppermute | solution.py:1008
  149.2 6.4 %collective-permute-start.35 = (bf16[64,384]{1,0:T(8,128)(2,1)S(1)}, bf16[64,384]{1,0:T(8,128)(2,1)S(1)}, u32[]{:S(2)}, u32[]{:S(2)}) collective-permute-start(bf16[64,384]{1,0:T(8,128)(2,1)S(1)} %get-tuple-element.322), channel_id=1, source_target_pairs={{0,16},{8,24},{16,0},{24,8},{1,17},{9,25},{17,1},{25,9},{2,18},{10... | collective-permute-start | bytes 147464 | tf_op jit(solution)/shard_map/ppermute | solution.py:1008
  151.4 5.9 %collective-permute-start.36 = (bf16[64,384]{1,0:T(8,128)(2,1)S(1)}, bf16[64,384]{1,0:T(8,128)(2,1)S(1)}, u32[]{:S(2)}, u32[]{:S(2)}) collective-permute-start(bf16[64,384]{1,0:T(8,128)(2,1)S(1)} %get-tuple-element.322), channel_id=1, source_target_pairs={{0,24},{8,16},{16,8},{24,0},{1,25},{9,17},{17,9},{25,1},{2,26},{10... | collective-permute-start | bytes 147464 | tf_op jit(solution)/shard_map/ppermute | solution.py:1008
  157.6 10.2 %collective-permute-start.41 = (bf16[4,64,384]{2,1,0:T(8,128)(2,1)S(1)}, bf16[4,64,384]{2,1,0:T(8,128)(2,1)S(1)}, u32[]{:S(2)}, u32[]{:S(2)}) collective-permute-start(bf16[4,64,384]{2,1,0:T(8,128)(2,1)S(1)} %pad_maximum_fusion.2.refs_0_), channel_id=1, source_target_pairs={{0,6},{2,4},{4,2},{6,0},{1,7},{3,5},{5,3},{7,1},{8,14},{10,12},{12... | collective-permute-start | bytes 589832 | tf_op jit(solution)/shard_map/ppermute | solution.py:1008
  159.1 10.9 %collective-permute-start.40 = (bf16[4,64,384]{2,1,0:T(8,128)(2,1)S(1)}, bf16[4,64,384]{2,1,0:T(8,128)(2,1)S(1)}, u32[]{:S(2)}, u32[]{:S(2)}) collective-permute-start(bf16[4,64,384]{2,1,0:T(8,128)(2,1)S(1)} %pad_maximum_fusion.2.refs_0_), channel_id=1, source_target_pairs={{0,4},{2,6},{4,0},{6,2},{1,5},{3,7},{5,1},{7,3},{8,12},{10,14},{12... | collective-permute-start | bytes 589832 | tf_op jit(solution)/shard_map/ppermute | solution.py:1008
  159.6 10.4 %collective-permute-start.39 = (bf16[4,64,384]{2,1,0:T(8,128)(2,1)S(1)}, bf16[4,64,384]{2,1,0:T(8,128)(2,1)S(1)}, u32[]{:S(2)}, u32[]{:S(2)}) collective-permute-start(bf16[4,64,384]{2,1,0:T(8,128)(2,1)S(1)} %pad_maximum_fusion.2.refs_0_), channel_id=1, source_target_pairs={{0,2},{2,0},{4,6},{6,4},{1,3},{3,1},{5,7},{7,5},{8,10},{10,8},{12,... | collective-permute-start | bytes 589832 | tf_op jit(solution)/shard_map/ppermute | solution.py:1008
  (58 other events, 352.6 us)
